TPU v7x, 32 devices: a whole 2x2x4 slice. The times are simulated.
32 devices in a mesh: leaf: 2 (over core), prow: 4 (over y, x), pcol: 4 (over z).
Axes of the slice: x: 2, y: 2, z: 4, core: 2. Of those that a mesh axis runs over, the one named last changes fastest.
Arguments:
- child_inverse: float32 [32, 512, 512], P(('leaf', 'prow', 'pcol')), parts along dimension 0, as said below
- child_coupling: float32 [32, 1024, 512], P(('leaf', 'prow', 'pcol')), parts along dimension 0, may hold values from -0.25 to 0.25
- child_blocks: int32 [32], P(('leaf', 'prow', 'pcol')), parts along dimension 0, may hold values from 2 to 8, as said below
- child_map: int32 [32, 8], P(('leaf', 'prow', 'pcol')), parts along dimension 0, may hold values from -1 to 15, as said below
- parent_front: float32 [4096, 2048], P(('leaf', 'prow'), 'pcol'), parts along dimension 0, as said below
Outputs:
- parent_factored: float32 [4096, 2048], P(('leaf', 'prow'), 'pcol'), parts along dimension 0
There are 2 independent parts, one for each index of `leaf`. A program takes and returns all parts, laid end to end along the dimension named above; each array names one. Nothing has to cross between parts.
Inputs may be any that keep to these rules, and one draw needn't show every extreme that they name: `child_inverse`: each matrix is lower triangular with a positive diagonal. `child_blocks`: the largest value 8 is taken by some child in every draw. `child_map`: in row c the first child_blocks[c] entries are distinct parent block ids in increasing order and the others are -1. `parent_front`: symmetric; the assembled front is positive definite.
All inputs are finite; a program needn't handle non-finite values.
Results may differ from a plain program's by a relative error of at most 0.0003.
Values sent between devices are 32-bit elements; how exact they have to be, the bound alone decides.
No kernel may reach another device: no remote copies, remote signals or barrier semaphores. Data moves between devices by JAX's collectives and lax.ppermute only.
A program may use at most 128 MiB of HBM per device.

v0:
```python
import jax
import jax.numpy as jnp
from jax import lax
from jax.sharding import PartitionSpec as P

SMAX = 1024
BLK = 128
PORD = 2048


def spread_2(value, axis, root):
    mine = lax.axis_index(axis) == root
    return lax.psum(jnp.where(mine, value, jnp.zeros_like(value)), axis)


def factor_child(inverse_block, coupling, blocks):
    row_ids = jnp.arange(coupling.shape[0])
    masked = jnp.where((row_ids < blocks * BLK)[:, None], coupling, jnp.zeros_like(coupling))
    return jnp.dot(
        masked, inverse_block.T, precision=lax.Precision.HIGHEST, preferred_element_type=jnp.float32
    )


def selection(mapping, block_total):
    return (mapping[None, :] == jnp.arange(block_total)[:, None]).astype(jnp.float32)


def body(child_inverse, child_coupling, child_blocks, child_map, parent_front):
    row_index = lax.axis_index("prow")
    col_index = lax.axis_index("pcol")
    row_count = lax.axis_size("prow")
    col_count = lax.axis_size("pcol")
    tile_rows = parent_front.shape[0]
    tile_cols = parent_front.shape[1]
    slot_count = SMAX // BLK
    block_total = PORD // BLK
    factors = jax.vmap(factor_child)(child_inverse, child_coupling, child_blocks)
    factor = factors[0]
    update = jnp.einsum(
        "ip,jp->ij",
        factor,
        factor,
        precision=lax.Precision.HIGHEST,
        preferred_element_type=jnp.float32,
    )
    select = selection(child_map[0], block_total)
    by_row = select.reshape(row_count, block_total // row_count, slot_count)
    by_col = select.reshape(col_count, block_total // col_count, slot_count)
    blocked = update.reshape(slot_count, BLK, slot_count, BLK)
    spread = jnp.einsum(
        "rbk,kiln,cdl->rcbidn", by_row, blocked, by_col, precision=lax.Precision.HIGHEST
    )
    child_sums = spread.reshape(row_count * col_count, tile_rows, tile_cols)
    received = lax.psum_scatter(child_sums, ("prow", "pcol"), scatter_dimension=0, tiled=True)
    contribution = received[0]
    assembled = parent_front - contribution
    column = spread_2(assembled, "pcol", 0)
    full_column = lax.all_gather(column, "prow", axis=0, tiled=True)
    diag_factor = jnp.linalg.cholesky(full_column[:tile_rows])
    solved = lax.linalg.triangular_solve(
        diag_factor, full_column, left_side=False, lower=True, transpose_a=True
    )
    panel_rows = jnp.concatenate([diag_factor, solved[tile_rows:]], 0)
    own_panel = lax.dynamic_slice_in_dim(panel_rows, row_index * tile_rows, tile_rows, 0)
    col_panel = lax.dynamic_slice_in_dim(panel_rows, col_index * tile_cols, tile_cols, 0)
    product = jnp.einsum(
        "ip,jp->ij",
        own_panel,
        col_panel,
        precision=lax.Precision.HIGHEST,
        preferred_element_type=jnp.float32,
    )
    global_rows = row_index * tile_rows + jnp.arange(tile_rows)
    global_cols = col_index * tile_cols + jnp.arange(tile_cols)
    padded = jnp.concatenate(
        [own_panel, jnp.zeros((tile_rows, tile_cols - tile_rows), jnp.float32)], 1
    )
    trailing = jnp.where(global_rows[:, None] >= tile_rows, assembled - product, assembled)
    return jnp.where(global_cols[None, :] < tile_rows, padded, trailing)


def solution(mesh):
    return jax.shard_map(
        body,
        mesh=mesh,
        in_specs=(
            P(("leaf", "prow", "pcol"), None, None),
            P(("leaf", "prow", "pcol"), None, None),
            P(("leaf", "prow", "pcol")),
            P(("leaf", "prow", "pcol"), None),
            P(("leaf", "prow"), "pcol"),
        ),
        out_specs=P(("leaf", "prow"), "pcol"),
        check_vma=False,
    )
```

profile of v0, /device:TPU:0, one launch (start us, length us, event | category | flops | bytes accessed | tf_op | source)
XLA Modules:
  0.0 718.4 jit_solution(3453841545430523411)
XLA Ops:
  7.3 1.8 broadcast_select_fusion
  9.1 3.5 fusion.25
  12.6 7.2 %convolution_bitcast_fusion.1 = f32[8,128,8,128,1]{3,1,2,0,4:T(8,128)S(1)} fusion(f32[8,128,512]{2,1,0:T(8,128)S(1)} %fusion.25), kind=kOutput, calls=%fused_computation.21 | convolution fusion | flops 6442450944 | bytes 6291456 | tf_op jit(solution)/shard_map/ip,jp->ij/dot_general | solution.py:39
  19.9 9.5 %convolution_bitcast_fusion = f32[128,8,128,4,4,1]{2,4,3,1,0,5:T(4,128)S(1)} fusion(f32[8,128,8,128,1]{3,1,2,0,4:T(8,128)S(1)} %convolution_bitcast_fusion.1, s32[4,4]{1,0:T(4,128)S(1)} %multiply_add_fusion, s32[8]{0:T(128)S(1)} %bitcast.86), kind=kOutput, calls=%fused_computation.5 | convolution fusion | flops 201326720 | bytes 12583008 | tf_op jit(solution)/shard_map/rbk,kiln,cdl->rcbidn/dot_general | solution.py:50
  29.4 15.8 %fusion.2 = f32[4,4,4,128,4,128]{5,4,1,2,0,3:T(4,128)} fusion(f32[128,8,128,4,4,1]{2,4,3,1,0,5:T(4,128)S(1)} %convolution_bitcast_fusion, s32[4,4]{1,0:T(4,128)S(1)} %multiply_add_fusion, s32[8]{0:T(128)S(1)} %bitcast.87), kind=kOutput, calls=%fused_computation.4 | convolution fusion | flops 402653312 | bytes 25165920 | tf_op jit(solution)/shard_map/rbk,kiln,cdl->rcbidn/dot_general | solution.py:50
  45.2 19.8 %copy.6 = f32[4,4,4,128,4,128]{3,2,5,4,1,0:T(4,128)} copy(f32[4,4,4,128,4,128]{5,4,1,2,0,3:T(4,128)} %fusion.2) | data formatting | bytes 33554432 | tf_op jit(solution)/shard_map/rbk,kiln,cdl->rcbidn/transpose | solution.py:50
  65.1 19.9 %reshape.89 = f32[16,512,512]{1,2,0:T(8,128)} reshape(f32[4,4,4,128,4,128]{3,2,5,4,1,0:T(4,128)} %copy.6) | data formatting | bytes 33554432 | tf_op jit(solution)/shard_map/reshape | solution.py:53
  85.0 1.1 copy-done.4
  86.5 351.4 %reduce-scatter.2.cloned.1.call-done = f32[1,512,512]{1,2,0:T(8,128)} async-done(((f32[16,512,512]{1,2,0:T(8,128)}), f32[1,512,512]{1,2,0:T(8,128)}) %reduce-scatter.2.cloned.1.call-update) | async-done | bytes 1048592 | tf_op jit(solution)/shard_map/reduce_scatter | solution.py:54
  437.9 2.4 broadcast_select_fusion.1
  440.8 50.4 %all-reduce.3.cloned.1.call-done = f32[512,512]{0,1:T(8,128)} async-done(((f32[512,512]{0,1:T(8,128)}), f32[512,512]{0,1:T(8,128)}) %all-reduce.3.cloned.1.call-update) | async-done | bytes 1048592 | tf_op jit(solution)/shard_map/psum | solution.py:13
  491.8 53.6 %all-gather.2.cloned.1.call-done = f32[2048,512]{0,1:T(8,128)} async-done(((f32[512,512]{0,1:T(8,128)}), f32[2048,512]{0,1:T(8,128)}) %all-gather.2.cloned.1.call-update) | async-done | bytes 4194320 | tf_op jit(solution)/shard_map/all_gather | solution.py:58
  545.4 1.3 slice.122
  547.0 1.4 fusion.24
  548.5 11.7 %cholesky.103 = f32[128,128]{1,0:T(8,128)S(1)} custom-call(f32[128,128]{1,0:T(8,128)S(1)} %cholesky.263), custom_call_target="Cholesky" | custom-call | tf_op jit(solution)/shard_map/jit(cholesky)/cholesky | solution.py:59
  560.2 9.8 %custom-call.30 = f32[1,128,128]{1,2,0:T(8,128)S(1)} custom-call(f32[1,128,128]{2,1,0:T(8,128)S(1)} %get-tuple-element.34), custom_call_target="InvertDiagBlocksLowerTriangular" | custom-call | tf_op jit(solution)/shard_map/jit(cholesky)/cholesky | solution.py:59
  570.7 11.7 %cholesky.215 = f32[128,128]{1,0:T(8,128)S(1)} custom-call(f32[128,128]{1,0:T(8,128)S(1)} %cholesky.267), custom_call_target="Cholesky" | custom-call | tf_op jit(solution)/shard_map/jit(cholesky)/cholesky | solution.py:59
  582.5 0.7 copy.11
  583.3 0.7 copy.9
  584.1 10.6 %custom-call.31 = f32[1,128,128]{1,2,0:T(8,128)} custom-call(f32[1,128,128]{2,1,0:T(8,128)S(1)} %get-tuple-element.32), custom_call_target="InvertDiagBlocksLowerTriangular" | custom-call | tf_op jit(solution)/shard_map/jit(cholesky)/cholesky | solution.py:59
  594.6 1.0 cholesky.222
  595.6 0.8 constant_dynamic-update-slice_fusion.2
  596.5 1.2 convolution_dynamic-update-slice_fusion
  598.2 11.7 %cholesky.236 = f32[128,128]{1,0:T(8,128)S(1)} custom-call(f32[128,128]{1,0:T(8,128)S(1)} %cholesky.272), custom_call_target="Cholesky" | custom-call | tf_op jit(solution)/shard_map/jit(cholesky)/cholesky | solution.py:59
  610.1 9.8 %custom-call.32 = f32[1,128,128]{1,2,0:T(8,128)S(1)} custom-call(f32[1,128,128]{2,1,0:T(8,128)S(1)} %get-tuple-element.30), custom_call_target="InvertDiagBlocksLowerTriangular" | custom-call | tf_op jit(solution)/shard_map/jit(cholesky)/cholesky | solution.py:59
  620.7 11.9 %cholesky.253 = f32[128,128]{1,0:T(8,128)S(1)} custom-call(f32[128,128]{1,0:T(8,128)S(1)} %convolution_subtract_fusion.4), custom_call_target="Cholesky" | custom-call | tf_op jit(solution)/shard_map/jit(cholesky)/cholesky | solution.py:59
  632.7 0.6 compare_reduce_fusion.1
  633.4 0.7 compare_reduce_fusion
  634.1 0.7 compare_reduce_fusion.2
  637.3 1.2 fusion.29
  639.1 14.2 %while.1 = (s32[]{:T(128)}, f32[512,512]{0,1:T(8,128)}, s32[4,2]{0,1:T(2,128)S(1)}, f32[4,128,128]{2,1,0:T(8,128)}, s32[]{:T(128)}) while((s32[]{:T(128)}, f32[512,512]{0,1:T(8,128)}, s32[4,2]{0,1:T(2,128)S(1)}, f32[4,128,128]{2,1,0:T(8,128)}, s32[]{:T(128)}) %tuple.25), condition=%wide.while_cond, body=%wide.while_body.sunk | while | flops 2 | bytes 393829 | solution.py:60
  639.8 2.2 dynamic-slice.7
  642.1 0.6 bitcast_dynamic-update-slice_fusion.2
  643.3 2.2 dynamic-slice.7
  646.9 2.2 dynamic-slice.7
  649.2 0.6 bitcast_dynamic-update-slice_fusion.2
  650.5 2.2 dynamic-slice.7
  653.4 40.1 %custom-call.33 = f32[4,128,128]{1,2,0:T(8,128)S(1)} custom-call(f32[4,128,128]{2,1,0:T(8,128)} %get-tuple-element.12), custom_call_target="InvertDiagBlocksLowerTriangular" | custom-call | tf_op jit(solution)/shard_map/triangular_solve | solution.py:60
  693.5 2.5 fusion.22
  696.0 2.3 convolution_subtract_fusion.1
  698.3 1.1 fusion.40
  699.4 2.2 convolution_subtract_fusion
  701.6 1.1 fusion.39
  702.7 3.2 fusion.13
  705.9 1.1 fusion.38
  707.0 0.9 fusion.5
  708.2 1.9 fusion.21
  710.2 1.3 copy.18
  (58 shorter events, 9.2 us)
Async XLA Ops:
  6.5 2.6 copy-start
  6.5 431.4 %reduce-scatter.2.cloned.1.call-start = ((), (), s32[]{:S(2)}) async-start(), calls=%async_computation.1 | async-start | bytes 17825792 | tf_op jit(solution)/shard_map/reduce_scatter | solution.py:54
  12.6 7.3 %copy-start.5 = (s32[1,8]{1,0:T(1,128)S(1)}, s32[1,8]{1,0:T(1,128)}, u32[]{:S(2)}) copy-start(s32[1,8]{1,0:T(1,128)} %param.8) | copy-start | bytes 100
  85.0 1.2 copy-start.4
  85.0 406.3 %all-reduce.3.cloned.1.call-start = ((), (), s32[]{:S(2)}) async-start(), calls=%async_computation.2 | async-start | bytes 2097152 | tf_op jit(solution)/shard_map/psum | solution.py:13
  440.4 105.0 %all-gather.2.cloned.1.call-start = ((), (), s32[]{:S(2)}) async-start(), calls=%async_computation.3 | async-start | bytes 5242880 | tf_op jit(solution)/shard_map/all_gather | solution.py:58
  693.5 5.9 copy-start.2
  707.0 1.2 copy-start.3
  707.0 4.5 copy-start.1
Sparse Core Ops, SparseCore 0:
  85.1 352.7 reduce-scatter.1
  440.5 50.7 all-reduce.2
  493.3 52.0 all-gather.1
where the time goes:
time: 728 us; the launch traced here: 718 us
  waiting for transfers between devices  455 us (62%)
  other arithmetic  128 us (18%)
  local copies, waits for them, and re-layouts  62.9 us (9%)
  matrix products  54.6 us (8%)
  between operations  17.1 us (2%)
    reduce_scatter x1, waiting for transfers between devices, body(): lax.psum_scatter(child_sums, ('prow', 'pcol'), scatter_dimension=0, tiled...  351 us
    another operation x14, other arithmetic, body(): diag_factor = jnp.linalg.cholesky(full_column[:tile_rows])  79.4 us
    all_gather x1, waiting for transfers between devices, body(): full_column = lax.all_gather(column, 'prow', axis=0, tiled=True)  53.6 us
    psum x1, waiting for transfers between devices, spread_2(): return lax.psum(jnp.where(mine, value, jnp.zeros_like(value)), axis)  50.4 us
    another operation x3, other arithmetic, body(): lax.linalg.triangular_solve(diag_factor, full_column, left_side=False, lo...  41.8 us
    dot_general x2, matrix products, body(): jnp.einsum('rbk,kiln,cdl->rcbidn', by_row, blocked, by_col, precision=lax...  25.3 us
    reshape x1, local copies, waits for them, and re-layouts, body(): child_sums = spread.reshape(row_count * col_count, tile_rows, tile_cols)  19.9 us
    transpose x1, local copies, waits for them, and re-layouts, body(): jnp.einsum('rbk,kiln,cdl->rcbidn', by_row, blocked, by_col, precision=lax...  19.8 us
  transfers between devices with their start and end apart: 3, of which 3 were waited for; matrix products, arithmetic and copies ran while one was open for 0% of the time, Pallas kernels for 0%

commit v1 on v0

v1 whole, which is shorter than its diff:
```python
import functools
import itertools
import math

import jax
import jax.numpy as jnp
import numpy as np
from jax import lax
from jax.experimental import pallas as pl
from jax.experimental.pallas import tpu as pltpu
from jax.sharding import PartitionSpec as P

F32 = jnp.float32
BF16 = jnp.bfloat16
SMEM = pl.BlockSpec(memory_space=pltpu.SMEM)
VMEM = pl.BlockSpec(memory_space=pltpu.VMEM)
STRIDE = 256


class Plan:
    def __init__(self, rows, per_tile, slots):
        self.rows, self.per_tile, self.slots = rows, per_tile, slots
        nb = per_tile
        self.diag = [(a, a - s) for s in range(nb) for a in range(s, nb)]
        self.full = [(a, (a + s) % nb) for s in range(nb) for a in range(nb)]
        self.share = (len(self.diag) + 1) // 2
        self.extra = nb * nb - 2 * self.share
        self.pairs = [(h, l) for h in range(1, rows) for l in range(1, h)]
        self.column = max(nb * nb, len(self.pairs) * self.extra)
        self.length = self.column + (rows - 1) * self.share
        total = rows * nb
        table = -np.ones((total, total), np.int32)
        for h in range(1, rows):
            for a in range(nb):
                for b in range(nb):
                    table[h * nb + a, b] = h * STRIDE + a * nb + b
            for e, (a, b) in enumerate(self.diag):
                row = h if e < self.share else 0
                table[h * nb + a, h * nb + b] = row * STRIDE + self.chunk(h) + e % self.share
        for k, (h, l) in enumerate(self.pairs):
            for e, (a, b) in enumerate(self.full):
                if e < self.share:
                    code = h * STRIDE + self.chunk(l) + e
                elif e < 2 * self.share:
                    code = l * STRIDE + self.chunk(h) + e - self.share
                else:
                    code = k * self.extra + e - 2 * self.share
                table[h * nb + a, l * nb + b] = code
        self.table = table
        self.slot_pairs = [(i, j) for i in range(slots) for j in range(i + 1)]
        self.crossing = self.bound()

    def chunk(self, col):
        return self.column + (col - 1) * self.share

    def bound(self):
        total = self.table.shape[0]
        if math.comb(total, self.slots) > 100000:
            return len(self.slot_pairs)
        subsets = np.array(list(itertools.combinations(range(total), self.slots)))
        i, j = np.array(self.slot_pairs).T
        codes = self.table[subsets[:, i], subsets[:, j]]
        most = 0
        for bit in range(self.rows.bit_length() - 1):
            for value in range(2):
                hit = (codes >= 0) & ((codes // STRIDE >> bit) % 2 == value)
                most = max(most, int(hit.sum(1).max()))
        return most


def split(x):
    high = x.astype(BF16)
    return high, (x - high.astype(F32)).astype(BF16)


def dot3(a, b):
    dims = (((1,), (1,)), ((), ()))
    dot = lambda u, v: lax.dot_general(u, v, dims, preferred_element_type=F32)
    return dot(a[0], b[0]) + (dot(a[0], b[1]) + dot(a[1], b[0]))


def dot_nt(a, b):
    return lax.dot_general(
        a, b, (((1,), (1,)), ((), ())), precision=lax.Precision.HIGHEST, preferred_element_type=F32
    )


def dot_nn(a, b):
    return lax.dot_general(
        a, b, (((1,), (0,)), ((), ())), precision=lax.Precision.HIGHEST, preferred_element_type=F32
    )


def head_kernel(place, blocks, mapping, coupling, inverse, parent, out, *, blk, per_tile):
    count = per_tile * blk
    rows = lax.broadcasted_iota(jnp.int32, (count, 1), 0)
    masked = jnp.where(rows < blocks[0] * blk, coupling[...], 0.0)
    factor = split(dot3(split(masked), split(inverse[...])))
    update = dot3(factor, factor)
    lower = [(i, j) for j in range(per_tile) for i in range(j, per_tile)]
    own = (place[0] == 0) & (place[1] == 0)

    @pl.when(own)
    def _():
        for e, (i, j) in enumerate(lower):
            out[e * blk : (e + 1) * blk, :] = parent[i * blk : (i + 1) * blk, j * blk : (j + 1) * blk]

    @pl.when(jnp.logical_not(own))
    def _():
        out[...] = jnp.zeros_like(out)

    for i in range(per_tile):
        for j in range(i + 1):
            p, q = mapping[0, i], mapping[0, j]

            @pl.when((i < blocks[0]) & (p < per_tile))
            def _():
                place_at = q * per_tile - (q * (q - 1)) // 2 + p - q
                window = pl.ds(pl.multiple_of(place_at * blk, blk), blk)
                out[window, :] -= update[i * blk : (i + 1) * blk, j * blk : (j + 1) * blk]


def head(place, blocks, mapping, coupling, inverse, parent, blk, per_tile):
    count = per_tile * blk
    pivots = inverse.shape[0]
    n_lower = per_tile * (per_tile + 1) // 2
    return pl.pallas_call(
        functools.partial(head_kernel, blk=blk, per_tile=per_tile),
        grid=(1,),
        in_specs=[SMEM, SMEM, SMEM]
        + [
            pl.BlockSpec((count, pivots), lambda s: (0, 0)),
            pl.BlockSpec((pivots, pivots), lambda s: (0, 0)),
            pl.BlockSpec(parent.shape, lambda s: (0, 0)),
        ],
        out_specs=pl.BlockSpec((n_lower * blk, blk), lambda s: (0, 0)),
        out_shape=jax.ShapeDtypeStruct((n_lower * blk, blk), F32),
        compiler_params=pltpu.CompilerParams(vmem_limit_bytes=40 * 2**20),
    )(place, blocks, mapping, coupling, inverse, parent)


def lookup(e, slot_i, slot_j, blocks, mapping, table):
    i, j = slot_i[e], slot_j[e]
    p, q = jnp.maximum(mapping[0, i], 0), jnp.maximum(mapping[0, j], 0)
    code = table[p, q]
    return i, j, jnp.where(i < blocks[0], code, -1)


def pack_kernel(
    place, blocks, mapping, slot_i, slot_j, table, coupling, inverse, own, cross0, cross1, high, low, update, *, blk, plan
):
    half = blk // 2
    rows = lax.broadcasted_iota(jnp.int32, (coupling.shape[0], 1), 0)
    masked = jnp.where(rows < blocks[0] * blk, coupling[...], 0.0)
    high[...], low[...] = split(dot3(split(masked), split(inverse[...])))
    width = 2 * blk
    for start in range(0, coupling.shape[0], width):
        cols = slice(start, start + width)
        update[start:, cols] = dot3((high[start:, :], low[start:, :]), (high[cols, :], low[cols, :]))
    row = place[0]

    def tell(e):
        i, j, code = lookup(e, slot_i, slot_j, blocks, mapping, table)
        dest = code // STRIDE
        valid = code >= 0
        return i, j, valid, [valid & (((dest >> bit) ^ (row >> bit)) % 2 == 1) for bit in range(2)]

    def one(e, counts):
        i, j, valid, crosses = tell(e)
        upper = update[pl.ds(pl.multiple_of(i * blk, blk), half), pl.ds(pl.multiple_of(j * blk, blk), blk)]
        lower = update[pl.ds(pl.multiple_of(i * blk + half, half), half), pl.ds(pl.multiple_of(j * blk, blk), blk)]

        @pl.when(valid)
        def _():
            own[0, e] = -upper
            own[1, e] = -lower

        @pl.when(crosses[0])
        def _():
            cross0[counts[0]] = -upper

        @pl.when(crosses[1])
        def _():
            cross1[counts[1]] = -lower

        return tuple(c + x.astype(jnp.int32) for c, x in zip(counts, crosses))

    lax.fori_loop(0, len(plan.slot_pairs), one, (0, 0))


def pack(place, blocks, mapping, tables, coupling, inverse, blk, plan):
    half = blk // 2
    order, pivots = coupling.shape
    count = len(plan.slot_pairs)
    return pl.pallas_call(
        functools.partial(pack_kernel, blk=blk, plan=plan),
        in_specs=[SMEM] * 6 + [VMEM] * 2,
        out_specs=[VMEM] * 3,
        out_shape=[
            jax.ShapeDtypeStruct((2, count, half, blk), F32),
            jax.ShapeDtypeStruct((plan.crossing, half, blk), F32),
            jax.ShapeDtypeStruct((plan.crossing, half, blk), F32),
        ],
        scratch_shapes=[
            pltpu.VMEM((order, pivots), BF16),
            pltpu.VMEM((order, pivots), BF16),
            pltpu.VMEM((order, order), F32),
        ],
        compiler_params=pltpu.CompilerParams(vmem_limit_bytes=48 * 2**20),
    )(place, blocks, mapping, *tables, coupling, inverse)


def merge_kernel(
    place, blocks, mapping, blocks0, mapping0, blocks1, mapping1, slot_i, slot_j, table,
    own, cross0, cross1, parent, keep_out, send_out, both, *, blk, plan,
):
    half = blk // 2
    nb = plan.per_tile
    both[...] = jnp.zeros_like(both)
    row, col = place[0], place[1]
    mine = [row % 2, (row >> 1) % 2]

    @pl.when((col == 0) & (row > 0))
    def _():
        for a in range(nb):
            for b in range(nb):
                for h in range(2):
                    top = a * blk + h * half
                    both[0, h, a * nb + b] = parent[top : top + half, b * blk : (b + 1) * blk]

    def bits(code):
        dest = code // STRIDE
        return [dest % 2, (dest >> 1) % 2], code % STRIDE

    def add(h, other, index, value):
        both[other, h, index] += value

    def one(e, counts):
        _, _, code = lookup(e, slot_i, slot_j, blocks, mapping, table)
        bit, index = bits(code)
        for h in range(2):

            @pl.when((code >= 0) & (bit[h] == mine[h]))
            def _():
                add(h, bit[1 - h] ^ mine[1 - h], index, own[h, e])

        new = []
        for h, (b, m, got) in enumerate([(blocks0, mapping0, cross0), (blocks1, mapping1, cross1)]):
            _, _, code = lookup(e, slot_i, slot_j, b, m, table)
            bit, index = bits(code)
            hit = (code >= 0) & (bit[h] == mine[h])

            @pl.when(hit)
            def _():
                add(h, bit[1 - h] ^ mine[1 - h], index, got[counts[h]])

            new.append(counts[h] + hit.astype(jnp.int32))
        return tuple(new)

    lax.fori_loop(0, len(plan.slot_pairs), one, (0, 0))
    keep_out[...] = both[0]
    send_out[...] = both[1]


def merge(place, own_info, info0, info1, tables, own, cross0, cross1, parent, blk, plan):
    half = blk // 2
    shape = jax.ShapeDtypeStruct((2, plan.length, half, blk), F32)
    return pl.pallas_call(
        functools.partial(merge_kernel, blk=blk, plan=plan),
        in_specs=[SMEM] * 10 + [VMEM] * 4,
        out_specs=[VMEM] * 2,
        out_shape=[shape, shape],
        scratch_shapes=[pltpu.VMEM((2,) + shape.shape, F32)],
        compiler_params=pltpu.CompilerParams(vmem_limit_bytes=48 * 2**20),
    )(place, *own_info, *info0, *info1, *tables, own, cross0, cross1, parent)


def factor_block(a, u_ref, w_ref):
    n = a.shape[0]
    x = (lax.broadcasted_iota(jnp.int32, (n, n), 0) == lax.broadcasted_iota(jnp.int32, (n, n), 1)).astype(F32)
    step = 8
    for t in range(n // step):
        at, xt = a[:step], x[:step]
        cols = [jnp.broadcast_to(at[:, step * t + q : step * t + q + 1], at.shape) for q in range(step)]
        pivot = {(p, q): jnp.broadcast_to(cols[q][p : p + 1], at.shape) for q in range(step) for p in range(q, step)}
        scale, low = [], {}
        for q in range(step):
            scale.append(lax.rsqrt(pivot[q, q]))
            for p in range(q + 1, step):
                low[p, q] = pivot[p, q] * scale[q]
            for p in range(q + 1, step):
                for m in range(q + 1, p + 1):
                    pivot[p, m] = pivot[p, m] - low[p, q] * low[m, q]
        rows_a = [jnp.broadcast_to(at[q : q + 1], at.shape) for q in range(step)]
        rows_x = [jnp.broadcast_to(xt[q : q + 1], xt.shape) for q in range(step)]
        u, w = [], []
        for q in range(step):
            u.append(rows_a[q] * scale[q])
            w.append(rows_x[q] * scale[q])
            for p in range(q + 1, step):
                rows_a[p] = rows_a[p] - low[p, q] * u[q]
                rows_x[p] = rows_x[p] - low[p, q] * w[q]
            u_ref[step * t + q : step * t + q + 1, :] = u[q][:1]
            w_ref[step * t + q : step * t + q + 1, :] = w[q][:1]
        if t == n // step - 1:
            break
        for q in reversed(range(step)):
            u[q] = u[q] * scale[q]
            w[q] = w[q] * scale[q]
            for p in range(q):
                u[p] = u[p] - low[q, p] * u[q]
                w[p] = w[p] - low[q, p] * w[q]
        a, x = a[step:], x[step:]
        cols = [jnp.broadcast_to(a[:, step * t + q : step * t + q + 1], a.shape) for q in range(step)]
        for q in range(step):
            a = a - cols[q] * jnp.broadcast_to(u[q][:1], a.shape)
            x = x - cols[q] * jnp.broadcast_to(w[q][:1], x.shape)


def cholesky_kernel(place, lower, l_ref, x_ref, s, u_ref, w_ref, *, nb):
    n = l_ref.shape[0]
    tiles = n // nb
    part = lower.shape[1]
    at = {}
    e = 0
    for j in range(tiles):
        for i in range(j, tiles):
            at[i, j] = e
            e += 1
    flat = jnp.concatenate([lower[place[0] ^ d] for d in range(lower.shape[0])], 0)
    for (i, j), e in at.items():
        block = flat[e * nb : (e + 1) * nb, :]
        s[i * nb : (i + 1) * nb, j * nb : (j + 1) * nb] = block
        if i > j:
            s[j * nb : (j + 1) * nb, i * nb : (i + 1) * nb] = block.T
    rows = lax.broadcasted_iota(jnp.int32, (n, 1), 0)
    eye = lax.broadcasted_iota(jnp.int32, (n, n), 0) == lax.broadcasted_iota(jnp.int32, (n, n), 1)
    x_ref[...] = eye.astype(F32)
    tri = lax.broadcasted_iota(jnp.int32, (nb, nb), 0) >= lax.broadcasted_iota(jnp.int32, (nb, nb), 1)

    def step(k, _):
        off = pl.multiple_of(k * nb, nb)
        window = pl.ds(off, nb)
        factor_block(s[window, window], u_ref, w_ref)
        w = w_ref[...]
        below = jnp.where(rows >= off + nb, dot_nt(s[:, window], w), 0.0)
        l_ref[:, window] = below
        l_ref[window, window] = jnp.where(tri, u_ref[...].T, 0.0)
        xk = dot_nn(w, x_ref[window, :])
        s[...] -= dot_nt(below, below)
        x_ref[...] -= dot_nn(below, xk)
        x_ref[window, :] = xk
        return 0

    lax.fori_loop(0, tiles, step, 0)


def cholesky(place, lower, n, blk):
    return pl.pallas_call(
        functools.partial(cholesky_kernel, nb=blk),
        in_specs=[SMEM, VMEM],
        out_specs=[VMEM] * 2,
        out_shape=[jax.ShapeDtypeStruct((n, n), F32)] * 2,
        scratch_shapes=[pltpu.VMEM((n, n), F32), pltpu.VMEM((blk, blk), F32), pltpu.VMEM((blk, blk), F32)],
        compiler_params=pltpu.CompilerParams(vmem_limit_bytes=32 * 2**20),
    )(place, lower)


def finish_kernel(
    place, row_list, col_list, share_own, share_other, extra, parent, l_ref, x_ref, out, a_row, a_col, tile, *, blk, plan
):
    half = blk // 2
    nb = plan.per_tile
    row, col = place[0], place[1]

    def put(ref, a, b, upper, lower, sign=None):
        ref[a * blk : a * blk + half, b * blk : (b + 1) * blk] = upper
        ref[a * blk + half : (a + 1) * blk, b * blk : (b + 1) * blk] = lower

    for a in range(nb):
        for b in range(nb):
            put(a_col, a, b, col_list[0, a * nb + b], col_list[1, a * nb + b])

    @pl.when((row == 0) & (col == 0))
    def _():
        out[...] = l_ref[...]

    @pl.when((row == 0) & (col > 0))
    def _():
        out[...] = a_col[...].T

    @pl.when(row > 0)
    def _():
        for a in range(nb):
            for b in range(nb):
                put(a_row, a, b, row_list[0, a * nb + b], row_list[1, a * nb + b])
        a_row[...] = dot_nt(a_row[...], x_ref[...])

    @pl.when((row > 0) & (col == 0))
    def _():
        out[...] = a_row[...]

    @pl.when((row > 0) & (col == row))
    def _():
        for e, (a, b) in enumerate(plan.diag):
            src = share_own if e < plan.share else extra
            at = e % plan.share
            put(tile, a, b, src[0, at], src[1, at])
            if a > b:
                put(tile, b, a, *jnp.split(jnp.concatenate([src[0, at], src[1, at]], 0).T, 2, 0))
        pair = split(a_row[...])
        out[...] = parent[...] + tile[...] - dot3(pair, pair)

    @pl.when((row > 0) & (col > 0) & (col != row))
    def _():
        def fill(high_share, low_share):
            for e, (a, b) in enumerate(plan.full):
                src = [high_share, low_share, extra][min(e // plan.share, 2)]
                at = e - plan.share * min(e // plan.share, 2)
                put(tile, a, b, src[0, at], src[1, at])

        @pl.when(row > col)
        def _():
            fill(share_own, share_other)

        @pl.when(row < col)
        def _():
            fill(share_other, share_own)
            tile[...] = tile[...].T

        product = dot3(split(a_row[...]), split(dot_nt(a_col[...], x_ref[...])))
        out[...] = parent[...] + tile[...] - product


def finish(place, row_list, col_list, share_own, share_other, extra, parent, l, x, blk, plan):
    return pl.pallas_call(
        functools.partial(finish_kernel, blk=blk, plan=plan),
        in_specs=[SMEM] + [VMEM] * 8,
        out_specs=VMEM,
        out_shape=jax.ShapeDtypeStruct(parent.shape, F32),
        scratch_shapes=[pltpu.VMEM(parent.shape, F32)] * 3,
        compiler_params=pltpu.CompilerParams(vmem_limit_bytes=48 * 2**20),
    )(place, row_list, col_list, share_own, share_other, extra, parent, l, x)


def trade(x, axis, bit):
    size = lax.axis_size(axis)
    return lax.ppermute(x, axis, [(d, d ^ bit) for d in range(size)])


def shift(x, axis, by):
    size = lax.axis_size(axis)
    return lax.ppermute(x, axis, [(d, (d + by) % size) for d in range(size)])


def part(x, index, size):
    return lax.dynamic_slice_in_dim(x, index * size, size, 0)


def sum_head(lower):
    rows, cols = lax.axis_size("prow"), lax.axis_size("pcol")
    me = lax.axis_index("prow")
    size = lower.shape[0] // rows
    total = part(lower, me, size)
    for bit in range(1, rows):
        total = total + trade(part(lower, me ^ bit, size), "prow", bit)
    around = [shift(total, "pcol", by) for by in range(1, cols)]
    total = functools.reduce(jnp.add, around, total)
    return jnp.stack([total] + [trade(total, "prow", bit) for bit in range(1, rows)])


def ring_scatter(x, chunk_of):
    cols = lax.axis_size("pcol")
    me = lax.axis_index("pcol")
    total = chunk_of(x, (me - 1) % cols)
    for step in range(1, cols):
        total = shift(total, "pcol", 1) + chunk_of(x, (me - 1 - step) % cols)
    return total


def sum_column(x):
    cols = lax.axis_size("pcol")
    me = lax.axis_index("pcol")
    shape = x.shape
    flat = x.reshape(-1, shape[-1])
    size = flat.shape[0] // cols
    piece = ring_scatter(flat, lambda a, c: part(a, c, size))
    result = lax.dynamic_update_slice_in_dim(jnp.zeros_like(flat), piece, me * size, 0)
    for step in range(1, cols):
        piece = shift(piece, "pcol", 1)
        result = lax.dynamic_update_slice_in_dim(result, piece, (me - step) % cols * size, 0)
    return result.reshape(shape)


def spread_column(x):
    rows, cols = lax.axis_size("prow"), lax.axis_size("pcol")
    me, col = lax.axis_index("prow"), lax.axis_index("pcol")
    move = lambda v, pairs: lax.ppermute(v, ("prow", "pcol"), [(s * cols + c, d * cols + c) for s, d, c in pairs])
    planes = range(1, min(rows, cols))
    first = [move(x[h], [(c, c ^ (1 << h), c) for c in planes]) for h in range(2)]
    second = []
    got = jnp.stack(first)
    for h in range(2):
        src = jnp.where(me == col, x[h], first[h])
        over = 2 >> h
        second.append(
            move(src, [(c, c ^ over, c) for c in planes] + [(c ^ (1 << h), c ^ 3, c) for c in planes])
        )
    halves = []
    for h in range(2):
        near = me == col ^ (1 << h)
        halves.append(jnp.where(me == col, x[h], jnp.where(near, first[h], second[h])))
    return jnp.stack(halves)


def body(child_inverse, child_coupling, child_blocks, child_map, parent_front, plan):
    me, col = lax.axis_index("prow"), lax.axis_index("pcol")
    rows, cols = lax.axis_size("prow"), lax.axis_size("pcol")
    n = parent_front.shape[0]
    blk = child_coupling.shape[1] // child_map.shape[1]
    inverse, coupling = child_inverse[0], child_coupling[0]
    place = jnp.stack([me, col]).astype(jnp.int32)
    slot_i, slot_j = (jnp.asarray(np.array(plan.slot_pairs, np.int32).T[k]) for k in range(2))
    tables = (slot_i, slot_j, jnp.asarray(plan.table))
    info = (child_blocks, child_map)
    info0, info1 = (tuple(trade(v, "prow", bit) for v in info) for bit in (1, 2))

    lower = head(place, *info, coupling, inverse, parent_front, blk, plan.per_tile)
    summed_head = sum_head(lower)
    own, cross0, cross1 = pack(place, *info, tables, coupling, inverse, blk, plan)
    keep, send = merge(
        place, info, info0, info1, tables, own, trade(cross0, "prow", 1), trade(cross1, "prow", 2), parent_front, blk, plan
    )

    def second(cut):
        return jnp.stack([cut(keep[0]) + trade(cut(send[0]), "prow", 2), cut(keep[1]) + trade(cut(send[1]), "prow", 1)])

    column = sum_column(second(lambda v: v[: plan.column]))
    rest = second(lambda v: v[plan.column :])

    def chunk_of(x, c):
        return lax.dynamic_slice_in_dim(x, jnp.maximum(c - 1, 0) * plan.share, plan.share, 1)

    share_own = ring_scatter(rest, chunk_of)
    l, x = cholesky(place, summed_head, n, blk)
    col_list = spread_column(column)

    swap = [(r * cols + c, c * cols + r) for r in range(1, rows) for c in range(1, cols) if r != c]
    share_other = lax.ppermute(share_own, ("prow", "pcol"), swap)
    extra = jnp.zeros((2, plan.extra) + column.shape[2:], F32)
    pair_of = np.zeros((rows, cols), np.int32)
    for k, (h, l_) in enumerate(plan.pairs):
        pair_of[h, l_] = pair_of[l_, h] = k
    wide = jnp.pad(share_own, ((0, 0), (0, plan.extra - plan.share), (0, 0), (0, 0)))
    for r in range(1, rows):
        pair = jnp.asarray(pair_of[r])[col]
        piece = lax.dynamic_slice_in_dim(column, pair * plan.extra, plan.extra, 1)
        got = lax.ppermute(jnp.where(col == r, wide, piece), "prow", [(0, r)])
        extra = extra + got
    return finish(place, column, col_list, share_own, share_other, extra, parent_front, l, x, blk, plan)


def solution(mesh):
    def run(child_inverse, child_coupling, child_blocks, child_map, parent_front):
        rows = mesh.shape["prow"]
        slots = child_map.shape[1]
        blk = child_coupling.shape[1] // slots
        order = parent_front.shape[1]
        plan = Plan(rows, order // rows // blk, slots)
        return jax.shard_map(
            functools.partial(body, plan=plan),
            mesh=mesh,
            in_specs=(
                P(("leaf", "prow", "pcol"), None, None),
                P(("leaf", "prow", "pcol"), None, None),
                P(("leaf", "prow", "pcol")),
                P(("leaf", "prow", "pcol"), None),
                P(("leaf", "prow"), "pcol"),
            ),
            out_specs=P(("leaf", "prow"), "pcol"),
            check_vma=False,
        )(child_inverse, child_coupling, child_blocks, child_map, parent_front)

    return run
```

time: 728 us -> 219 us (0.30)
  the two profiles are of different devices: /device:TPU:0 before, /device:TPU:28 now
where the time goes in v1:
time: 219 us; the launch traced here: 218 us
  waiting for transfers between devices  76.9 us (35%)
  Pallas kernels  56.7 us (26%)
  starting transfers between devices  50.1 us (23%)
  local copies, waits for them, and re-layouts  18.1 us (8%)
  other arithmetic  13.5 us (6%)
  between operations  3.07 us (1%)
    ppermute x16, waiting for transfers between devices, trade(): return lax.ppermute(x, axis, [(d, d ^ bit) for d in range(size)])  33.1 us
    pallas_call x1, Pallas kernels, cholesky(): pl.pallas_call(functools.partial(cholesky_kernel, nb=blk), in_specs=[SMEM...  30.4 us
    ppermute x12, waiting for transfers between devices, shift(): return lax.ppermute(x, axis, [(d, (d + by) % size) for d in range(size)])  26.3 us
    ppermute x16, starting transfers between devices, trade(): return lax.ppermute(x, axis, [(d, d ^ bit) for d in range(size)])  19.9 us
    ppermute x12, starting transfers between devices, shift(): return lax.ppermute(x, axis, [(d, (d + by) % size) for d in range(size)])  13.8 us
    ppermute x4, waiting for transfers between devices, spread_column(): lax.ppermute(v, ('prow', 'pcol'), [(s * cols + c, d * cols + c) for s, d,...  10.3 us
    ppermute x1, starting transfers between devices, body(): share_other = lax.ppermute(share_own, ('prow', 'pcol'), swap)  8.84 us
    pallas_call x1, Pallas kernels, merge(): pl.pallas_call(functools.partial(merge_kernel, blk=blk, plan=plan), in_sp...  8.65 us
  transfers between devices with their start and end apart: 36, of which 15 were waited for; matrix products, arithmetic and copies ran while one was open for 8% of the time, Pallas kernels for 15%

profile of v1, /device:TPU:28, one launch (start us, length us, event | category | flops | bytes accessed | tf_op | source)
XLA Modules:
  0.0 218.5 jit_solution(3630450630999501190)
XLA Ops:
  0.7 1.6 copy-done.1
  2.3 1.2 copy-done.3
  6.2 7.6 %shard_map.109 = (f32[2,36,64,128]{3,2,1,0:T(8,128)}, f32[28,64,128]{2,1,0:T(8,128)S(1)}, f32[28,64,128]{2,1,0:T(8,128)S(1)}) custom-call(s32[2]{0:T(128)S(1)} %pad_add_fusion.place, s32[1]{0:T(128)S(6)} %copy.16.blocks, s32[1,8]{1,0:T(1,128)S(1)} %copy-done.7, s32[36]{0:T(128)S(1)} %copy-done.9, s32[36]{0:T(128)S(1)} %copy-done.10, s32[16,16]{1,0:T(8,128)S(1)} %copy-done.6, ...), custom_call_target="tpu_custom_call" | custom-call | tf_op jit(solution)/shard_map/pallas_call | solution.py:195
  13.8 1.5 collective-permute-start.4
  16.4 1.5 collective-permute-start.1
  17.9 1.5 collective-permute-start.2
  19.4 16.6 %collective-permute-done.blocks0 = s32[1]{0:T(128)} collective-permute-done((s32[1]{0:T(128)}, s32[1]{0:T(128)}, u32[]{:S(2)}, u32[]{:S(2)}) %collective-permute-start) | collective-permute-done | bytes 36 | tf_op jit(solution)/shard_map/ppermute | solution.py:448
  37.3 2.2 collective-permute-done.3.mapping1
  39.5 8.6 %shard_map.110 = (f32[2,33,64,128]{3,2,1,0:T(8,128)S(1)}, f32[2,33,64,128]{3,2,1,0:T(8,128)}) custom-call(s32[2]{0:T(128)S(1)} %pad_add_fusion.place, s32[1]{0:T(128)S(6)} %copy.16.blocks, s32[1,8]{1,0:T(1,128)S(1)} %copy-done.7, s32[1]{0:T(128)} %collective-permute-done.blocks0, s32[1,8]{1,0:T(1,128)S(1)} %collective-permute-done.1.mapping0, ...), custom_call_target="tpu_custom_call" | custom-call | tf_op jit(solution)/shard_map/pallas_call | solution.py:268
  48.1 3.2 %slice_bitcast_fusion.1 = (f32[18,64,128]{2,1,0:T(8,128)}, f32[18,64,128]{2,1,0:T(8,128)}) fusion(f32[2,33,64,128]{3,2,1,0:T(8,128)} %get-tuple-element.16), kind=kLoop, calls=%fused_computation.18 | loop fusion | bytes 2359296 | tf_op jit(solution)/shard_map/slice | solution.py:538
  51.8 1.5 collective-permute-start.7
  53.3 11.2 %collective-permute-done.6 = f32[18,64,128]{2,1,0:T(8,128)} collective-permute-done((f32[18,64,128]{2,1,0:T(8,128)}, f32[18,64,128]{2,1,0:T(8,128)}, u32[]{:S(2)}, u32[]{:S(2)}) %collective-permute-start.6) | collective-permute-done | bytes 589856 | tf_op jit(solution)/shard_map/ppermute | solution.py:448
  64.9 1.5 fusion.1
  66.9 7.3 %collective-permute-done.8 = f32[576,128]{1,0:T(8,128)S(1)} collective-permute-done((f32[576,128]{1,0:T(8,128)S(1)}, f32[576,128]{1,0:T(8,128)S(1)}, u32[]{:S(2)}, u32[]{:S(2)}) %collective-permute-start.8) | collective-permute-done | bytes 294944 | tf_op jit(solution)/shard_map/ppermute | solution.py:453
  75.0 1.2 collective-permute-start.9
  76.2 2.2 %slice_bitcast_fusion.2 = (f32[15,64,128]{2,1,0:T(8,128)}, f32[15,64,128]{2,1,0:T(8,128)}) fusion(f32[2,33,64,128]{3,2,1,0:T(8,128)} %get-tuple-element.16), kind=kLoop, calls=%fused_computation.23 | loop fusion | bytes 1966080 | tf_op jit(solution)/shard_map/slice | solution.py:539
  78.4 1.5 collective-permute-start.19
  80.0 1.5 collective-permute-start.18
  81.5 1.6 copy-done.2
  83.0 2.7 %shard_map.111 = f32[1280,128]{1,0:T(8,128)S(1)} custom-call(s32[2]{0:T(128)S(1)} %pad_add_fusion.place, s32[1]{0:T(128)S(6)} %copy.16.blocks, s32[1,8]{1,0:T(1,128)S(1)} %copy-done.8, f32[1024,512]{1,0:T(8,128)S(1)} %bitcast.54, f32[512,512]{1,0:T(8,128)S(1)} %bitcast.56, f32[512,512]{1,0:T(8,128)S(1)} %copy-done), custom_call_target="tpu_custom_call" | custom-call | tf_op jit(solution)/shard_map/pallas_call | solution.py:127
  85.8 1.1 dynamic-slice_add_fusion.1
  89.1 1.6 fusion.2
  92.3 4.6 %collective-permute-done.10 = f32[576,128]{1,0:T(8,128)S(1)} collective-permute-done((f32[576,128]{1,0:T(8,128)S(1)}, f32[576,128]{1,0:T(8,128)S(1)}, u32[]{:S(2)}, u32[]{:S(2)}) %collective-permute-start.10) | collective-permute-done | bytes 294944 | tf_op jit(solution)/shard_map/ppermute | solution.py:453
  97.0 1.8 constant_dynamic-update-slice_fusion.3
  98.7 1.9 collective-permute-start.11
  101.4 1.6 collective-permute-start.29
  103.5 1.4 collective-permute-start.27
  104.9 1.8 fusion.8
  107.4 2.9 %collective-permute-done.11 = f32[576,128]{1,0:T(8,128)} collective-permute-done((f32[576,128]{1,0:T(8,128)}, f32[576,128]{1,0:T(8,128)}, u32[]{:S(2)}, u32[]{:S(2)}) %collective-permute-start.11) | collective-permute-done | bytes 294944 | tf_op jit(solution)/shard_map/ppermute | solution.py:453
  110.3 2.5 %collective-permute-start.12 = (f32[576,128]{1,0:T(8,128)}, f32[576,128]{1,0:T(8,128)}, u32[]{:S(2)}, u32[]{:S(2)}) collective-permute-start(f32[576,128]{1,0:T(8,128)} %collective-permute-done.11), channel_id=1, source_target_pairs={{0,1},{1,2},{2,3},{3,0},{4,5},{5,6},{6,7},{7,4},{8,9},{9,10},{10,1... | collective-permute-start | bytes 884744 | tf_op jit(solution)/shard_map/ppermute | solution.py:453
  116.7 1.1 add_add_fusion.2
  118.4 3.3 %collective-permute-start.30 = (f32[320,128]{1,0:T(8,128)S(1)}, f32[320,128]{1,0:T(8,128)S(1)}, u32[]{:S(2)}, u32[]{:S(2)}) collective-permute-start(f32[320,128]{1,0:T(8,128)S(1)} %add_add_fusion.2), channel_id=1, source_target_pairs={{0,1},{1,2},{2,3},{3,0},{4,5},{5,6},{6,7},{7,4},{8,9},{9,10},{10,1... | collective-permute-start | bytes 491528 | tf_op jit(solution)/shard_map/ppermute | solution.py:453
  121.7 7.5 %collective-permute-done.12 = f32[576,128]{1,0:T(8,128)} collective-permute-done((f32[576,128]{1,0:T(8,128)}, f32[576,128]{1,0:T(8,128)}, u32[]{:S(2)}, u32[]{:S(2)}) %collective-permute-start.12) | collective-permute-done | bytes 294944 | tf_op jit(solution)/shard_map/ppermute | solution.py:453
  129.2 1.1 fusion.10
  130.3 2.3 %collective-permute-start.22 = (f32[2,5,64,128]{3,2,1,0:T(8,128)S(1)}, f32[2,5,64,128]{3,2,1,0:T(8,128)S(1)}, u32[]{:S(2)}, u32[]{:S(2)}) collective-permute-start(f32[2,5,64,128]{3,2,1,0:T(8,128)S(1)} %fusion.10), channel_id=1, source_target_pairs={{0,1},{1,2},{2,3},{3,0},{4,5},{5,6},{6,7},{7,4},{8,9},{9,10},{10,1... | collective-permute-start | bytes 983048 | tf_op jit(solution)/shard_map/ppermute | solution.py:453
  134.6 4.0 %collective-permute-done.13 = f32[576,128]{1,0:T(8,128)S(1)} collective-permute-done((f32[576,128]{1,0:T(8,128)}, f32[576,128]{1,0:T(8,128)S(1)}, u32[]{:S(2)}, u32[]{:S(2)}) %collective-permute-start.13) | collective-permute-done | bytes 294944 | tf_op jit(solution)/shard_map/ppermute | solution.py:453
  139.6 2.7 %collective-permute-start.35 = (f32[320,128]{1,0:T(8,128)S(1)}, f32[320,128]{1,0:T(8,128)S(1)}, u32[]{:S(2)}, u32[]{:S(2)}) collective-permute-start(f32[320,128]{1,0:T(8,128)S(1)} %add_add_fusion.1), channel_id=1, source_target_pairs={{0,12},{4,8},{8,4},{12,0},{1,13},{5,9},{9,5},{13,1},{2,14},{6,10},... | collective-permute-start | bytes 491528 | tf_op jit(solution)/shard_map/ppermute | solution.py:448
  142.3 2.7 %collective-permute-start.34 = (f32[320,128]{1,0:T(8,128)S(1)}, f32[320,128]{1,0:T(8,128)S(1)}, u32[]{:S(2)}, u32[]{:S(2)}) collective-permute-start(f32[320,128]{1,0:T(8,128)S(1)} %add_add_fusion.1), channel_id=1, source_target_pairs={{0,8},{4,12},{8,0},{12,4},{1,9},{5,13},{9,1},{13,5},{2,10},{6,14},... | collective-permute-start | bytes 491528 | tf_op jit(solution)/shard_map/ppermute | solution.py:448
  145.0 1.3 collective-permute-start.14
  148.6 1.3 collective-permute-start.25
  149.9 10.2 %collective-permute-done.14 = f32[18,64,128]{2,1,0:T(8,128)S(1)} collective-permute-done((f32[18,64,128]{2,1,0:T(8,128)S(1)}, f32[18,64,128]{2,1,0:T(8,128)S(1)}, u32[]{:S(2)}, u32[]{:S(2)}) %collective-permute-start.14) | collective-permute-done | bytes 589856 | tf_op jit(solution)/shard_map/ppermute | solution.py:498
  160.1 1.3 collective-permute-start.17
  161.5 1.5 collective-permute-start.15
  163.1 30.4 %shard_map.112 = (f32[512,512]{1,0:T(8,128)S(1)}, f32[512,512]{1,0:T(8,128)S(1)}) custom-call(s32[2]{0:T(128)S(1)} %pad_add_fusion.place, f32[4,320,128]{2,1,0:T(8,128)S(1)} %pad_maximum_fusion.2.lower), custom_call_target="tpu_custom_call" | custom-call | tf_op jit(solution)/shard_map/pallas_call | solution.py:359
  193.5 8.8 %collective-permute-start.23 = (f32[2,5,64,128]{3,2,1,0:T(8,128)S(1)}, f32[2,5,64,128]{3,2,1,0:T(8,128)S(1)}, u32[]{:S(2)}, u32[]{:S(2)}) collective-permute-start(f32[2,5,64,128]{3,2,1,0:T(8,128)S(1)} %fusion.5.share_own), channel_id=1, source_target_pairs={{6,9},{7,13},{9,6},{11,14},{13,7},{14,11},{22,25},{23,29},{25,22},... | collective-permute-start | bytes 983048 | tf_op jit(solution)/shard_map/ppermute | solution.py:549
  202.7 1.2 pad_maximum_fusion.1.col_list
  203.9 7.2 %collective-permute-done.23.share_other = f32[2,5,64,128]{3,2,1,0:T(8,128)S(1)} collective-permute-done((f32[2,5,64,128]{3,2,1,0:T(8,128)S(1)}, f32[2,5,64,128]{3,2,1,0:T(8,128)S(1)}, u32[]{:S(2)}, u32[]{:S(2)}) %collective-permute-start.23) | collective-permute-done | bytes 327712 | tf_op jit(solution)/shard_map/ppermute | solution.py:549
  211.1 7.4 %shard_map.113 = f32[512,512]{1,0:T(8,128)} custom-call(s32[2]{0:T(128)S(1)} %pad_add_fusion.place, f32[2,18,64,128]{3,2,1,0:T(8,128)S(1)} %bitcast.52, f32[2,18,64,128]{3,2,1,0:T(8,128)} %pad_maximum_fusion.1.col_list, f32[2,5,64,128]{3,2,1,0:T(8,128)S(1)} %fusion.5.share_own, f32[2,5,64,128]{3,2,1,0:T(8,128)S(1)} %collective-permute-done.23.share_other, ...), custom_call_target="tpu_custom_call" | custom-call | tf_op jit(solution)/shard_map/pallas_call | solution.py:436
  (98 shorter events, 21.4 us)
Async XLA Ops:
  0.7 1.6 copy-start.1
  6.2 33.3 %copy-start = (f32[512,512]{1,0:T(8,128)S(1)}, f32[512,512]{1,0:T(8,128)}, u32[]{:S(2)}) copy-start(f32[512,512]{1,0:T(8,128)} %parent.5) | copy-start | bytes 3145732
  13.8 25.6 %collective-permute-start.4 = (f32[28,64,128]{2,1,0:T(8,128)S(1)}, f32[28,64,128]{2,1,0:T(8,128)S(1)}, u32[]{:S(2)}, u32[]{:S(2)}) collective-permute-start(f32[28,64,128]{2,1,0:T(8,128)S(1)} %get-tuple-element.13), channel_id=1, source_target_pairs={{0,4},{4,0},{8,12},{12,8},{1,5},{5,1},{9,13},{13,9},{2,6},{6,2},{1... | collective-permute-start | bytes 2752520 | tf_op jit(solution)/shard_map/ppermute | solution.py:448
  15.3 24.2 %collective-permute-start.5 = (f32[28,64,128]{2,1,0:T(8,128)S(1)}, f32[28,64,128]{2,1,0:T(8,128)S(1)}, u32[]{:S(2)}, u32[]{:S(2)}) collective-permute-start(f32[28,64,128]{2,1,0:T(8,128)S(1)} %get-tuple-element.14), channel_id=1, source_target_pairs={{0,8},{4,12},{8,0},{12,4},{1,9},{5,13},{9,1},{13,5},{2,10},{6,14},... | collective-permute-start | bytes 2752520 | tf_op jit(solution)/shard_map/ppermute | solution.py:448
  15.8 20.1 %collective-permute-start = (s32[1]{0:T(128)}, s32[1]{0:T(128)}, u32[]{:S(2)}, u32[]{:S(2)}) collective-permute-start(s32[1]{0:T(128)} %param.13), channel_id=1, source_target_pairs={{0,4},{4,0},{8,12},{12,8},{1,5},{5,1},{9,13},{13,9},{2,6},{6,2},{1... | collective-permute-start | bytes 20 | tf_op jit(solution)/shard_map/ppermute | solution.py:448
  16.4 20.9 %collective-permute-start.1 = (s32[1,8]{1,0:T(1,128)S(1)}, s32[1,8]{1,0:T(1,128)S(1)}, u32[]{:S(2)}, u32[]{:S(2)}) collective-permute-start(s32[1,8]{1,0:T(1,128)S(1)} %copy-done.7), channel_id=1, source_target_pairs={{0,4},{4,0},{8,12},{12,8},{1,5},{5,1},{9,13},{13,9},{2,6},{6,2},{1... | collective-permute-start | bytes 104 | tf_op jit(solution)/shard_map/ppermute | solution.py:448
  17.9 19.4 %collective-permute-start.2 = (s32[1]{0:T(128)}, s32[1]{0:T(128)}, u32[]{:S(2)}, u32[]{:S(2)}) collective-permute-start(s32[1]{0:T(128)} %param.13), channel_id=1, source_target_pairs={{0,8},{4,12},{8,0},{12,4},{1,9},{5,13},{9,1},{13,5},{2,10},{6,14},... | collective-permute-start | bytes 20 | tf_op jit(solution)/shard_map/ppermute | solution.py:448
  35.9 3.5 %collective-permute-start.3 = (s32[1,8]{1,0:T(1,128)S(1)}, s32[1,8]{1,0:T(1,128)S(1)}, u32[]{:S(2)}, u32[]{:S(2)}) collective-permute-start(s32[1,8]{1,0:T(1,128)S(1)} %copy-done.7), channel_id=1, source_target_pairs={{0,8},{4,12},{8,0},{12,4},{1,9},{5,13},{9,1},{13,5},{2,10},{6,14},... | collective-permute-start | bytes 104 | tf_op jit(solution)/shard_map/ppermute | solution.py:448
  48.1 16.7 %copy-start.5 = (f32[2,33,64,128]{3,2,1,0:T(8,128)}, f32[2,33,64,128]{3,2,1,0:T(8,128)S(1)}, u32[]{:S(2)}) copy-start(f32[2,33,64,128]{3,2,1,0:T(8,128)S(1)} %get-tuple-element.15) | copy-start | bytes 6488068
  51.3 13.2 %collective-permute-start.6 = (f32[18,64,128]{2,1,0:T(8,128)}, f32[18,64,128]{2,1,0:T(8,128)}, u32[]{:S(2)}, u32[]{:S(2)}) collective-permute-start(f32[18,64,128]{2,1,0:T(8,128)} %get-tuple-element.27), channel_id=1, source_target_pairs={{0,8},{4,12},{8,0},{12,4},{1,9},{5,13},{9,1},{13,5},{2,10},{6,14},... | collective-permute-start | bytes 1769480 | tf_op jit(solution)/shard_map/ppermute | solution.py:448
  51.8 13.0 %collective-permute-start.7 = (f32[18,64,128]{2,1,0:T(8,128)}, f32[18,64,128]{2,1,0:T(8,128)}, u32[]{:S(2)}, u32[]{:S(2)}) collective-permute-start(f32[18,64,128]{2,1,0:T(8,128)} %get-tuple-element.28), channel_id=1, source_target_pairs={{0,4},{4,0},{8,12},{12,8},{1,5},{5,1},{9,13},{13,9},{2,6},{6,2},{1... | collective-permute-start | bytes 1769480 | tf_op jit(solution)/shard_map/ppermute | solution.py:448
  66.4 7.8 %copy-start.13 = (f32[2,18,64,128]{3,2,1,0:T(8,128)}, f32[2,18,64,128]{3,2,1,0:T(8,128)S(1)}, u32[]{:S(2)}) copy-start(f32[2,18,64,128]{3,2,1,0:T(8,128)S(1)} %pad_maximum_fusion) | copy-start | bytes 3538948
  66.5 7.7 %collective-permute-start.8 = (f32[576,128]{1,0:T(8,128)S(1)}, f32[576,128]{1,0:T(8,128)S(1)}, u32[]{:S(2)}, u32[]{:S(2)}) collective-permute-start(f32[576,128]{1,0:T(8,128)S(1)} %constant_dynamic-slice_fusion.3), channel_id=1, source_target_pairs={{0,1},{1,2},{2,3},{3,0},{4,5},{5,6},{6,7},{7,4},{8,9},{9,10},{10,1... | collective-permute-start | bytes 884744 | tf_op jit(solution)/shard_map/ppermute | solution.py:453
  75.0 6.5 %copy-start.4 = (f32[1,512,512]{2,1,0:T(8,128)S(1)}, f32[1,512,512]{2,1,0:T(8,128)}, u32[]{:S(2)}) copy-start(f32[1,512,512]{2,1,0:T(8,128)} %param.11) | copy-start | bytes 3145732
  75.0 6.5 %copy-start.8 = (s32[1,8]{1,0:T(1,128)S(1)}, s32[1,8]{1,0:T(1,128)}, u32[]{:S(2)}) copy-start(s32[1,8]{1,0:T(1,128)} %mapping.5) | copy-start | bytes 100
  75.0 10.8 %collective-permute-start.9 = (f32[576,128]{1,0:T(8,128)}, f32[576,128]{1,0:T(8,128)}, u32[]{:S(2)}, u32[]{:S(2)}) collective-permute-start(f32[576,128]{1,0:T(8,128)} %dynamic-slice_add_fusion.2), channel_id=1, source_target_pairs={{0,1},{1,2},{2,3},{3,0},{4,5},{5,6},{6,7},{7,4},{8,9},{9,10},{10,1... | collective-permute-start | bytes 884744 | tf_op jit(solution)/shard_map/ppermute | solution.py:453
  78.4 9.0 %collective-permute-start.19 = (f32[15,64,128]{2,1,0:T(8,128)}, f32[15,64,128]{2,1,0:T(8,128)S(1)}, u32[]{:S(2)}, u32[]{:S(2)}) collective-permute-start(f32[15,64,128]{2,1,0:T(8,128)} %get-tuple-element.23), channel_id=1, source_target_pairs={{0,4},{4,0},{8,12},{12,8},{1,5},{5,1},{9,13},{13,9},{2,6},{6,2},{1... | collective-permute-start | bytes 1474568 | tf_op jit(solution)/shard_map/ppermute | solution.py:448
  80.0 9.1 %collective-permute-start.18 = (f32[15,64,128]{2,1,0:T(8,128)}, f32[15,64,128]{2,1,0:T(8,128)}, u32[]{:S(2)}, u32[]{:S(2)}) collective-permute-start(f32[15,64,128]{2,1,0:T(8,128)} %get-tuple-element.24), channel_id=1, source_target_pairs={{0,8},{4,12},{8,0},{12,4},{1,9},{5,13},{9,1},{13,5},{2,10},{6,14},... | collective-permute-start | bytes 1474568 | tf_op jit(solution)/shard_map/ppermute | solution.py:448
  81.5 1.6 copy-start.2
  86.9 10.0 %collective-permute-start.10 = (f32[576,128]{1,0:T(8,128)S(1)}, f32[576,128]{1,0:T(8,128)S(1)}, u32[]{:S(2)}, u32[]{:S(2)}) collective-permute-start(f32[576,128]{1,0:T(8,128)S(1)} %dynamic-slice_add_fusion.1), channel_id=1, source_target_pairs={{0,1},{1,2},{2,3},{3,0},{4,5},{5,6},{6,7},{7,4},{8,9},{9,10},{10,1... | collective-permute-start | bytes 884744 | tf_op jit(solution)/shard_map/ppermute | solution.py:453
  90.7 6.3 %copy-start.11 = (f32[1,15,64,128]{3,2,1,0:T(8,128)}, f32[1,15,64,128]{3,2,1,0:T(8,128)S(1)}, u32[]{:S(2)}) copy-start(f32[1,15,64,128]{3,2,1,0:T(8,128)S(1)} %get-tuple-element.22) | copy-start | bytes 1474564
  91.6 13.3 %collective-permute-start.20 = (f32[2,5,64,128]{3,2,1,0:T(8,128)}, f32[2,5,64,128]{3,2,1,0:T(8,128)}, u32[]{:S(2)}, u32[]{:S(2)}) collective-permute-start(f32[2,5,64,128]{3,2,1,0:T(8,128)} %fusion.6), channel_id=1, source_target_pairs={{0,1},{1,2},{2,3},{3,0},{4,5},{5,6},{6,7},{7,4},{8,9},{9,10},{10,1... | collective-permute-start | bytes 983048 | tf_op jit(solution)/shard_map/ppermute | solution.py:453
  98.7 14.1 %copy-start.17 = (s32[4]{0:T(128)S(1)}, s32[4]{0:T(128)}, u32[]{:S(2)}) copy-start(s32[4]{0:T(128)} %constant.111.clone) | copy-start | bytes 52
  98.7 15.3 %copy-start.16 = (s32[4]{0:T(128)S(1)}, s32[4]{0:T(128)}, u32[]{:S(2)}) copy-start(s32[4]{0:T(128)} %constant.112.clone) | copy-start | bytes 52
  98.7 16.7 %copy-start.15 = (s32[4]{0:T(128)S(1)}, s32[4]{0:T(128)}, u32[]{:S(2)}) copy-start(s32[4]{0:T(128)} %constant.110.clone) | copy-start | bytes 52
  98.7 11.6 %collective-permute-start.11 = (f32[576,128]{1,0:T(8,128)}, f32[576,128]{1,0:T(8,128)}, u32[]{:S(2)}, u32[]{:S(2)}) collective-permute-start(f32[576,128]{1,0:T(8,128)} %get-tuple-element.20), channel_id=1, source_target_pairs={{0,1},{1,2},{2,3},{3,0},{4,5},{5,6},{6,7},{7,4},{8,9},{9,10},{10,1... | collective-permute-start | bytes 884744 | tf_op jit(solution)/shard_map/ppermute | solution.py:453
  101.4 15.3 %collective-permute-start.29 = (f32[320,128]{1,0:T(8,128)}, f32[320,128]{1,0:T(8,128)}, u32[]{:S(2)}, u32[]{:S(2)}) collective-permute-start(f32[320,128]{1,0:T(8,128)} %get-tuple-element.35), channel_id=1, source_target_pairs={{0,12},{4,8},{8,4},{12,0},{1,13},{5,9},{9,5},{13,1},{2,14},{6,10},... | collective-permute-start | bytes 491528 | tf_op jit(solution)/shard_map/ppermute | solution.py:448
  103.0 13.7 %collective-permute-start.28 = (f32[320,128]{1,0:T(8,128)}, f32[320,128]{1,0:T(8,128)}, u32[]{:S(2)}, u32[]{:S(2)}) collective-permute-start(f32[320,128]{1,0:T(8,128)} %get-tuple-element.36), channel_id=1, source_target_pairs={{0,8},{4,12},{8,0},{12,4},{1,9},{5,13},{9,1},{13,5},{2,10},{6,14},... | collective-permute-start | bytes 491528 | tf_op jit(solution)/shard_map/ppermute | solution.py:448
  103.5 13.2 %collective-permute-start.27 = (f32[320,128]{1,0:T(8,128)S(1)}, f32[320,128]{1,0:T(8,128)}, u32[]{:S(2)}, u32[]{:S(2)}) collective-permute-start(f32[320,128]{1,0:T(8,128)S(1)} %get-tuple-element.34), channel_id=1, source_target_pairs={{0,4},{4,0},{8,12},{12,8},{1,5},{5,1},{9,13},{13,9},{2,6},{6,2},{1... | collective-permute-start | bytes 491528 | tf_op jit(solution)/shard_map/ppermute | solution.py:448
  106.7 22.6 %collective-permute-start.21 = (f32[2,5,64,128]{3,2,1,0:T(8,128)}, f32[2,5,64,128]{3,2,1,0:T(8,128)}, u32[]{:S(2)}, u32[]{:S(2)}) collective-permute-start(f32[2,5,64,128]{3,2,1,0:T(8,128)} %fusion.8), channel_id=1, source_target_pairs={{0,1},{1,2},{2,3},{3,0},{4,5},{5,6},{6,7},{7,4},{8,9},{9,10},{10,1... | collective-permute-start | bytes 983048 | tf_op jit(solution)/shard_map/ppermute | solution.py:453
  110.3 18.9 %collective-permute-start.12 = (f32[576,128]{1,0:T(8,128)}, f32[576,128]{1,0:T(8,128)}, u32[]{:S(2)}, u32[]{:S(2)}) collective-permute-start(f32[576,128]{1,0:T(8,128)} %collective-permute-done.11), channel_id=1, source_target_pairs={{0,1},{1,2},{2,3},{3,0},{4,5},{5,6},{6,7},{7,4},{8,9},{9,10},{10,1... | collective-permute-start | bytes 884744 | tf_op jit(solution)/shard_map/ppermute | solution.py:453
  117.8 21.7 %collective-permute-start.32 = (f32[320,128]{1,0:T(8,128)S(1)}, f32[320,128]{1,0:T(8,128)S(1)}, u32[]{:S(2)}, u32[]{:S(2)}) collective-permute-start(f32[320,128]{1,0:T(8,128)S(1)} %add_add_fusion.2), channel_id=1, source_target_pairs={{0,3},{1,0},{2,1},{3,2},{4,7},{5,4},{6,5},{7,6},{8,11},{9,8},{10,9... | collective-permute-start | bytes 491528 | tf_op jit(solution)/shard_map/ppermute | solution.py:453
  117.9 21.7 %collective-permute-start.31 = (f32[320,128]{1,0:T(8,128)S(1)}, f32[320,128]{1,0:T(8,128)S(1)}, u32[]{:S(2)}, u32[]{:S(2)}) collective-permute-start(f32[320,128]{1,0:T(8,128)S(1)} %add_add_fusion.2), channel_id=1, source_target_pairs={{0,2},{1,3},{2,0},{3,1},{4,6},{5,7},{6,4},{7,5},{8,10},{9,11},{10,... | collective-permute-start | bytes 491528 | tf_op jit(solution)/shard_map/ppermute | solution.py:453
  118.4 21.1 %collective-permute-start.30 = (f32[320,128]{1,0:T(8,128)S(1)}, f32[320,128]{1,0:T(8,128)S(1)}, u32[]{:S(2)}, u32[]{:S(2)}) collective-permute-start(f32[320,128]{1,0:T(8,128)S(1)} %add_add_fusion.2), channel_id=1, source_target_pairs={{0,1},{1,2},{2,3},{3,0},{4,5},{5,6},{6,7},{7,4},{8,9},{9,10},{10,1... | collective-permute-start | bytes 491528 | tf_op jit(solution)/shard_map/ppermute | solution.py:453
  129.2 9.4 %collective-permute-start.13 = (f32[576,128]{1,0:T(8,128)}, f32[576,128]{1,0:T(8,128)S(1)}, u32[]{:S(2)}, u32[]{:S(2)}) collective-permute-start(f32[576,128]{1,0:T(8,128)} %collective-permute-done.12), channel_id=1, source_target_pairs={{0,1},{1,2},{2,3},{3,0},{4,5},{5,6},{6,7},{7,4},{8,9},{9,10},{10,1... | collective-permute-start | bytes 884744 | tf_op jit(solution)/shard_map/ppermute | solution.py:453
  130.3 14.7 %collective-permute-start.22 = (f32[2,5,64,128]{3,2,1,0:T(8,128)S(1)}, f32[2,5,64,128]{3,2,1,0:T(8,128)S(1)}, u32[]{:S(2)}, u32[]{:S(2)}) collective-permute-start(f32[2,5,64,128]{3,2,1,0:T(8,128)S(1)} %fusion.10), channel_id=1, source_target_pairs={{0,1},{1,2},{2,3},{3,0},{4,5},{5,6},{6,7},{7,4},{8,9},{9,10},{10,1... | collective-permute-start | bytes 983048 | tf_op jit(solution)/shard_map/ppermute | solution.py:453
  138.6 7.7 %copy-start.12 = (f32[1,15,64,128]{3,2,1,0:T(8,128)S(1)}, f32[1,15,64,128]{3,2,1,0:T(8,128)}, u32[]{:S(2)}) copy-start(f32[1,15,64,128]{3,2,1,0:T(8,128)} %copy-done.11) | copy-start | bytes 1474564
  138.7 7.8 %collective-permute-start.16 = (f32[18,64,128]{2,1,0:T(8,128)S(1)}, f32[18,64,128]{2,1,0:T(8,128)S(1)}, u32[]{:S(2)}, u32[]{:S(2)}) collective-permute-start(f32[18,64,128]{2,1,0:T(8,128)S(1)} %bitcast.60), channel_id=1, source_target_pairs={{5,13},{10,2},{15,7},{21,29},{26,18},{31,23}} | collective-permute-start | bytes 1769480 | tf_op jit(solution)/shard_map/ppermute | solution.py:498
  139.6 7.6 %collective-permute-start.35 = (f32[320,128]{1,0:T(8,128)S(1)}, f32[320,128]{1,0:T(8,128)S(1)}, u32[]{:S(2)}, u32[]{:S(2)}) collective-permute-start(f32[320,128]{1,0:T(8,128)S(1)} %add_add_fusion.1), channel_id=1, source_target_pairs={{0,12},{4,8},{8,4},{12,0},{1,13},{5,9},{9,5},{13,1},{2,14},{6,10},... | collective-permute-start | bytes 491528 | tf_op jit(solution)/shard_map/ppermute | solution.py:448
  142.3 6.3 %collective-permute-start.34 = (f32[320,128]{1,0:T(8,128)S(1)}, f32[320,128]{1,0:T(8,128)S(1)}, u32[]{:S(2)}, u32[]{:S(2)}) collective-permute-start(f32[320,128]{1,0:T(8,128)S(1)} %add_add_fusion.1), channel_id=1, source_target_pairs={{0,8},{4,12},{8,0},{12,4},{1,9},{5,13},{9,1},{13,5},{2,10},{6,14},... | collective-permute-start | bytes 491528 | tf_op jit(solution)/shard_map/ppermute | solution.py:448
  145.0 16.5 %collective-permute-start.33 = (f32[320,128]{1,0:T(8,128)S(1)}, f32[320,128]{1,0:T(8,128)S(1)}, u32[]{:S(2)}, u32[]{:S(2)}) collective-permute-start(f32[320,128]{1,0:T(8,128)S(1)} %add_add_fusion.1), channel_id=1, source_target_pairs={{0,4},{4,0},{8,12},{12,8},{1,5},{5,1},{9,13},{13,9},{2,6},{6,2},{1... | collective-permute-start | bytes 491528 | tf_op jit(solution)/shard_map/ppermute | solution.py:448
  145.0 15.1 %collective-permute-start.14 = (f32[18,64,128]{2,1,0:T(8,128)S(1)}, f32[18,64,128]{2,1,0:T(8,128)S(1)}, u32[]{:S(2)}, u32[]{:S(2)}) collective-permute-start(f32[18,64,128]{2,1,0:T(8,128)S(1)} %bitcast.57), channel_id=1, source_target_pairs={{5,1},{10,14},{15,11},{21,17},{26,30},{31,27}} | collective-permute-start | bytes 1769480 | tf_op jit(solution)/shard_map/ppermute | solution.py:498
  146.5 47.0 %collective-permute-start.26 = (f32[2,6,64,128]{3,2,1,0:T(8,128)S(1)}, f32[2,6,64,128]{3,2,1,0:T(8,128)S(1)}, u32[]{:S(2)}, u32[]{:S(2)}) collective-permute-start(f32[2,6,64,128]{3,2,1,0:T(8,128)S(1)} %get-tuple-element.30), channel_id=1, source_target_pairs={{0,12},{1,13},{2,14},{3,15},{16,28},{17,29},{18,30},{19,31}} | collective-permute-start | bytes 1179656 | tf_op jit(solution)/shard_map/ppermute | solution.py:558
  147.3 55.1 %collective-permute-start.24 = (f32[2,6,64,128]{3,2,1,0:T(8,128)S(1)}, f32[2,6,64,128]{3,2,1,0:T(8,128)S(1)}, u32[]{:S(2)}, u32[]{:S(2)}) collective-permute-start(f32[2,6,64,128]{3,2,1,0:T(8,128)S(1)} %get-tuple-element.31), channel_id=1, source_target_pairs={{0,4},{1,5},{2,6},{3,7},{16,20},{17,21},{18,22},{19,23}} | collective-permute-start | bytes 1179656 | tf_op jit(solution)/shard_map/ppermute | solution.py:558
  148.6 53.7 %collective-permute-start.25 = (f32[2,6,64,128]{3,2,1,0:T(8,128)S(1)}, f32[2,6,64,128]{3,2,1,0:T(8,128)S(1)}, u32[]{:S(2)}, u32[]{:S(2)}) collective-permute-start(f32[2,6,64,128]{3,2,1,0:T(8,128)S(1)} %get-tuple-element.29), channel_id=1, source_target_pairs={{0,8},{1,9},{2,10},{3,11},{16,24},{17,25},{18,26},{19,27}} | collective-permute-start | bytes 1179656 | tf_op jit(solution)/shard_map/ppermute | solution.py:558
  160.1 42.3 %collective-permute-start.17 = (f32[18,64,128]{2,1,0:T(8,128)S(1)}, f32[18,64,128]{2,1,0:T(8,128)S(1)}, u32[]{:S(2)}, u32[]{:S(2)}) collective-permute-start(f32[18,64,128]{2,1,0:T(8,128)S(1)} %broadcast_select_fusion), channel_id=1, source_target_pairs={{5,1},{10,14},{15,11},{13,9},{2,6},{7,3},{21,17},{26,30},{31,27},{... | collective-permute-start | bytes 1769480 | tf_op jit(solution)/shard_map/ppermute | solution.py:498
  161.5 41.1 %collective-permute-start.15 = (f32[18,64,128]{2,1,0:T(8,128)S(1)}, f32[18,64,128]{2,1,0:T(8,128)S(1)}, u32[]{:S(2)}, u32[]{:S(2)}) collective-permute-start(f32[18,64,128]{2,1,0:T(8,128)S(1)} %broadcast_select_fusion.1), channel_id=1, source_target_pairs={{5,13},{10,2},{15,7},{1,9},{14,6},{11,3},{21,29},{26,18},{31,23},{... | collective-permute-start | bytes 1769480 | tf_op jit(solution)/shard_map/ppermute | solution.py:498
  193.5 17.6 %collective-permute-start.23 = (f32[2,5,64,128]{3,2,1,0:T(8,128)S(1)}, f32[2,5,64,128]{3,2,1,0:T(8,128)S(1)}, u32[]{:S(2)}, u32[]{:S(2)}) collective-permute-start(f32[2,5,64,128]{3,2,1,0:T(8,128)S(1)} %fusion.5.share_own), channel_id=1, source_target_pairs={{6,9},{7,13},{9,6},{11,14},{13,7},{14,11},{22,25},{23,29},{25,22},... | collective-permute-start | bytes 983048 | tf_op jit(solution)/shard_map/ppermute | solution.py:549
  (6 other events, 4.7 us)

commit v2 on v0

v2 whole, which is shorter than its diff:
```python
import functools

import jax
import jax.numpy as jnp
import numpy as np
from jax import lax
from jax.experimental import pallas as pl
from jax.experimental.pallas import tpu as pltpu
from jax.sharding import Mesh
from jax.sharding import PartitionSpec as P

F32 = jnp.float32
BF16 = jnp.bfloat16
SMEM = pl.BlockSpec(memory_space=pltpu.SMEM)
VMEM = pl.BlockSpec(memory_space=pltpu.VMEM)
GROUP = ("prow", "near")


def vmem(megabytes):
    return pltpu.CompilerParams(vmem_limit_bytes=megabytes * 2**20)


class Plan:
    def __init__(self, rows, near, far, per_tile, slots, blk):
        self.rows, self.near, self.far = rows, near, far
        self.per_tile, self.slots, self.blk = per_tile, slots, blk
        self.members = rows * near
        self.strip = blk // self.members
        nb = per_tile
        self.lower = [(a, b) for b in range(nb) for a in range(b, nb)]
        self.full = [(a, b) for a in range(nb) for b in range(nb)]
        self.pairs = [(h, l) for h in range(1, rows) for l in range(1, h)]
        self.n_head = len(self.lower)
        self.n_column = (rows - 1) * nb * nb
        self.n_rest = (rows - 1) * len(self.lower) + len(self.pairs) * nb * nb
        self.total = self.n_head + self.n_column + self.n_rest
        self.slot_pairs = [(i, j) for j in range(slots) for i in range(j, slots)]
        table = np.full((rows * nb + 1, rows * nb + 1), self.total, np.int32)
        rest = self.n_head + self.n_column
        for r in range(rows):
            for e, (a, b) in enumerate(self.lower):
                at = e if r == 0 else rest + self.rest_at(r, r) + e
                table[r * nb + a + 1, r * nb + b + 1] = at
        for h in range(1, rows):
            for l in range(h):
                for e, (a, b) in enumerate(self.full):
                    at = self.n_head + (h - 1) * nb * nb + e if l == 0 else rest + self.rest_at(h, l) + e
                    table[h * nb + a + 1, l * nb + b + 1] = at
        self.table = table

    def rest_at(self, r, c):
        if r == 0 or c == 0:
            return 0
        if r == c:
            return (r - 1) * len(self.lower)
        k = self.pairs.index((max(r, c), min(r, c)))
        return (self.rows - 1) * len(self.lower) + k * len(self.full)


def split(x):
    high = x.astype(BF16)
    return high, (x - high.astype(F32)).astype(BF16)


def dot3(a, b):
    dims = (((1,), (1,)), ((), ()))
    dot = lambda u, v: lax.dot_general(u, v, dims, preferred_element_type=F32)
    return dot(a[0], b[0]) + (dot(a[0], b[1]) + dot(a[1], b[0]))


def dot_nt(a, b):
    return lax.dot_general(
        a, b, (((1,), (1,)), ((), ())), precision=lax.Precision.HIGHEST, preferred_element_type=F32
    )


def dot_nn(a, b):
    return lax.dot_general(
        a, b, (((1,), (0,)), ((), ())), precision=lax.Precision.HIGHEST, preferred_element_type=F32
    )


def parent_kernel(mapping, parent, out, *, plan):
    nb, blk, size = plan.per_tile, plan.blk, plan.strip
    lanes = lax.broadcasted_iota(jnp.int32, (size, blk), 1)
    coded = jnp.zeros((size, blk), F32)
    for s in range(plan.slots):
        coded = jnp.where(lanes == s, mapping[0, s].astype(F32), coded)
    for d in range(plan.members):
        for e, (a, b) in enumerate(plan.full):
            top = a * blk + d * size
            out[d, e] = parent[top : top + size, b * blk : (b + 1) * blk]
        out[d, len(plan.full)] = coded


def parent_strips(mapping, parent, plan):
    return pl.pallas_call(
        functools.partial(parent_kernel, plan=plan),
        in_specs=[SMEM, VMEM],
        out_specs=VMEM,
        out_shape=jax.ShapeDtypeStruct((plan.members, len(plan.full) + 1, plan.strip, plan.blk), F32),
        compiler_params=vmem(16),
    )(mapping, parent)


def update_kernel(blocks, coupling, inverse, out, high, low, update, *, plan):
    blk, size = plan.blk, plan.strip
    order = coupling.shape[0]
    rows = lax.broadcasted_iota(jnp.int32, (order, 1), 0)
    masked = jnp.where(rows < blocks[0] * blk, coupling[...], 0.0)
    high[...], low[...] = split(dot3(split(masked), split(inverse[...])))
    width = 2 * blk
    for start in range(0, order, width):
        cols = slice(start, start + width)
        update[start:, cols] = dot3((high[start:, :], low[start:, :]), (high[cols, :], low[cols, :]))
    for e, (i, j) in enumerate(plan.slot_pairs):
        for d in range(plan.members):
            top = i * blk + d * size
            out[d, e] = update[top : top + size, j * blk : (j + 1) * blk]


def update_strips(blocks, coupling, inverse, plan):
    order, pivots = coupling.shape
    shape = (plan.members, len(plan.slot_pairs), plan.strip, plan.blk)
    return pl.pallas_call(
        functools.partial(update_kernel, plan=plan),
        in_specs=[SMEM, VMEM, VMEM],
        out_specs=VMEM,
        out_shape=jax.ShapeDtypeStruct(shape, F32),
        scratch_shapes=[
            pltpu.VMEM((order, pivots), BF16),
            pltpu.VMEM((order, pivots), BF16),
            pltpu.VMEM((order, order), F32),
        ],
        compiler_params=vmem(40),
    )(blocks, coupling, inverse)


def merge_kernel(place, maps, table, strips, parents, head, column, rest, total, *, plan):
    nb = plan.per_tile
    total[...] = jnp.zeros_like(total)

    @pl.when(place[1] == 0)
    def _():
        for e, (a, b) in enumerate(plan.lower):
            total[e] = parents[0, a * nb + b]
        for r in range(1, plan.rows):
            for e in range(nb * nb):
                total[plan.n_head + (r - 1) * nb * nb + e] = parents[r * plan.near, e]

    def one(source, _):
        ids = [maps[source, s] + 1 for s in range(plan.slots)]
        for e, (i, j) in enumerate(plan.slot_pairs):
            at = table[ids[i], ids[j]]
            total[at] -= strips[source, e]
        return 0

    lax.fori_loop(0, plan.members, one, 0)
    head[...] = total[: plan.n_head]
    column[...] = total[plan.n_head : plan.n_head + plan.n_column]
    rest[...] = total[plan.n_head + plan.n_column : plan.total]


def merge(place, maps, strips, parents, plan):
    tail = (plan.strip, plan.blk)
    return pl.pallas_call(
        functools.partial(merge_kernel, plan=plan),
        in_specs=[SMEM] * 3 + [VMEM] * 2,
        out_specs=[VMEM] * 3,
        out_shape=[jax.ShapeDtypeStruct((n,) + tail, F32) for n in (plan.n_head, plan.n_column, plan.n_rest)],
        scratch_shapes=[pltpu.VMEM((plan.total + 1,) + tail, F32)],
        compiler_params=vmem(24),
    )(place, maps, jnp.asarray(plan.table), strips, parents)


def column_kernel(place, mine, other, out, total, *, plan):
    nb2 = len(plan.full)
    total[...] = mine[...] + other[...]
    for r in range(plan.rows):
        for n in range(plan.near):
            d = r * plan.near + n
            out[d, :nb2] = total[max(r - 1, 0) * nb2 : max(r - 1, 0) * nb2 + nb2]
            col = jnp.maximum(place[1] * plan.near + n - 1, 0)
            out[d, nb2:] = total[pl.ds(col * nb2, nb2)]


def column_strips(place, mine, other, plan):
    return pl.pallas_call(
        functools.partial(column_kernel, plan=plan),
        in_specs=[SMEM] + [VMEM] * 2,
        out_specs=VMEM,
        out_shape=jax.ShapeDtypeStruct((plan.members, 2 * len(plan.full)) + mine.shape[1:], F32),
        scratch_shapes=[pltpu.VMEM(mine.shape, F32)],
        compiler_params=vmem(16),
    )(place, mine, other)


def rest_kernel(place, starts, mine, other, out, total, *, plan):
    nb2 = len(plan.full)
    total[...] = mine[...] + other[...]
    for r in range(plan.rows):
        for n in range(plan.near):
            out[r * plan.near + n] = total[pl.ds(starts[place[1] * plan.near + n, r], nb2)]


def rest_strips(place, mine, other, plan):
    cols = plan.near * plan.far
    starts = np.array([[plan.rest_at(r, c) for r in range(plan.rows)] for c in range(cols)], np.int32)
    return pl.pallas_call(
        functools.partial(rest_kernel, plan=plan),
        in_specs=[SMEM] * 2 + [VMEM] * 2,
        out_specs=VMEM,
        out_shape=jax.ShapeDtypeStruct((plan.members, len(plan.full)) + mine.shape[1:], F32),
        scratch_shapes=[pltpu.VMEM(mine.shape, F32)],
        compiler_params=vmem(16),
    )(place, jnp.asarray(starts), mine, other)


def factor_block(a, u_ref, w_ref):
    n = a.shape[0]
    x = (lax.broadcasted_iota(jnp.int32, (n, n), 0) == lax.broadcasted_iota(jnp.int32, (n, n), 1)).astype(F32)
    step = 8
    for t in range(n // step):
        at, xt = a[:step], x[:step]
        cols = [jnp.broadcast_to(at[:, step * t + q : step * t + q + 1], at.shape) for q in range(step)]
        pivot = {(p, q): jnp.broadcast_to(cols[q][p : p + 1], at.shape) for q in range(step) for p in range(q, step)}
        scale, low = [], {}
        for q in range(step):
            scale.append(lax.rsqrt(pivot[q, q]))
            for p in range(q + 1, step):
                low[p, q] = pivot[p, q] * scale[q]
            for p in range(q + 1, step):
                for m in range(q + 1, p + 1):
                    pivot[p, m] = pivot[p, m] - low[p, q] * low[m, q]
        rows_a = [jnp.broadcast_to(at[q : q + 1], at.shape) for q in range(step)]
        rows_x = [jnp.broadcast_to(xt[q : q + 1], xt.shape) for q in range(step)]
        u, w = [], []
        for q in range(step):
            u.append(rows_a[q] * scale[q])
            w.append(rows_x[q] * scale[q])
            for p in range(q + 1, step):
                rows_a[p] = rows_a[p] - low[p, q] * u[q]
                rows_x[p] = rows_x[p] - low[p, q] * w[q]
            u_ref[step * t + q : step * t + q + 1, :] = u[q][:1]
            w_ref[step * t + q : step * t + q + 1, :] = w[q][:1]
        if t == n // step - 1:
            break
        for q in reversed(range(step)):
            u[q] = u[q] * scale[q]
            w[q] = w[q] * scale[q]
            for p in range(q):
                u[p] = u[p] - low[q, p] * u[q]
                w[p] = w[p] - low[q, p] * w[q]
        a, x = a[step:], x[step:]
        cols = [jnp.broadcast_to(a[:, step * t + q : step * t + q + 1], a.shape) for q in range(step)]
        for q in range(step):
            a = a - cols[q] * jnp.broadcast_to(u[q][:1], a.shape)
            x = x - cols[q] * jnp.broadcast_to(w[q][:1], x.shape)


def cholesky_kernel(lower, l_ref, x_ref, s, u_ref, w_ref, *, plan):
    n = l_ref.shape[0]
    nb = plan.blk
    size = plan.strip
    for e, (i, j) in enumerate(plan.lower):
        rows = slice(i * nb, (i + 1) * nb)
        cols = slice(j * nb, (j + 1) * nb)
        block = jnp.concatenate([lower[d, e] for d in range(plan.members)], 0)
        s[rows, cols] = block
        if i > j:
            s[cols, rows] = block.T
    rows = lax.broadcasted_iota(jnp.int32, (n, 1), 0)
    eye = lax.broadcasted_iota(jnp.int32, (n, n), 0) == lax.broadcasted_iota(jnp.int32, (n, n), 1)
    x_ref[...] = eye.astype(F32)
    tri = lax.broadcasted_iota(jnp.int32, (nb, nb), 0) >= lax.broadcasted_iota(jnp.int32, (nb, nb), 1)

    def step(k, _):
        off = pl.multiple_of(k * nb, nb)
        window = pl.ds(off, nb)
        factor_block(s[window, window], u_ref, w_ref)
        w = w_ref[...]
        below = jnp.where(rows >= off + nb, dot_nt(s[:, window], w), 0.0)
        l_ref[:, window] = below
        l_ref[window, window] = jnp.where(tri, u_ref[...].T, 0.0)
        xk = dot_nn(w, x_ref[window, :])
        s[...] -= dot_nt(below, below)
        x_ref[...] -= dot_nn(below, xk)
        x_ref[window, :] = xk
        return 0

    lax.fori_loop(0, n // nb, step, 0)


def cholesky(lower, n, plan):
    blk = plan.blk
    return pl.pallas_call(
        functools.partial(cholesky_kernel, plan=plan),
        in_specs=[VMEM],
        out_specs=[VMEM] * 2,
        out_shape=[jax.ShapeDtypeStruct((n, n), F32)] * 2,
        scratch_shapes=[pltpu.VMEM((n, n), F32), pltpu.VMEM((blk, blk), F32), pltpu.VMEM((blk, blk), F32)],
        compiler_params=vmem(24),
    )(lower)


def finish_kernel(place, columns, rests, parent, l_ref, x_ref, out, a_row, a_col, tile, *, plan):
    nb, blk, size = plan.per_tile, plan.blk, plan.strip
    nb2 = nb * nb
    row = place[0]
    col = place[1] * plan.near + place[2]

    def put(ref, source, first, blocks):
        for e, (a, b) in enumerate(blocks):
            for d in range(plan.members):
                top = a * blk + d * size
                ref[top : top + size, b * blk : (b + 1) * blk] = source[d, first + e]

    @pl.when((row == 0) & (col == 0))
    def _():
        out[...] = l_ref[...]

    @pl.when((row == 0) & (col > 0))
    def _():
        put(a_col, columns, nb2, plan.full)
        out[...] = a_col[...].T

    @pl.when(row > 0)
    def _():
        put(a_row, columns, 0, plan.full)
        a_row[...] = dot_nt(a_row[...], x_ref[...])

    @pl.when((row > 0) & (col == 0))
    def _():
        out[...] = a_row[...]

    @pl.when((row > 0) & (col == row))
    def _():
        put(tile, rests, 0, plan.lower)
        for a, b in plan.lower:
            if a > b:
                tile[b * blk : (b + 1) * blk, a * blk : (a + 1) * blk] = tile[
                    a * blk : (a + 1) * blk, b * blk : (b + 1) * blk
                ].T
        pair = split(a_row[...])
        out[...] = parent[...] + tile[...] - dot3(pair, pair)

    @pl.when((row > 0) & (col > 0) & (col != row))
    def _():
        put(a_col, columns, nb2, plan.full)
        put(tile, rests, 0, plan.full)

        @pl.when(row < col)
        def _():
            tile[...] = tile[...].T

        product = dot3(split(a_row[...]), split(dot_nt(a_col[...], x_ref[...])))
        out[...] = parent[...] + tile[...] - product


def finish(place, columns, rests, parent, l, x, plan):
    return pl.pallas_call(
        functools.partial(finish_kernel, plan=plan),
        in_specs=[SMEM] + [VMEM] * 5,
        out_specs=VMEM,
        out_shape=jax.ShapeDtypeStruct(parent.shape, F32),
        scratch_shapes=[pltpu.VMEM(parent.shape, F32)] * 3,
        compiler_params=vmem(32),
    )(place, columns, rests, parent, l, x)


def all_to_all(x):
    return lax.all_to_all(x, GROUP, 0, 0, tiled=True)


def across(x, plan):
    others = [
        lax.ppermute(x, "far", [(f, (f + by) % plan.far) for f in range(plan.far)]) for by in range(1, plan.far)
    ]
    return functools.reduce(jnp.add, others)


def body(child_inverse, child_coupling, child_blocks, child_map, parent_front, plan):
    place = jnp.stack([lax.axis_index(a) for a in ("prow", "far", "near")]).astype(jnp.int32)
    parents = all_to_all(parent_strips(child_map, parent_front, plan))
    maps = parents[:, len(plan.full), 0, : plan.slots].astype(jnp.int32)
    strips = all_to_all(update_strips(child_blocks, child_coupling[0], child_inverse[0], plan))
    head, column, rest = merge(place, maps, strips, parents, plan)
    head = head + across(head, plan)
    heads = all_to_all(jnp.broadcast_to(head, (plan.members,) + head.shape))
    l, x = cholesky(heads, parent_front.shape[0], plan)
    columns = all_to_all(column_strips(place, column, across(column, plan), plan))
    rests = all_to_all(rest_strips(place, rest, across(rest, plan), plan))
    return finish(place, columns, rests, parent_front, l, x, plan)


def solution(mesh):
    rows, cols = mesh.shape["prow"], mesh.shape["pcol"]
    near = 2 if cols % 2 == 0 else 1
    fine = Mesh(
        mesh.devices.reshape(mesh.shape["leaf"], rows, cols // near, near), ("leaf", "prow", "far", "near")
    )
    device = P(("leaf", "prow", "far", "near"))

    def run(child_inverse, child_coupling, child_blocks, child_map, parent_front):
        slots = child_map.shape[1]
        blk = child_coupling.shape[1] // slots
        plan = Plan(rows, near, cols // near, parent_front.shape[1] // cols // blk, slots, blk)
        tile = P(("leaf", "prow"), ("far", "near"))
        return jax.shard_map(
            functools.partial(body, plan=plan),
            mesh=fine,
            in_specs=(device, device, device, device, tile),
            out_specs=tile,
            check_vma=False,
        )(child_inverse, child_coupling, child_blocks, child_map, parent_front)

    return run
```

time: 728 us -> 183 us (0.25)
  the two profiles are of different devices: /device:TPU:0 before, /device:TPU:12 now
where the time goes in v2:
time: 183 us; the launch traced here: 182 us
  waiting for transfers between devices  82.2 us (45%)
  Pallas kernels  48 us (26%)
  starting transfers between devices  35.6 us (19%)
  local copies, waits for them, and re-layouts  15.6 us (9%)
    ppermute x3, waiting for transfers between devices, across(): lax.ppermute(x, 'far', [(f, (f + by) % plan.far) for f in range(plan.far)])  48.4 us
    all_to_all x5, waiting for transfers between devices, all_to_all(): return lax.all_to_all(x, GROUP, 0, 0, tiled=True)  33.8 us
    pallas_call x1, Pallas kernels, cholesky(): pl.pallas_call(functools.partial(cholesky_kernel, plan=plan), in_specs=[V...  29.8 us
    all_to_all x5, starting transfers between devices, all_to_all(): return lax.all_to_all(x, GROUP, 0, 0, tiled=True)  27.4 us
    unnamed x40, local copies, waits for them, and re-layouts  14.7 us
    ppermute x3, starting transfers between devices, across(): lax.ppermute(x, 'far', [(f, (f + by) % plan.far) for f in range(plan.far)])  8.2 us
    pallas_call x1, Pallas kernels, finish(): pl.pallas_call(functools.partial(finish_kernel, plan=plan), in_specs=[SME...  6.56 us
    pallas_call x1, Pallas kernels, update_strips(): pl.pallas_call(functools.partial(update_kernel, plan=plan), in_specs=[SME...  3.86 us
  transfers between devices with their start and end apart: 8, of which 5 were waited for; matrix products, arithmetic and copies ran while one was open for 0% of the time, Pallas kernels for 21%

profile of v2, /device:TPU:12, one launch (start us, length us, event | category | flops | bytes accessed | tf_op | source)
XLA Modules:
  0.0 182.2 jit_solution(16473628033002866186)
XLA Ops:
  0.0 1.2 copy-done.1
  1.2 0.7 copy-done.19
  1.9 1.6 shard_map.73
  3.5 5.1 %all-to-all-start = ((f32[8,17,16,128]{3,2,1,0:T(8,128)}), f32[8,17,16,128]{3,2,1,0:T(8,128)S(1)}, u32[]{:S(2)}, u32[]{:S(2)}) async-start(f32[8,17,16,128]{3,2,1,0:T(8,128)} %shard_map.73), calls=%async_computation | async-start | bytes 2228224 | tf_op jit(solution)/shard_map/all_to_all | solution.py:372
  9.3 0.0 copy-done.7
  9.3 0.0 copy-start.8
  9.3 1.2 copy-done.8
  10.5 3.9 %shard_map.74 = f32[8,36,16,128]{3,2,1,0:T(8,128)S(1)} custom-call(s32[1]{0:T(128)S(6)} %copy.8.blocks, f32[1024,512]{1,0:T(8,128)S(1)} %bitcast.6, f32[512,512]{1,0:T(8,128)S(1)} %bitcast.7), custom_call_target="tpu_custom_call" | custom-call | tf_op jit(solution)/shard_map/pallas_call | solution.py:125
  14.4 0.0 copy-start
  14.4 1.4 copy-done
  15.8 6.5 %all-to-all-done.parents = f32[8,17,16,128]{3,2,1,0:T(8,128)S(1)} async-done(((f32[8,17,16,128]{3,2,1,0:T(8,128)}), f32[8,17,16,128]{3,2,1,0:T(8,128)S(1)}, u32[]{:S(2)}, u32[]{:S(2)}) %all-to-all-start) | async-done | bytes 1114144 | tf_op jit(solution)/shard_map/all_to_all | solution.py:372
  22.3 5.9 %all-to-all-start.1 = ((f32[8,36,16,128]{3,2,1,0:T(8,128)}), f32[8,36,16,128]{3,2,1,0:T(8,128)S(1)}, u32[]{:S(2)}, u32[]{:S(2)}) async-start(f32[8,36,16,128]{3,2,1,0:T(8,128)} %copy-done), calls=%async_computation.1 | async-start | bytes 4718592 | tf_op jit(solution)/shard_map/all_to_all | solution.py:372
  28.2 0.1 pad_add_fusion.place
  28.3 27.2 %all-to-all-done.1.strips = f32[8,36,16,128]{3,2,1,0:T(8,128)S(1)} async-done(((f32[8,36,16,128]{3,2,1,0:T(8,128)}), f32[8,36,16,128]{3,2,1,0:T(8,128)S(1)}, u32[]{:S(2)}, u32[]{:S(2)}) %all-to-all-start.1) | async-done | bytes 2359328 | tf_op jit(solution)/shard_map/all_to_all | solution.py:372
  55.5 0.0 copy-done.17
  55.6 2.5 %shard_map.75 = (f32[10,16,128]{2,1,0:T(8,128)S(1)}, f32[48,16,128]{2,1,0:T(8,128)S(1)}, f32[78,16,128]{2,1,0:T(8,128)S(1)}) custom-call(s32[3]{0:T(128)S(1)} %pad_add_fusion.place, s32[8,8]{1,0:T(8,128)S(1)} %bitcast.8, s32[17,17]{1,0:T(8,128)S(1)} %copy-done.17, f32[8,36,16,128]{3,2,1,0:T(8,128)S(1)} %all-to-all-done.1.strips, ...), custom_call_target="tpu_custom_call" | custom-call | tf_op jit(solution)/shard_map/pallas_call | solution.py:166
  58.0 0.0 copy-start.13
  58.0 0.8 copy-done.13
  58.9 0.8 copy-done.15
  59.6 2.4 %collective-permute-start.2 = (f32[10,16,128]{2,1,0:T(8,128)S(1)}, f32[10,16,128]{2,1,0:T(8,128)S(1)}, u32[]{:S(2)}, u32[]{:S(2)}) collective-permute-start(f32[10,16,128]{2,1,0:T(8,128)S(1)} %get-tuple-element.12), channel_id=1, source_target_pairs={{0,2},{2,0},{1,3},{3,1},{4,6},{6,4},{5,7},{7,5},{8,10},{10,8},{9,1... | collective-permute-start | bytes 245768 | tf_op jit(solution)/shard_map/ppermute | solution.py:377
  62.0 2.9 %collective-permute-done.2 = f32[10,16,128]{2,1,0:T(8,128)S(1)} collective-permute-done((f32[10,16,128]{2,1,0:T(8,128)S(1)}, f32[10,16,128]{2,1,0:T(8,128)S(1)}, u32[]{:S(2)}, u32[]{:S(2)}) %collective-permute-start.2) | collective-permute-done | bytes 81952 | tf_op jit(solution)/shard_map/ppermute | solution.py:377
  65.0 0.9 broadcast_in_dim.3
  65.9 6.4 %all-to-all-start.4 = ((f32[8,10,16,128]{3,2,1,0:T(8,128)}), f32[8,10,16,128]{3,2,1,0:T(8,128)S(1)}, u32[]{:S(2)}, u32[]{:S(2)}) async-start(f32[8,10,16,128]{3,2,1,0:T(8,128)} %broadcast_in_dim.3), calls=%async_computation.4 | async-start | bytes 1310720 | tf_op jit(solution)/shard_map/all_to_all | solution.py:372
  72.3 0.0 copy-done.14
  72.3 2.4 %collective-permute-start.1 = (f32[78,16,128]{2,1,0:T(8,128)S(1)}, f32[78,16,128]{2,1,0:T(8,128)S(1)}, u32[]{:S(2)}, u32[]{:S(2)}) collective-permute-start(f32[78,16,128]{2,1,0:T(8,128)S(1)} %copy-done.14), channel_id=1, source_target_pairs={{0,2},{2,0},{1,3},{3,1},{4,6},{6,4},{5,7},{7,5},{8,10},{10,8},{9,1... | collective-permute-start | bytes 1916936 | tf_op jit(solution)/shard_map/ppermute | solution.py:377
  74.7 26.5 %collective-permute-done.1.other = f32[78,16,128]{2,1,0:T(8,128)S(1)} collective-permute-done((f32[78,16,128]{2,1,0:T(8,128)S(1)}, f32[78,16,128]{2,1,0:T(8,128)S(1)}, u32[]{:S(2)}, u32[]{:S(2)}) %collective-permute-start.1) | collective-permute-done | bytes 639008 | tf_op jit(solution)/shard_map/ppermute | solution.py:377
  101.2 0.0 copy-done.18
  101.2 1.7 shard_map.77
  102.9 0.0 all-to-all-done.4.lower
  102.9 0.9 copy-done.5
  103.8 5.1 %all-to-all-start.3 = ((f32[8,16,16,128]{3,2,1,0:T(8,128)}), f32[8,16,16,128]{3,2,1,0:T(8,128)S(1)}, u32[]{:S(2)}, u32[]{:S(2)}) async-start(f32[8,16,16,128]{3,2,1,0:T(8,128)} %shard_map.77), calls=%async_computation.3 | async-start | bytes 2097152 | tf_op jit(solution)/shard_map/all_to_all | solution.py:372
  108.9 0.0 copy-done.16
  108.9 3.4 %collective-permute-start = (f32[48,16,128]{2,1,0:T(8,128)S(1)}, f32[48,16,128]{2,1,0:T(8,128)S(1)}, u32[]{:S(2)}, u32[]{:S(2)}) collective-permute-start(f32[48,16,128]{2,1,0:T(8,128)S(1)} %copy-done.16), channel_id=1, source_target_pairs={{0,2},{2,0},{1,3},{3,1},{4,6},{6,4},{5,7},{7,5},{8,10},{10,8},{9,1... | collective-permute-start | bytes 1179656 | tf_op jit(solution)/shard_map/ppermute | solution.py:377
  112.3 18.9 %collective-permute-done.other = f32[48,16,128]{2,1,0:T(8,128)S(1)} collective-permute-done((f32[48,16,128]{2,1,0:T(8,128)S(1)}, f32[48,16,128]{2,1,0:T(8,128)S(1)}, u32[]{:S(2)}, u32[]{:S(2)}) %collective-permute-start) | collective-permute-done | bytes 393248 | tf_op jit(solution)/shard_map/ppermute | solution.py:377
  131.2 2.1 %shard_map.76 = f32[8,32,16,128]{3,2,1,0:T(8,128)} custom-call(s32[3]{0:T(128)S(1)} %pad_add_fusion.place, f32[48,16,128]{2,1,0:T(8,128)S(1)} %copy-done.16, f32[48,16,128]{2,1,0:T(8,128)S(1)} %collective-permute-done.other), custom_call_target="tpu_custom_call" | custom-call | tf_op jit(solution)/shard_map/pallas_call | solution.py:188
  133.2 0.0 all-to-all-done.3.rests
  133.2 1.0 copy-done.3
  134.2 4.9 %all-to-all-start.2 = ((f32[8,32,16,128]{3,2,1,0:T(8,128)}), f32[8,32,16,128]{3,2,1,0:T(8,128)S(1)}, u32[]{:S(2)}, u32[]{:S(2)}) async-start(f32[8,32,16,128]{3,2,1,0:T(8,128)} %shard_map.76), calls=%async_computation.2 | async-start | bytes 4194304 | tf_op jit(solution)/shard_map/all_to_all | solution.py:372
  139.1 1.1 copy-done.6
  140.1 29.8 %shard_map.78 = (f32[512,512]{1,0:T(8,128)S(1)}, f32[512,512]{1,0:T(8,128)S(1)}) custom-call(f32[8,10,16,128]{3,2,1,0:T(8,128)S(1)} %copy-done.6), custom_call_target="tpu_custom_call" | custom-call | tf_op jit(solution)/shard_map/pallas_call | solution.py:296
  170.0 0.0 copy-start.9
  170.0 1.0 copy-done.9
  171.0 1.0 copy-done.11
  171.9 0.0 all-to-all-done.2.columns
  171.9 1.2 copy-done.4
  173.2 1.2 copy-done.10
  174.4 1.2 copy-done.12
  175.6 6.6 %shard_map.79 = f32[512,512]{1,0:T(8,128)} custom-call(s32[3]{0:T(128)S(1)} %pad_add_fusion.place, f32[8,32,16,128]{3,2,1,0:T(8,128)S(1)} %all-to-all-done.2.columns, f32[8,16,16,128]{3,2,1,0:T(8,128)S(1)} %copy-done.4, f32[512,512]{1,0:T(8,128)S(1)} %copy-done.2, f32[512,512]{1,0:T(8,128)S(1)} %copy-done.10, f32[512,512]{1,0:T(8,128)S(1)} %copy-done.12), custom_call_target="tpu_custom_call" | custom-call | tf_op jit(solution)/shard_map/pallas_call | solution.py:361
  (19 shorter events, 0.0 us)
Async XLA Ops:
  0.0 1.2 copy-start.1
  1.2 0.7 copy-start.19
  1.9 7.4 %copy-start.7 = (f32[1,1024,512]{2,1,0:T(8,128)S(1)}, f32[1,1024,512]{2,1,0:T(8,128)}, u32[]{:S(2)}) copy-start(f32[1,1024,512]{2,1,0:T(8,128)} %param.8) | copy-start | bytes 6291460
  3.5 18.9 %all-to-all-start = ((f32[8,17,16,128]{3,2,1,0:T(8,128)}), f32[8,17,16,128]{3,2,1,0:T(8,128)S(1)}, u32[]{:S(2)}, u32[]{:S(2)}) async-start(f32[8,17,16,128]{3,2,1,0:T(8,128)} %shard_map.73), calls=%async_computation | async-start | bytes 2228224 | tf_op jit(solution)/shard_map/all_to_all | solution.py:372
  9.3 1.2 copy-start.8
  14.4 1.4 copy-start
  15.8 39.8 %copy-start.17 = (s32[17,17]{1,0:T(8,128)S(1)}, s32[17,17]{1,0:T(8,128)}, u32[]{:S(2)}) copy-start(s32[17,17]{1,0:T(8,128)} %constant.15.clone.table) | copy-start | bytes 3472
  22.3 33.2 %all-to-all-start.1 = ((f32[8,36,16,128]{3,2,1,0:T(8,128)}), f32[8,36,16,128]{3,2,1,0:T(8,128)S(1)}, u32[]{:S(2)}, u32[]{:S(2)}) async-start(f32[8,36,16,128]{3,2,1,0:T(8,128)} %copy-done), calls=%async_computation.1 | async-start | bytes 4718592 | tf_op jit(solution)/shard_map/all_to_all | solution.py:372
  55.6 45.7 %copy-start.18 = (s32[4,4]{1,0:T(4,128)S(1)}, s32[4,4]{1,0:T(4,128)}, u32[]{:S(2)}) copy-start(s32[4,4]{1,0:T(4,128)} %constant.16.clone.starts) | copy-start | bytes 196
  58.0 0.8 copy-start.13
  58.8 0.8 copy-start.15
  59.6 12.7 %copy-start.14 = (f32[78,16,128]{2,1,0:T(8,128)S(1)}, f32[78,16,128]{2,1,0:T(8,128)}, u32[]{:S(2)}) copy-start(f32[78,16,128]{2,1,0:T(8,128)} %copy-done.13) | copy-start | bytes 1916932
  59.6 5.4 %collective-permute-start.2 = (f32[10,16,128]{2,1,0:T(8,128)S(1)}, f32[10,16,128]{2,1,0:T(8,128)S(1)}, u32[]{:S(2)}, u32[]{:S(2)}) collective-permute-start(f32[10,16,128]{2,1,0:T(8,128)S(1)} %get-tuple-element.12), channel_id=1, source_target_pairs={{0,2},{2,0},{1,3},{3,1},{4,6},{6,4},{5,7},{7,5},{8,10},{10,8},{9,1... | collective-permute-start | bytes 245768 | tf_op jit(solution)/shard_map/ppermute | solution.py:377
  65.9 37.0 %all-to-all-start.4 = ((f32[8,10,16,128]{3,2,1,0:T(8,128)}), f32[8,10,16,128]{3,2,1,0:T(8,128)S(1)}, u32[]{:S(2)}, u32[]{:S(2)}) async-start(f32[8,10,16,128]{3,2,1,0:T(8,128)} %broadcast_in_dim.3), calls=%async_computation.4 | async-start | bytes 1310720 | tf_op jit(solution)/shard_map/all_to_all | solution.py:372
  72.3 36.6 %copy-start.16 = (f32[48,16,128]{2,1,0:T(8,128)S(1)}, f32[48,16,128]{2,1,0:T(8,128)}, u32[]{:S(2)}) copy-start(f32[48,16,128]{2,1,0:T(8,128)} %copy-done.15) | copy-start | bytes 1179652
  72.3 28.9 %collective-permute-start.1 = (f32[78,16,128]{2,1,0:T(8,128)S(1)}, f32[78,16,128]{2,1,0:T(8,128)S(1)}, u32[]{:S(2)}, u32[]{:S(2)}) collective-permute-start(f32[78,16,128]{2,1,0:T(8,128)S(1)} %copy-done.14), channel_id=1, source_target_pairs={{0,2},{2,0},{1,3},{3,1},{4,6},{6,4},{5,7},{7,5},{8,10},{10,8},{9,1... | collective-permute-start | bytes 1916936 | tf_op jit(solution)/shard_map/ppermute | solution.py:377
  102.9 0.9 copy-start.5
  103.8 29.4 %all-to-all-start.3 = ((f32[8,16,16,128]{3,2,1,0:T(8,128)}), f32[8,16,16,128]{3,2,1,0:T(8,128)S(1)}, u32[]{:S(2)}, u32[]{:S(2)}) async-start(f32[8,16,16,128]{3,2,1,0:T(8,128)} %shard_map.77), calls=%async_computation.3 | async-start | bytes 2097152 | tf_op jit(solution)/shard_map/all_to_all | solution.py:372
  108.9 22.3 %collective-permute-start = (f32[48,16,128]{2,1,0:T(8,128)S(1)}, f32[48,16,128]{2,1,0:T(8,128)S(1)}, u32[]{:S(2)}, u32[]{:S(2)}) collective-permute-start(f32[48,16,128]{2,1,0:T(8,128)S(1)} %copy-done.16), channel_id=1, source_target_pairs={{0,2},{2,0},{1,3},{3,1},{4,6},{6,4},{5,7},{7,5},{8,10},{10,8},{9,1... | collective-permute-start | bytes 1179656 | tf_op jit(solution)/shard_map/ppermute | solution.py:377
  133.2 38.7 %copy-start.2 = (f32[512,512]{1,0:T(8,128)S(1)}, f32[512,512]{1,0:T(8,128)}, u32[]{:S(2)}) copy-start(f32[512,512]{1,0:T(8,128)} %parent.3) | copy-start | bytes 3145732
  133.2 1.0 copy-start.3
  134.2 37.7 %all-to-all-start.2 = ((f32[8,32,16,128]{3,2,1,0:T(8,128)}), f32[8,32,16,128]{3,2,1,0:T(8,128)S(1)}, u32[]{:S(2)}, u32[]{:S(2)}) async-start(f32[8,32,16,128]{3,2,1,0:T(8,128)} %shard_map.76), calls=%async_computation.2 | async-start | bytes 4194304 | tf_op jit(solution)/shard_map/all_to_all | solution.py:372
  139.1 1.1 copy-start.6
  170.0 1.0 copy-start.9
  171.0 1.0 copy-start.11
  171.9 1.2 copy-start.4
  173.2 1.2 copy-start.10
  174.4 1.2 copy-start.12

commit v3 on v2

--- a/solution.py
+++ b/solution.py
@@ -13,6 +13,7 @@
 BF16 = jnp.bfloat16
 SMEM = pl.BlockSpec(memory_space=pltpu.SMEM)
 VMEM = pl.BlockSpec(memory_space=pltpu.VMEM)
+AFTER = pl.BlockSpec(memory_space=pl.ANY)
 GROUP = ("prow", "near")
 
 
@@ -34,6 +35,8 @@
         self.n_column = (rows - 1) * nb * nb
         self.n_rest = (rows - 1) * len(self.lower) + len(self.pairs) * nb * nb
         self.total = self.n_head + self.n_column + self.n_rest
+        self.first = len(self.full) // 2
+        self.n_parent = max(len(self.lower), len(self.full) - self.first)
         self.slot_pairs = [(i, j) for j in range(slots) for i in range(j, slots)]
         table = np.full((rows * nb + 1, rows * nb + 1), self.total, np.int32)
         rest = self.n_head + self.n_column
@@ -80,30 +83,7 @@
     )
 
 
-def parent_kernel(mapping, parent, out, *, plan):
-    nb, blk, size = plan.per_tile, plan.blk, plan.strip
-    lanes = lax.broadcasted_iota(jnp.int32, (size, blk), 1)
-    coded = jnp.zeros((size, blk), F32)
-    for s in range(plan.slots):
-        coded = jnp.where(lanes == s, mapping[0, s].astype(F32), coded)
-    for d in range(plan.members):
-        for e, (a, b) in enumerate(plan.full):
-            top = a * blk + d * size
-            out[d, e] = parent[top : top + size, b * blk : (b + 1) * blk]
-        out[d, len(plan.full)] = coded
-
-
-def parent_strips(mapping, parent, plan):
-    return pl.pallas_call(
-        functools.partial(parent_kernel, plan=plan),
-        in_specs=[SMEM, VMEM],
-        out_specs=VMEM,
-        out_shape=jax.ShapeDtypeStruct((plan.members, len(plan.full) + 1, plan.strip, plan.blk), F32),
-        compiler_params=vmem(16),
-    )(mapping, parent)
-
-
-def update_kernel(blocks, coupling, inverse, out, high, low, update, *, plan):
+def update_kernel(place, blocks, mapping, coupling, inverse, parent, out, high, low, update, *, plan):
     blk, size = plan.blk, plan.strip
     order = coupling.shape[0]
     rows = lax.broadcasted_iota(jnp.int32, (order, 1), 0)
@@ -118,13 +98,43 @@
             top = i * blk + d * size
             out[d, e] = update[top : top + size, j * blk : (j + 1) * blk]
 
-
-def update_strips(blocks, coupling, inverse, plan):
+    base = len(plan.slot_pairs)
+    row, col = place[0], place[1] * plan.near + place[2]
+
+    def send(blocks, transposed):
+        for e, (a, b) in enumerate(blocks):
+            p, q = (b, a) if transposed else (a, b)
+            block = parent[p * blk : (p + 1) * blk, q * blk : (q + 1) * blk]
+            block = block.T if transposed else block
+            for d in range(plan.members):
+                out[d, base + e] = block[d * size : (d + 1) * size]
+
+    @pl.when((row == 0) & (col == 0))
+    def _():
+        send(plan.lower, False)
+
+    @pl.when((row > 0) & (col == 0))
+    def _():
+        send(plan.full[: plan.first], False)
+
+    @pl.when((row == 0) & (col > 0))
+    def _():
+        send(plan.full[plan.first :], True)
+
+    lanes = lax.broadcasted_iota(jnp.int32, (size, blk), 1)
+    coded = jnp.zeros((size, blk), F32)
+    for s in range(plan.slots):
+        coded = jnp.where(lanes == s, mapping[0, s].astype(F32), coded)
+    for d in range(plan.members):
+        out[d, base + plan.n_parent] = coded
+
+
+def update_strips(place, blocks, mapping, coupling, inverse, parent, plan):
     order, pivots = coupling.shape
-    shape = (plan.members, len(plan.slot_pairs), plan.strip, plan.blk)
+    shape = (plan.members, len(plan.slot_pairs) + plan.n_parent + 1, plan.strip, plan.blk)
     return pl.pallas_call(
         functools.partial(update_kernel, plan=plan),
-        in_specs=[SMEM, VMEM, VMEM],
+        in_specs=[SMEM] * 3 + [VMEM] * 3,
         out_specs=VMEM,
         out_shape=jax.ShapeDtypeStruct(shape, F32),
         scratch_shapes=[
@@ -133,20 +143,30 @@
             pltpu.VMEM((order, order), F32),
         ],
         compiler_params=vmem(40),
-    )(blocks, coupling, inverse)
-
-
-def merge_kernel(place, maps, table, strips, parents, head, column, rest, total, *, plan):
-    nb = plan.per_tile
+    )(place, blocks, mapping, coupling, inverse, parent)
+
+
+def merge_kernel(place, maps, table, strips, *refs, plan, rest):
+    total = refs[-1]
+    nb2 = len(plan.full)
     total[...] = jnp.zeros_like(total)
-
-    @pl.when(place[1] == 0)
-    def _():
-        for e, (a, b) in enumerate(plan.lower):
-            total[e] = parents[0, a * nb + b]
-        for r in range(1, plan.rows):
-            for e in range(nb * nb):
-                total[plan.n_head + (r - 1) * nb * nb + e] = parents[r * plan.near, e]
+    if not rest:
+        base = len(plan.slot_pairs)
+
+        @pl.when(place[1] == 0)
+        def _():
+            for e in range(plan.n_head):
+                total[e] = strips[0, base + e]
+            for r in range(1, plan.rows):
+                for e in range(plan.first):
+                    total[plan.n_head + (r - 1) * nb2 + e] = strips[r * plan.near, base + e]
+
+        for c in range(1, plan.rows):
+
+            @pl.when(place[1] == c // plan.near)
+            def _():
+                for e in range(plan.first, nb2):
+                    total[plan.n_head + (c - 1) * nb2 + e] = strips[c % plan.near, base + e - plan.first]
 
     def one(source, _):
         ids = [maps[source, s] + 1 for s in range(plan.slots)]
@@ -156,21 +176,30 @@
         return 0
 
     lax.fori_loop(0, plan.members, one, 0)
-    head[...] = total[: plan.n_head]
-    column[...] = total[plan.n_head : plan.n_head + plan.n_column]
-    rest[...] = total[plan.n_head + plan.n_column : plan.total]
-
-
-def merge(place, maps, strips, parents, plan):
+    if rest:
+        refs[-2][...] = total[: plan.n_rest]
+    else:
+        refs[0][...] = total[: plan.n_head]
+        refs[1][...] = total[plan.n_head : plan.n_head + plan.n_column]
+
+
+def merge(place, maps, strips, plan, rest, after=()):
     tail = (plan.strip, plan.blk)
-    return pl.pallas_call(
-        functools.partial(merge_kernel, plan=plan),
-        in_specs=[SMEM] * 3 + [VMEM] * 2,
-        out_specs=[VMEM] * 3,
-        out_shape=[jax.ShapeDtypeStruct((n,) + tail, F32) for n in (plan.n_head, plan.n_column, plan.n_rest)],
-        scratch_shapes=[pltpu.VMEM((plan.total + 1,) + tail, F32)],
+    begin = plan.n_head + plan.n_column
+    if rest:
+        counts = [plan.n_rest]
+        table = np.where(plan.table >= begin, plan.table - begin, plan.n_rest)
+    else:
+        counts = [plan.n_head, plan.n_column]
+        table = np.minimum(plan.table, begin)
+    return pl.pallas_call(
+        functools.partial(merge_kernel, plan=plan, rest=rest),
+        in_specs=[SMEM] * 3 + [VMEM] + [AFTER] * len(after),
+        out_specs=[VMEM] * len(counts),
+        out_shape=[jax.ShapeDtypeStruct((n,) + tail, F32) for n in counts],
+        scratch_shapes=[pltpu.VMEM((sum(counts) + 1,) + tail, F32)],
         compiler_params=vmem(24),
-    )(place, maps, jnp.asarray(plan.table), strips, parents)
+    )(place, maps, jnp.asarray(table.astype(np.int32)), strips, *after)
 
 
 def column_kernel(place, mine, other, out, total, *, plan):
@@ -195,7 +224,7 @@
     )(place, mine, other)
 
 
-def rest_kernel(place, starts, mine, other, out, total, *, plan):
+def rest_kernel(place, starts, mine, other, after, out, total, *, plan):
     nb2 = len(plan.full)
     total[...] = mine[...] + other[...]
     for r in range(plan.rows):
@@ -203,17 +232,17 @@
             out[r * plan.near + n] = total[pl.ds(starts[place[1] * plan.near + n, r], nb2)]
 
 
-def rest_strips(place, mine, other, plan):
+def rest_strips(place, mine, other, plan, after):
     cols = plan.near * plan.far
     starts = np.array([[plan.rest_at(r, c) for r in range(plan.rows)] for c in range(cols)], np.int32)
     return pl.pallas_call(
         functools.partial(rest_kernel, plan=plan),
-        in_specs=[SMEM] * 2 + [VMEM] * 2,
+        in_specs=[SMEM] * 2 + [VMEM] * 2 + [AFTER],
         out_specs=VMEM,
         out_shape=jax.ShapeDtypeStruct((plan.members, len(plan.full)) + mine.shape[1:], F32),
         scratch_shapes=[pltpu.VMEM(mine.shape, F32)],
         compiler_params=vmem(16),
-    )(place, jnp.asarray(starts), mine, other)
+    )(place, jnp.asarray(starts), mine, other, after)
 
 
 def factor_block(a, u_ref, w_ref):
@@ -258,7 +287,7 @@
             x = x - cols[q] * jnp.broadcast_to(w[q][:1], x.shape)
 
 
-def cholesky_kernel(lower, l_ref, x_ref, s, u_ref, w_ref, *, plan):
+def cholesky_kernel(lower, after, l_ref, x_ref, s, u_ref, w_ref, *, plan):
     n = l_ref.shape[0]
     nb = plan.blk
     size = plan.strip
@@ -291,42 +320,43 @@
     lax.fori_loop(0, n // nb, step, 0)
 
 
-def cholesky(lower, n, plan):
+def cholesky(lower, n, plan, after):
     blk = plan.blk
     return pl.pallas_call(
         functools.partial(cholesky_kernel, plan=plan),
-        in_specs=[VMEM],
+        in_specs=[VMEM, AFTER],
         out_specs=[VMEM] * 2,
         out_shape=[jax.ShapeDtypeStruct((n, n), F32)] * 2,
         scratch_shapes=[pltpu.VMEM((n, n), F32), pltpu.VMEM((blk, blk), F32), pltpu.VMEM((blk, blk), F32)],
         compiler_params=vmem(24),
-    )(lower)
-
-
-def finish_kernel(place, columns, rests, parent, l_ref, x_ref, out, a_row, a_col, tile, *, plan):
-    nb, blk, size = plan.per_tile, plan.blk, plan.strip
-    nb2 = nb * nb
+    )(lower, after)
+
+
+def put(ref, source, first, blocks, plan):
+    blk, size = plan.blk, plan.strip
+    for e, (a, b) in enumerate(blocks):
+        for d in range(plan.members):
+            top = a * blk + d * size
+            ref[top : top + size, b * blk : (b + 1) * blk] = source[d, first + e]
+
+
+def panel_kernel(place, columns, parent, l_ref, x_ref, out, a_row, a_col, *, plan):
+    nb2 = len(plan.full)
     row = place[0]
     col = place[1] * plan.near + place[2]
 
-    def put(ref, source, first, blocks):
-        for e, (a, b) in enumerate(blocks):
-            for d in range(plan.members):
-                top = a * blk + d * size
-                ref[top : top + size, b * blk : (b + 1) * blk] = source[d, first + e]
-
     @pl.when((row == 0) & (col == 0))
     def _():
         out[...] = l_ref[...]
 
     @pl.when((row == 0) & (col > 0))
     def _():
-        put(a_col, columns, nb2, plan.full)
+        put(a_col, columns, nb2, plan.full, plan)
         out[...] = a_col[...].T
 
     @pl.when(row > 0)
     def _():
-        put(a_row, columns, 0, plan.full)
+        put(a_row, columns, 0, plan.full, plan)
         a_row[...] = dot_nt(a_row[...], x_ref[...])
 
     @pl.when((row > 0) & (col == 0))
@@ -335,37 +365,65 @@
 
     @pl.when((row > 0) & (col == row))
     def _():
-        put(tile, rests, 0, plan.lower)
+        pair = split(a_row[...])
+        out[...] = parent[...] - dot3(pair, pair)
+
+    @pl.when((row > 0) & (col > 0) & (col != row))
+    def _():
+        put(a_col, columns, nb2, plan.full, plan)
+        out[...] = parent[...] - dot3(split(a_row[...]), split(dot_nt(a_col[...], x_ref[...])))
+
+
+def panel(place, columns, parent, l, x, plan):
+    return pl.pallas_call(
+        functools.partial(panel_kernel, plan=plan),
+        in_specs=[SMEM] + [VMEM] * 4,
+        out_specs=VMEM,
+        out_shape=jax.ShapeDtypeStruct(parent.shape, F32),
+        scratch_shapes=[pltpu.VMEM(parent.shape, F32)] * 2,
+        compiler_params=vmem(32),
+    )(place, columns, parent, l, x)
+
+
+def finish_kernel(place, rests, base, out, tile, *, plan):
+    blk = plan.blk
+    row = place[0]
+    col = place[1] * plan.near + place[2]
+
+    @pl.when((row == 0) | (col == 0))
+    def _():
+        out[...] = base[...]
+
+    @pl.when((row > 0) & (col == row))
+    def _():
+        put(tile, rests, 0, plan.lower, plan)
         for a, b in plan.lower:
             if a > b:
                 tile[b * blk : (b + 1) * blk, a * blk : (a + 1) * blk] = tile[
                     a * blk : (a + 1) * blk, b * blk : (b + 1) * blk
                 ].T
-        pair = split(a_row[...])
-        out[...] = parent[...] + tile[...] - dot3(pair, pair)
-
-    @pl.when((row > 0) & (col > 0) & (col != row))
-    def _():
-        put(a_col, columns, nb2, plan.full)
-        put(tile, rests, 0, plan.full)
-
-        @pl.when(row < col)
-        def _():
-            tile[...] = tile[...].T
-
-        product = dot3(split(a_row[...]), split(dot_nt(a_col[...], x_ref[...])))
-        out[...] = parent[...] + tile[...] - product
-
-
-def finish(place, columns, rests, parent, l, x, plan):
+        out[...] = base[...] + tile[...]
+
+    @pl.when((row > col) & (col > 0))
+    def _():
+        put(tile, rests, 0, plan.full, plan)
+        out[...] = base[...] + tile[...]
+
+    @pl.when((row > 0) & (row < col))
+    def _():
+        put(tile, rests, 0, plan.full, plan)
+        out[...] = base[...] + tile[...].T
+
+
+def finish(place, rests, base, plan):
     return pl.pallas_call(
         functools.partial(finish_kernel, plan=plan),
-        in_specs=[SMEM] + [VMEM] * 5,
+        in_specs=[SMEM] + [VMEM] * 2,
         out_specs=VMEM,
-        out_shape=jax.ShapeDtypeStruct(parent.shape, F32),
-        scratch_shapes=[pltpu.VMEM(parent.shape, F32)] * 3,
-        compiler_params=vmem(32),
-    )(place, columns, rests, parent, l, x)
+        out_shape=jax.ShapeDtypeStruct(base.shape, F32),
+        scratch_shapes=[pltpu.VMEM(base.shape, F32)],
+        compiler_params=vmem(24),
+    )(place, rests, base)
 
 
 def all_to_all(x):
@@ -381,16 +439,20 @@
 
 def body(child_inverse, child_coupling, child_blocks, child_map, parent_front, plan):
     place = jnp.stack([lax.axis_index(a) for a in ("prow", "far", "near")]).astype(jnp.int32)
-    parents = all_to_all(parent_strips(child_map, parent_front, plan))
-    maps = parents[:, len(plan.full), 0, : plan.slots].astype(jnp.int32)
-    strips = all_to_all(update_strips(child_blocks, child_coupling[0], child_inverse[0], plan))
-    head, column, rest = merge(place, maps, strips, parents, plan)
+    strips = all_to_all(
+        update_strips(place, child_blocks, child_map, child_coupling[0], child_inverse[0], parent_front, plan)
+    )
+    maps = strips[:, -1, 0, : plan.slots].astype(jnp.int32)
+    head, column = merge(place, maps, strips, plan, False)
     head = head + across(head, plan)
     heads = all_to_all(jnp.broadcast_to(head, (plan.members,) + head.shape))
-    l, x = cholesky(heads, parent_front.shape[0], plan)
-    columns = all_to_all(column_strips(place, column, across(column, plan), plan))
-    rests = all_to_all(rest_strips(place, rest, across(rest, plan), plan))
-    return finish(place, columns, rests, parent_front, l, x, plan)
+    (rest,) = merge(place, maps, strips, plan, True, (heads,))
+    sent = column_strips(place, column, across(column, plan), plan)
+    columns = all_to_all(sent)
+    l, x = cholesky(heads, parent_front.shape[0], plan, sent)
+    base = panel(place, columns, parent_front, l, x, plan)
+    rests = all_to_all(rest_strips(place, rest, across(rest, plan), plan, l))
+    return finish(place, rests, base, plan)
 
 
 def solution(mesh):

time: 183 us -> 149 us (0.81)
  the two profiles are of different devices: /device:TPU:12 before, /device:TPU:0 now
where the time goes in v3:
time: 149 us
  Pallas kernels  47.1 us (32%)
  blocking collectives  43.6 us (29%)
  waiting for transfers between devices  27.4 us (18%)
  starting transfers between devices  20.7 us (14%)
  local copies, waits for them, and re-layouts  9.11 us (6%)
    all_to_all x1, blocking collectives, all_to_all(): return lax.all_to_all(x, GROUP, 0, 0, tiled=True)  43.6 us
    pallas_call x1, Pallas kernels, cholesky(): pl.pallas_call(functools.partial(cholesky_kernel, plan=plan), in_specs=[V...  31 us
    ppermute x3, waiting for transfers between devices, across(): lax.ppermute(x, 'far', [(f, (f + by) % plan.far) for f in range(plan.far)])  19.1 us
    all_to_all x3, starting transfers between devices, all_to_all(): return lax.all_to_all(x, GROUP, 0, 0, tiled=True)  13.6 us
    all_to_all x3, waiting for transfers between devices, all_to_all(): return lax.all_to_all(x, GROUP, 0, 0, tiled=True)  8.22 us
    unnamed x24, local copies, waits for them, and re-layouts  8.22 us
    ppermute x3, starting transfers between devices, across(): lax.ppermute(x, 'far', [(f, (f + by) % plan.far) for f in range(plan.far)])  7.05 us
    pallas_call x2, Pallas kernels, merge(): pl.pallas_call(functools.partial(merge_kernel, plan=plan, rest=rest), in_...  5.12 us
  transfers between devices with their start and end apart: 6, of which 3 were waited for; matrix products, arithmetic and copies ran while one was open for 0% of the time, Pallas kernels for 25%

profile of v3, /device:TPU:0, one launch (start us, length us, event | category | flops | bytes accessed | tf_op | source)
XLA Modules:
  0.0 148.7 jit_solution(5452496593629695323)
XLA Ops:
  0.7 0.1 pad_add_fusion.place
  0.7 0.0 copy-start.2
  0.7 1.2 copy-done.2
  2.0 0.0 copy-start.4
  2.0 1.6 %copy-done.4 = f32[1,1024,512]{2,1,0:T(8,128)S(1)} copy-done((f32[1,1024,512]{2,1,0:T(8,128)S(1)}, f32[1,1024,512]{2,1,0:T(8,128)}, u32[]{:S(2)}) %copy-start.4) | copy-done | bytes 2097176
  3.5 0.0 copy-start.7
  3.5 1.2 copy-done.7
  4.8 0.0 copy-start.11
  4.8 0.7 copy-done.11
  5.4 4.5 %shard_map.82 = f32[8,47,16,128]{3,2,1,0:T(8,128)S(1)} custom-call(s32[3]{0:T(128)S(1)} %pad_add_fusion.place, s32[1]{0:T(128)S(6)} %copy.9.blocks, s32[1,8]{1,0:T(1,128)S(1)} %copy-done.11, f32[1024,512]{1,0:T(8,128)S(1)} %bitcast.6, f32[512,512]{1,0:T(8,128)S(1)} %bitcast.7, f32[512,512]{1,0:T(8,128)S(1)} %copy-done.2), custom_call_target="tpu_custom_call" | custom-call | tf_op jit(solution)/shard_map/pallas_call | solution.py:135
  9.9 0.0 copy-start.9
  9.9 43.6 %all_to_all.20.strips = f32[8,47,16,128]{3,2,1,0:T(8,128)S(1)} all-to-all(f32[8,47,16,128]{3,2,1,0:T(8,128)S(1)} %shard_map.82), channel_id=1, replica_groups=mesh['leaf'=2,'prow'=4,'far'=2,'near'=2] {'prow','near'}, dimensions={0} | all-to-all | bytes 6160384 | tf_op jit(solution)/shard_map/all_to_all | solution.py:430
  53.5 0.0 copy-done.9
  53.5 2.6 %shard_map.83 = (f32[10,16,128]{2,1,0:T(8,128)S(1)}, f32[48,16,128]{2,1,0:T(8,128)S(1)}) custom-call(s32[3]{0:T(128)S(1)} %pad_add_fusion.place, s32[8,8]{1,0:T(8,128)S(1)} %bitcast.8, s32[17,17]{1,0:T(8,128)S(1)} %copy-done.9, f32[8,47,16,128]{3,2,1,0:T(8,128)S(1)} %all_to_all.20.strips), custom_call_target="tpu_custom_call" | custom-call | tf_op jit(solution)/shard_map/pallas_call | solution.py:195
  56.2 2.7 %collective-permute-start = (f32[10,16,128]{2,1,0:T(8,128)S(1)}, f32[10,16,128]{2,1,0:T(8,128)S(1)}, u32[]{:S(2)}, u32[]{:S(2)}) collective-permute-start(f32[10,16,128]{2,1,0:T(8,128)S(1)} %get-tuple-element.9), channel_id=1, source_target_pairs={{0,2},{2,0},{1,3},{3,1},{4,6},{6,4},{5,7},{7,5},{8,10},{10,8},{9,1... | collective-permute-start | bytes 245768 | tf_op jit(solution)/shard_map/ppermute | solution.py:435
  58.9 3.3 %collective-permute-done = f32[10,16,128]{2,1,0:T(8,128)S(1)} collective-permute-done((f32[10,16,128]{2,1,0:T(8,128)S(1)}, f32[10,16,128]{2,1,0:T(8,128)S(1)}, u32[]{:S(2)}, u32[]{:S(2)}) %collective-permute-start) | collective-permute-done | bytes 81952 | tf_op jit(solution)/shard_map/ppermute | solution.py:435
  62.2 0.9 broadcast_in_dim.3
  63.1 4.2 %all-to-all-start.1 = ((f32[8,10,16,128]{3,2,1,0:T(8,128)}), f32[8,10,16,128]{3,2,1,0:T(8,128)}, u32[]{:S(2)}, u32[]{:S(2)}) async-start(f32[8,10,16,128]{3,2,1,0:T(8,128)} %broadcast_in_dim.3), calls=%async_computation.1 | async-start | bytes 1310720 | tf_op jit(solution)/shard_map/all_to_all | solution.py:430
  67.3 0.0 copy-start.8
  67.3 2.1 %collective-permute-start.2 = (f32[48,16,128]{2,1,0:T(8,128)S(1)}, f32[48,16,128]{2,1,0:T(8,128)S(1)}, u32[]{:S(2)}, u32[]{:S(2)}) collective-permute-start(f32[48,16,128]{2,1,0:T(8,128)S(1)} %get-tuple-element.10.mine), channel_id=1, source_target_pairs={{0,2},{2,0},{1,3},{3,1},{4,6},{6,4},{5,7},{7,5},{8,10},{10,8},{9,1... | collective-permute-start | bytes 1179656 | tf_op jit(solution)/shard_map/ppermute | solution.py:435
  69.4 15.9 %collective-permute-done.2.other = f32[48,16,128]{2,1,0:T(8,128)S(1)} collective-permute-done((f32[48,16,128]{2,1,0:T(8,128)S(1)}, f32[48,16,128]{2,1,0:T(8,128)S(1)}, u32[]{:S(2)}, u32[]{:S(2)}) %collective-permute-start.2) | collective-permute-done | bytes 393248 | tf_op jit(solution)/shard_map/ppermute | solution.py:435
  85.3 0.7 shard_map.85.after
  86.0 0.0 copy-start
  86.0 1.3 copy-done
  87.3 0.0 all-to-all-done.1.refs_0_.lower
  87.3 4.3 %all-to-all-start.3 = ((f32[8,32,16,128]{3,2,1,0:T(8,128)}), f32[8,32,16,128]{3,2,1,0:T(8,128)}, u32[]{:S(2)}, u32[]{:S(2)}) async-start(f32[8,32,16,128]{3,2,1,0:T(8,128)} %copy-done), calls=%async_computation.3 | async-start | bytes 4194304 | tf_op jit(solution)/shard_map/all_to_all | solution.py:430
  91.6 0.0 copy-done.8
  91.7 0.0 copy-start.1
  91.7 0.0 copy-start.10
  91.7 2.5 %shard_map.84.mine = f32[78,16,128]{2,1,0:T(8,128)S(1)} custom-call(s32[3]{0:T(128)S(1)} %pad_add_fusion.place, s32[8,8]{1,0:T(8,128)S(1)} %bitcast.9, s32[17,17]{1,0:T(8,128)S(1)} %copy-done.8, f32[8,47,16,128]{3,2,1,0:T(8,128)S(1)} %all_to_all.20.strips, f32[8,10,16,128]{3,2,1,0:T(8,128)} %all-to-all-done.1.refs_0_.lower), custom_call_target="tpu_custom_call" | custom-call | tf_op jit(solution)/shard_map/pallas_call | solution.py:195
  94.1 2.2 %collective-permute-start.1 = (f32[78,16,128]{2,1,0:T(8,128)S(1)}, f32[78,16,128]{2,1,0:T(8,128)S(1)}, u32[]{:S(2)}, u32[]{:S(2)}) collective-permute-start(f32[78,16,128]{2,1,0:T(8,128)S(1)} %shard_map.84.mine), channel_id=1, source_target_pairs={{0,2},{2,0},{1,3},{3,1},{4,6},{6,4},{5,7},{7,5},{8,10},{10,8},{9,1... | collective-permute-start | bytes 1916936 | tf_op jit(solution)/shard_map/ppermute | solution.py:435
  96.3 0.0 copy-done.1
  96.4 31.0 %shard_map.86 = (f32[512,512]{1,0:T(8,128)S(1)}, f32[512,512]{1,0:T(8,128)S(1)}) custom-call(f32[8,10,16,128]{3,2,1,0:T(8,128)} %all-to-all-done.1.refs_0_.lower, f32[8,32,16,128]{3,2,1,0:T(8,128)S(1)} %copy-done.1), custom_call_target="tpu_custom_call" | custom-call | tf_op jit(solution)/shard_map/pallas_call | solution.py:325
  127.3 0.0 copy-start.5
  127.3 1.0 copy-done.5
  128.3 0.0 copy-start.3
  128.3 0.0 collective-permute-done.1.other
  128.3 0.0 copy-done.10
  128.3 1.7 %shard_map.87 = f32[8,16,16,128]{3,2,1,0:T(8,128)} custom-call(s32[3]{0:T(128)S(1)} %pad_add_fusion.place, s32[4,4]{1,0:T(4,128)S(1)} %copy-done.10, f32[78,16,128]{2,1,0:T(8,128)S(1)} %shard_map.84.mine, f32[78,16,128]{2,1,0:T(8,128)S(1)} %collective-permute-done.1.other, f32[512,512]{1,0:T(8,128)S(1)} %get-tuple-element.11.after.l_ref), custom_call_target="tpu_custom_call" | custom-call | tf_op jit(solution)/shard_map/pallas_call | solution.py:238
  130.0 0.0 all-to-all-done.3.columns
  130.0 5.1 %all-to-all-start.2 = ((f32[8,16,16,128]{3,2,1,0:T(8,128)}), f32[8,16,16,128]{3,2,1,0:T(8,128)}, u32[]{:S(2)}, u32[]{:S(2)}) async-start(f32[8,16,16,128]{3,2,1,0:T(8,128)} %shard_map.87), calls=%async_computation.2 | async-start | bytes 2097152 | tf_op jit(solution)/shard_map/all_to_all | solution.py:430
  135.1 0.0 copy-done.3
  135.1 0.0 copy-start.6
  135.1 1.2 copy-done.6
  136.3 1.9 %shard_map.88.base = f32[512,512]{1,0:T(8,128)S(1)} custom-call(s32[3]{0:T(128)S(1)} %pad_add_fusion.place, f32[8,32,16,128]{3,2,1,0:T(8,128)} %all-to-all-done.3.columns, f32[512,512]{1,0:T(8,128)S(1)} %copy-done.3, f32[512,512]{1,0:T(8,128)S(1)} %get-tuple-element.11.after.l_ref, f32[512,512]{1,0:T(8,128)S(1)} %copy-done.6), custom_call_target="tpu_custom_call" | custom-call | tf_op jit(solution)/shard_map/pallas_call | solution.py:378
  138.2 8.2 %all-to-all-done.2.rests = f32[8,16,16,128]{3,2,1,0:T(8,128)} async-done(((f32[8,16,16,128]{3,2,1,0:T(8,128)}), f32[8,16,16,128]{3,2,1,0:T(8,128)}, u32[]{:S(2)}, u32[]{:S(2)}) %all-to-all-start.2) | async-done | bytes 1048608 | tf_op jit(solution)/shard_map/all_to_all | solution.py:430
  146.4 2.3 %shard_map.89 = f32[512,512]{1,0:T(8,128)} custom-call(s32[3]{0:T(128)S(1)} %pad_add_fusion.place, f32[8,16,16,128]{3,2,1,0:T(8,128)} %all-to-all-done.2.rests, f32[512,512]{1,0:T(8,128)S(1)} %shard_map.88.base), custom_call_target="tpu_custom_call" | custom-call | tf_op jit(solution)/shard_map/pallas_call | solution.py:419
  (2 shorter events, 0.0 us)
Async XLA Ops:
  0.7 1.2 copy-start.2
  2.0 1.6 %copy-start.4 = (f32[1,1024,512]{2,1,0:T(8,128)S(1)}, f32[1,1024,512]{2,1,0:T(8,128)}, u32[]{:S(2)}) copy-start(f32[1,1024,512]{2,1,0:T(8,128)} %param.9) | copy-start | bytes 6291460
  3.5 1.2 copy-start.7
  4.8 0.7 copy-start.11
  9.9 43.6 %copy-start.9 = (s32[17,17]{1,0:T(8,128)S(1)}, s32[17,17]{1,0:T(8,128)}, u32[]{:S(2)}) copy-start(s32[17,17]{1,0:T(8,128)} %constant.17.clone.table) | copy-start | bytes 3472
  56.2 6.0 %collective-permute-start = (f32[10,16,128]{2,1,0:T(8,128)S(1)}, f32[10,16,128]{2,1,0:T(8,128)S(1)}, u32[]{:S(2)}, u32[]{:S(2)}) collective-permute-start(f32[10,16,128]{2,1,0:T(8,128)S(1)} %get-tuple-element.9), channel_id=1, source_target_pairs={{0,2},{2,0},{1,3},{3,1},{4,6},{6,4},{5,7},{7,5},{8,10},{10,8},{9,1... | collective-permute-start | bytes 245768 | tf_op jit(solution)/shard_map/ppermute | solution.py:435
  63.1 24.2 %all-to-all-start.1 = ((f32[8,10,16,128]{3,2,1,0:T(8,128)}), f32[8,10,16,128]{3,2,1,0:T(8,128)}, u32[]{:S(2)}, u32[]{:S(2)}) async-start(f32[8,10,16,128]{3,2,1,0:T(8,128)} %broadcast_in_dim.3), calls=%async_computation.1 | async-start | bytes 1310720 | tf_op jit(solution)/shard_map/all_to_all | solution.py:430
  67.3 24.4 %copy-start.8 = (s32[17,17]{1,0:T(8,128)S(1)}, s32[17,17]{1,0:T(8,128)}, u32[]{:S(2)}) copy-start(s32[17,17]{1,0:T(8,128)} %constant.18.clone.table) | copy-start | bytes 3472
  67.3 18.0 %collective-permute-start.2 = (f32[48,16,128]{2,1,0:T(8,128)S(1)}, f32[48,16,128]{2,1,0:T(8,128)S(1)}, u32[]{:S(2)}, u32[]{:S(2)}) collective-permute-start(f32[48,16,128]{2,1,0:T(8,128)S(1)} %get-tuple-element.10.mine), channel_id=1, source_target_pairs={{0,2},{2,0},{1,3},{3,1},{4,6},{6,4},{5,7},{7,5},{8,10},{10,8},{9,1... | collective-permute-start | bytes 1179656 | tf_op jit(solution)/shard_map/ppermute | solution.py:435
  86.0 1.3 copy-start
  87.3 42.7 %all-to-all-start.3 = ((f32[8,32,16,128]{3,2,1,0:T(8,128)}), f32[8,32,16,128]{3,2,1,0:T(8,128)}, u32[]{:S(2)}, u32[]{:S(2)}) async-start(f32[8,32,16,128]{3,2,1,0:T(8,128)} %copy-done), calls=%async_computation.3 | async-start | bytes 4194304 | tf_op jit(solution)/shard_map/all_to_all | solution.py:430
  91.7 4.7 %copy-start.1 = (f32[8,32,16,128]{3,2,1,0:T(8,128)S(1)}, f32[8,32,16,128]{3,2,1,0:T(8,128)}, u32[]{:S(2)}) copy-start(f32[8,32,16,128]{3,2,1,0:T(8,128)} %copy-done) | copy-start | bytes 6291460
  91.7 36.6 %copy-start.10 = (s32[4,4]{1,0:T(4,128)S(1)}, s32[4,4]{1,0:T(4,128)}, u32[]{:S(2)}) copy-start(s32[4,4]{1,0:T(4,128)} %constant.19.clone.starts) | copy-start | bytes 196
  94.1 34.2 %collective-permute-start.1 = (f32[78,16,128]{2,1,0:T(8,128)S(1)}, f32[78,16,128]{2,1,0:T(8,128)S(1)}, u32[]{:S(2)}, u32[]{:S(2)}) collective-permute-start(f32[78,16,128]{2,1,0:T(8,128)S(1)} %shard_map.84.mine), channel_id=1, source_target_pairs={{0,2},{2,0},{1,3},{3,1},{4,6},{6,4},{5,7},{7,5},{8,10},{10,8},{9,1... | collective-permute-start | bytes 1916936 | tf_op jit(solution)/shard_map/ppermute | solution.py:435
  127.3 1.0 copy-start.5
  128.3 6.8 %copy-start.3 = (f32[512,512]{1,0:T(8,128)S(1)}, f32[512,512]{1,0:T(8,128)}, u32[]{:S(2)}) copy-start(f32[512,512]{1,0:T(8,128)} %parent.3) | copy-start | bytes 3145732
  130.0 16.4 %all-to-all-start.2 = ((f32[8,16,16,128]{3,2,1,0:T(8,128)}), f32[8,16,16,128]{3,2,1,0:T(8,128)}, u32[]{:S(2)}, u32[]{:S(2)}) async-start(f32[8,16,16,128]{3,2,1,0:T(8,128)} %shard_map.87), calls=%async_computation.2 | async-start | bytes 2097152 | tf_op jit(solution)/shard_map/all_to_all | solution.py:430
  135.1 1.2 copy-start.6

commit v4 on v3

v4 whole, which is shorter than its diff:
```python
import functools

import jax
import jax.numpy as jnp
import numpy as np
from jax import lax
from jax.experimental import pallas as pl
from jax.experimental.pallas import tpu as pltpu
from jax.sharding import Mesh
from jax.sharding import PartitionSpec as P

F32 = jnp.float32
BF16 = jnp.bfloat16
SMEM = pl.BlockSpec(memory_space=pltpu.SMEM)
VMEM = pl.BlockSpec(memory_space=pltpu.VMEM)
HBM = pl.BlockSpec(memory_space=pltpu.HBM)
AFTER = pl.BlockSpec(memory_space=pl.ANY)
GROUP = ("prow", "near")


def in_hbm(x):
    return pltpu.with_memory_space_constraint(x, pltpu.HBM)


def in_vmem(x):
    return pltpu.with_memory_space_constraint(x, pltpu.VMEM)


TOKEN = jax.ShapeDtypeStruct((8, 128), F32)


def call(kernel, megabytes, **kwargs):
    return pl.pallas_call(
        kernel,
        compiler_params=pltpu.CompilerParams(vmem_limit_bytes=megabytes * 2**20),
        cost_estimate=pl.CostEstimate(flops=1, bytes_accessed=1, transcendentals=0),
        **kwargs,
    )


class Plan:
    def __init__(self, rows, near, far, per_tile, slots, blk):
        self.rows, self.near, self.far = rows, near, far
        self.per_tile, self.slots, self.blk = per_tile, slots, blk
        self.members = rows * near
        self.strip = blk // self.members
        nb = per_tile
        self.lower = [(a, b) for b in range(nb) for a in range(b, nb)]
        self.full = [(a, b) for a in range(nb) for b in range(nb)]
        self.pairs = [(h, l) for h in range(1, rows) for l in range(1, h)]
        self.n_head = len(self.lower)
        self.n_column = (rows - 1) * nb * nb
        tiles = [(r, r) for r in range(1, rows)] + self.pairs
        need = {t: sorted({c // near for c in t}) for t in tiles}
        tiles.sort(key=lambda t: need[t])
        size = {t: len(self.lower) if t[0] == t[1] else nb * nb for t in tiles}
        self.starts = {t: sum(size[u] for u in tiles[:k]) for k, t in enumerate(tiles)}
        self.n_rest = sum(size.values())
        spans = []
        for f in range(far):
            held = [t for t in tiles if f in need[t]]
            spans.append((min(self.starts[t] for t in held), max(self.starts[t] + size[t] for t in held)))
        self.window = max(end - begin for begin, end in spans)
        self.begins = [min(begin, self.n_rest - self.window) for begin, _ in spans]
        self.total = self.n_head + self.n_column + self.n_rest
        self.first = len(self.full) // 2
        self.n_parent = max(len(self.lower), len(self.full) - self.first)
        self.slot_pairs = [(i, j) for j in range(slots) for i in range(j, slots)]
        self.early = sum(j < nb for _, j in self.slot_pairs)
        table = np.full((rows * nb + 1, rows * nb + 1), self.total, np.int32)
        rest = self.n_head + self.n_column
        for r in range(rows):
            for e, (a, b) in enumerate(self.lower):
                at = e if r == 0 else rest + self.rest_at(r, r) + e
                table[r * nb + a + 1, r * nb + b + 1] = at
        for h in range(1, rows):
            for l in range(h):
                for e, (a, b) in enumerate(self.full):
                    at = self.n_head + (h - 1) * nb * nb + e if l == 0 else rest + self.rest_at(h, l) + e
                    table[h * nb + a + 1, l * nb + b + 1] = at
        self.table = table

    def rest_at(self, r, c):
        if r == 0 or c == 0:
            return 0
        return self.starts[max(r, c), min(r, c)]


def split(x):
    high = x.astype(BF16)
    return high, (x - high.astype(F32)).astype(BF16)


def dot3(a, b):
    dims = (((1,), (1,)), ((), ()))
    dot = lambda u, v: lax.dot_general(u, v, dims, preferred_element_type=F32)
    return dot(a[0], b[0]) + (dot(a[0], b[1]) + dot(a[1], b[0]))


def dot_nt(a, b):
    return lax.dot_general(
        a, b, (((1,), (1,)), ((), ())), precision=lax.Precision.HIGHEST, preferred_element_type=F32
    )


def dot_nn(a, b):
    return lax.dot_general(
        a, b, (((1,), (0,)), ((), ())), precision=lax.Precision.HIGHEST, preferred_element_type=F32
    )


def update_kernel(
    place, blocks, mapping, coupling, inverse, parent, early, late, left, right, own, high, low, update, sems, *, plan
):
    blk, size = plan.blk, plan.strip
    order = coupling.shape[0]
    width = order // 2
    starts = [0, width]
    copies = [pltpu.make_async_copy(inverse, right, sems.at[0])]
    for k, start in enumerate(starts):
        window = pl.ds(start, width)
        copies.append(pltpu.make_async_copy(coupling.at[window], left.at[window], sems.at[k + 1]))
    copies.append(pltpu.make_async_copy(parent, own, sems.at[len(starts) + 1]))
    for copy in copies:
        copy.start()
    base = plan.early
    lanes = lax.broadcasted_iota(jnp.int32, (size, blk), 1)
    coded = jnp.zeros((size, blk), F32)
    for s in range(plan.slots):
        coded = jnp.where(lanes == s, mapping[0, s].astype(F32), coded)
    for d in range(plan.members):
        early[d, base + plan.n_parent] = coded
    copies[0].wait()
    factor_of = split(right[...])
    for k, start in enumerate(starts):
        window = slice(start, start + width)
        copies[k + 1].wait()
        rows = start + lax.broadcasted_iota(jnp.int32, (width, 1), 0)
        masked = jnp.where(rows < blocks[0] * blk, left[window, :], 0.0)
        high[window, :], low[window, :] = split(dot3(split(masked), factor_of))
    panel = 2 * blk
    for start in range(0, order, panel):
        cols = slice(start, start + panel)
        update[start:, cols] = dot3((high[start:, :], low[start:, :]), (high[cols, :], low[cols, :]))
    for e, (i, j) in enumerate(plan.slot_pairs):
        for d in range(plan.members):
            top = i * blk + d * size
            strip = update[top : top + size, j * blk : (j + 1) * blk]
            if e < plan.early:
                early[d, e] = strip
            else:
                late[d, e - plan.early] = strip

    copies[-1].wait()
    row, col = place[0], place[1] * plan.near + place[2]

    def send(blocks, transposed):
        for e, (a, b) in enumerate(blocks):
            p, q = (b, a) if transposed else (a, b)
            block = own[p * blk : (p + 1) * blk, q * blk : (q + 1) * blk]
            block = block.T if transposed else block
            for d in range(plan.members):
                early[d, base + e] = block[d * size : (d + 1) * size]

    @pl.when((row == 0) & (col == 0))
    def _():
        send(plan.lower, False)

    @pl.when((row > 0) & (col == 0))
    def _():
        send(plan.full[: plan.first], False)

    @pl.when((row == 0) & (col > 0))
    def _():
        send(plan.full[plan.first :], True)


def update_strips(place, blocks, mapping, coupling, inverse, parent, plan):
    order, pivots = coupling.shape
    counts = (plan.early + plan.n_parent + 1, len(plan.slot_pairs) - plan.early)
    return call(
        functools.partial(update_kernel, plan=plan),
        24,
        in_specs=[SMEM] * 3 + [HBM] * 3,
        out_specs=[VMEM] * 2,
        out_shape=[jax.ShapeDtypeStruct((plan.members, n, plan.strip, plan.blk), F32) for n in counts],
        scratch_shapes=[
            pltpu.VMEM(coupling.shape, F32),
            pltpu.VMEM(inverse.shape, F32),
            pltpu.VMEM(parent.shape, F32),
            pltpu.VMEM((order, pivots), BF16),
            pltpu.VMEM((order, pivots), BF16),
            pltpu.VMEM((order, order), F32),
            pltpu.SemaphoreType.DMA((4,)),
        ],
    )(place, blocks, mapping, *(in_hbm(v) for v in (coupling, inverse, parent)))


def merge_head_kernel(place, maps, table, early, head, token, total, *, plan):
    token[...] = jnp.zeros_like(token)
    base = plan.early

    @pl.when(place[1] == 0)
    def _():
        for e in range(plan.n_head):
            total[e] = early[0, base + e]

    @pl.when(place[1] != 0)
    def _():
        total[...] = jnp.zeros_like(total)

    def one(source, _):
        ids = [maps[source, s] + 1 for s in range(plan.per_tile)]
        for e, (i, j) in enumerate(plan.slot_pairs[: plan.early]):
            if i < plan.per_tile:
                total[table[ids[i], ids[j]]] -= early[source, e]
        return 0

    lax.fori_loop(0, plan.members, one, 0)
    head[...] = total[: plan.n_head]


def merge_head(place, maps, early, plan):
    tail = (plan.strip, plan.blk)
    table = np.minimum(plan.table, plan.n_head).astype(np.int32)
    return call(
        functools.partial(merge_head_kernel, plan=plan),
        6,
        in_specs=[SMEM] * 3 + [VMEM],
        out_specs=[VMEM] * 2,
        out_shape=[jax.ShapeDtypeStruct((plan.n_head,) + tail, F32), TOKEN],
        scratch_shapes=[pltpu.VMEM((plan.n_head + 1,) + tail, F32)],
    )(place, maps, jnp.asarray(table), early)


def merge_column_kernel(place, maps, table, early, after, column, total, *, plan):
    nb2 = len(plan.full)
    total[...] = jnp.zeros_like(total)
    base = plan.early

    @pl.when(place[1] == 0)
    def _():
        for r in range(1, plan.rows):
            for e in range(plan.first):
                total[(r - 1) * nb2 + e] = early[r * plan.near, base + e]

    for c in range(1, plan.rows):

        @pl.when(place[1] == c // plan.near)
        def _():
            for e in range(plan.first, nb2):
                total[(c - 1) * nb2 + e] = early[c % plan.near, base + e - plan.first]

    def one(source, _):
        ids = [maps[source, s] + 1 for s in range(plan.slots)]
        for e, (i, j) in enumerate(plan.slot_pairs[: plan.early]):
            if i > 0:
                total[table[ids[i], ids[j]]] -= early[source, e]
        return 0

    lax.fori_loop(0, plan.members, one, 0)
    column[...] = total[: plan.n_column]


def merge_column(place, maps, early, plan, after):
    tail = (plan.strip, plan.blk)
    first, last = plan.n_head, plan.n_head + plan.n_column
    inside = (plan.table >= first) & (plan.table < last)
    table = np.where(inside, plan.table - first, plan.n_column).astype(np.int32)
    return call(
        functools.partial(merge_column_kernel, plan=plan),
        8,
        in_specs=[SMEM] * 3 + [VMEM] + [AFTER],
        out_specs=VMEM,
        out_shape=jax.ShapeDtypeStruct((plan.n_column,) + tail, F32),
        scratch_shapes=[pltpu.VMEM((plan.n_column + 1,) + tail, F32)],
    )(place, maps, jnp.asarray(table), early, after)


def merge_rest_kernel(place, maps, table, begins, early, late, after, keep, send, token, total, *, plan):
    token[...] = jnp.zeros_like(token)
    total[...] = jnp.zeros_like(total)

    def one(source, _):
        ids = [maps[source, s] + 1 for s in range(plan.slots)]
        for e, (i, j) in enumerate(plan.slot_pairs):
            strip = early[source, e] if e < plan.early else late[source, e - plan.early]
            total[table[ids[i], ids[j]]] -= strip
        return 0

    lax.fori_loop(0, plan.members, one, 0)
    keep[...] = total[pl.ds(begins[place[1]], plan.window)]
    send[...] = total[pl.ds(begins[(place[1] + 1) % plan.far], plan.window)]


def merge_rest(place, maps, early, late, plan, after):
    first = plan.n_head + plan.n_column
    table = np.where(plan.table >= first, plan.table - first, plan.n_rest).astype(np.int32)
    shape = jax.ShapeDtypeStruct((plan.window, plan.strip, plan.blk), F32)
    return call(
        functools.partial(merge_rest_kernel, plan=plan),
        8,
        in_specs=[SMEM] * 4 + [VMEM] * 2 + [AFTER],
        out_specs=[VMEM] * 3,
        out_shape=[shape, shape, TOKEN],
        scratch_shapes=[pltpu.VMEM((plan.n_rest + 1, plan.strip, plan.blk), F32)],
    )(place, maps, jnp.asarray(table), jnp.asarray(np.array(plan.begins, np.int32)), early, late, after)


def column_kernel(place, mine, other, *refs, plan):
    sent, token, total, out, sems = refs[-5:]
    token[...] = jnp.zeros_like(token)
    nb2 = len(plan.full)
    total[...] = mine[...] + other[...]
    for r in range(plan.rows):
        for n in range(plan.near):
            d = r * plan.near + n
            out[d, :nb2] = total[max(r - 1, 0) * nb2 : max(r - 1, 0) * nb2 + nb2]
            col = jnp.maximum(place[1] * plan.near + n - 1, 0)
            out[d, nb2:] = total[pl.ds(col * nb2, nb2)]
            pltpu.make_async_copy(out.at[d], sent.at[d], sems.at[d]).start()
    for d in range(plan.members):
        pltpu.make_async_copy(out.at[d], sent.at[d], sems.at[d]).wait()


def column_strips(place, mine, other, plan, after):
    shape = (plan.members, 2 * len(plan.full)) + mine.shape[1:]
    return call(
        functools.partial(column_kernel, plan=plan),
        12,
        in_specs=[SMEM] + [VMEM] * 2 + [AFTER] * len(after),
        out_specs=[HBM, VMEM],
        out_shape=[pltpu.HBM(shape, F32), TOKEN],
        scratch_shapes=[
            pltpu.VMEM(mine.shape, F32),
            pltpu.VMEM(shape, F32),
            pltpu.SemaphoreType.DMA((plan.members,)),
        ],
    )(place, mine, other, *after)


def rest_kernel(place, starts, mine, other, after, out, token, total, *, plan):
    token[...] = jnp.zeros_like(token)
    nb2 = len(plan.full)
    total[...] = mine[...] + other[...]
    for r in range(plan.rows):
        for n in range(plan.near):
            out[r * plan.near + n] = total[pl.ds(starts[place[1] * plan.near + n, r], nb2)]


def rest_strips(place, mine, other, plan, after):
    cols = plan.near * plan.far
    nb2 = len(plan.full)
    starts = np.zeros((cols, plan.rows), np.int32)
    for c in range(1, cols):
        for r in range(1, plan.rows):
            starts[c, r] = min(plan.rest_at(r, c) - plan.begins[c // plan.near], plan.window - nb2)
    return call(
        functools.partial(rest_kernel, plan=plan),
        6,
        in_specs=[SMEM] * 2 + [VMEM] * 2 + [AFTER],
        out_specs=[VMEM] * 2,
        out_shape=[jax.ShapeDtypeStruct((plan.members, len(plan.full)) + mine.shape[1:], F32), TOKEN],
        scratch_shapes=[pltpu.VMEM(mine.shape, F32)],
    )(place, jnp.asarray(starts), mine, other, after)


def factor_block(a):
    step = 8
    count = a.shape[0] // step
    sub = lax.broadcasted_iota(jnp.int32, (step, a.shape[1]), 0)
    out = []
    for t in range(count):
        top = a[:step]
        row = lambda v, q: jnp.broadcast_to(v[q : q + 1], v.shape)
        col = lambda v, q: jnp.broadcast_to(v[:, step * t + q : step * t + q + 1], v.shape)
        cols = [col(top, q) for q in range(step)]
        pivot = {(p, q): row(cols[q], p) for q in range(step) for p in range(q, step)}
        scale, low = [], {}
        for q in range(step):
            scale.append(lax.rsqrt(pivot[q, q]))
            for p in range(q + 1, step):
                low[p, q] = pivot[p, q] * scale[q]
            for p in range(q + 1, step):
                for m in range(q + 1, p + 1):
                    pivot[p, m] = pivot[p, m] - low[p, q] * low[m, q]
        rows = [row(top, q) for q in range(step)]
        u = []
        for q in range(step):
            u.append(rows[q] * scale[q])
            for p in range(q + 1, step):
                rows[p] = rows[p] - low[p, q] * u[q]
        done = u[0]
        for q in range(1, step):
            done = jnp.where(sub == q, u[q], done)
        out.append(done)
        if t == count - 1:
            break
        for q in reversed(range(step)):
            u[q] = u[q] * scale[q]
            for p in range(q):
                u[p] = u[p] - low[q, p] * u[q]
        a = a[step:]
        cols = [col(a, q) for q in range(step)]
        for q in range(step):
            a = a - cols[q] * jnp.broadcast_to(u[q][:1], a.shape)
    return jnp.concatenate(out, 0)


def cholesky_kernel(place, *refs, plan):
    heads, (l_ref, x_ref, token, s) = refs[: plan.rows], refs[-4:]
    token[...] = jnp.zeros_like(token)
    n = l_ref.shape[0]
    blk, nb = plan.blk, plan.blk // 2
    l_ref[...] = jnp.zeros_like(l_ref)
    x_ref[...] = jnp.zeros_like(x_ref)
    for k, ref in enumerate(heads):
        for m in range(plan.near):
            member = (place[0] ^ k) * plan.near + (place[2] ^ m)
            for e, (i, j) in enumerate(plan.lower):
                top = pl.multiple_of(i * blk + member * plan.strip, plan.strip)
                s[pl.ds(top, plan.strip), j * blk : (j + 1) * blk] = ref[m, e]
    for i, j in plan.lower:
        if i > j:
            s[j * blk : (j + 1) * blk, i * blk : (i + 1) * blk] = s[i * blk : (i + 1) * blk, j * blk : (j + 1) * blk].T
    r, c = (lax.broadcasted_iota(jnp.int32, (nb, nb), d) for d in range(2))
    for off in range(0, n, nb):
        end = off + nb
        both = factor_block(jnp.concatenate([s[off:end, off:end], (r == c).astype(F32)], 1))
        w = both[:, nb:]
        l_ref[off:end, off:end] = jnp.where(r >= c, both[:, :nb].T, 0.0)
        x_ref[off:end, off:end] = w
        if off:
            x_ref[off:end, :off] = dot_nn(w, x_ref[off:end, :off])
        if end < n:
            below = dot_nt(s[end:, off:end], w)
            s[end:, end:] -= dot_nt(below, below)
            l_ref[end:, off:end] = below
            x_ref[end:, :end] -= dot_nn(below, x_ref[off:end, :end])


def cholesky(place, heads, n, plan, after):
    square = jax.ShapeDtypeStruct((n, n), F32)
    return call(
        functools.partial(cholesky_kernel, plan=plan),
        12,
        in_specs=[SMEM] + [VMEM] * plan.rows + [AFTER],
        out_specs=[VMEM] * 3,
        out_shape=[square, square, TOKEN],
        scratch_shapes=[pltpu.VMEM((n, n), F32)],
    )(place, *heads, after)


def put(ref, source, first, blocks, plan):
    blk, size = plan.blk, plan.strip
    for e, (a, b) in enumerate(blocks):
        for d in range(plan.members):
            top = a * blk + d * size
            ref[top : top + size, b * blk : (b + 1) * blk] = source[d, first + e]


def panel_kernel(place, columns, parent, l_ref, x_ref, after, out, a_row, a_col, *, plan):
    nb2 = len(plan.full)
    row = place[0]
    col = place[1] * plan.near + place[2]

    @pl.when((row == 0) & (col == 0))
    def _():
        out[...] = l_ref[...]

    @pl.when((row == 0) & (col > 0))
    def _():
        put(a_col, columns, nb2, plan.full, plan)
        out[...] = a_col[...].T

    @pl.when(row > 0)
    def _():
        put(a_row, columns, 0, plan.full, plan)
        a_row[...] = dot_nt(a_row[...], x_ref[...])

    @pl.when((row > 0) & (col == 0))
    def _():
        out[...] = a_row[...]

    @pl.when((row > 0) & (col == row))
    def _():
        pair = split(a_row[...])
        out[...] = parent[...] - dot3(pair, pair)

    @pl.when((row > 0) & (col > 0) & (col != row))
    def _():
        put(a_col, columns, nb2, plan.full, plan)
        out[...] = parent[...] - dot3(split(a_row[...]), split(dot_nt(a_col[...], x_ref[...])))


def panel(place, columns, parent, l, x, plan, after):
    return call(
        functools.partial(panel_kernel, plan=plan),
        12,
        in_specs=[SMEM] + [VMEM] * 4 + [AFTER],
        out_specs=VMEM,
        out_shape=jax.ShapeDtypeStruct(parent.shape, F32),
        scratch_shapes=[pltpu.VMEM(parent.shape, F32)] * 2,
    )(place, columns, parent, l, x, after)


def finish_kernel(place, rests_in, base_in, out, tile, rests, base, sems, *, plan):
    blk = plan.blk
    copies = [pltpu.make_async_copy(rests_in, rests, sems.at[0]), pltpu.make_async_copy(base_in, base, sems.at[1])]
    for copy in copies:
        copy.start()
    for copy in copies:
        copy.wait()
    row = place[0]
    col = place[1] * plan.near + place[2]

    @pl.when((row == 0) | (col == 0))
    def _():
        out[...] = base[...]

    @pl.when((row > 0) & (col == row))
    def _():
        put(tile, rests, 0, plan.lower, plan)
        for a, b in plan.lower:
            if a > b:
                tile[b * blk : (b + 1) * blk, a * blk : (a + 1) * blk] = tile[
                    a * blk : (a + 1) * blk, b * blk : (b + 1) * blk
                ].T
        out[...] = base[...] + tile[...]

    @pl.when((row > col) & (col > 0))
    def _():
        put(tile, rests, 0, plan.full, plan)
        out[...] = base[...] + tile[...]

    @pl.when((row > 0) & (row < col))
    def _():
        put(tile, rests, 0, plan.full, plan)
        out[...] = base[...] + tile[...].T


def finish(place, rests, base, plan):
    return call(
        functools.partial(finish_kernel, plan=plan),
        10,
        in_specs=[SMEM] + [HBM] * 2,
        out_specs=VMEM,
        out_shape=jax.ShapeDtypeStruct(base.shape, F32),
        scratch_shapes=[
            pltpu.VMEM(base.shape, F32),
            pltpu.VMEM(rests.shape, F32),
            pltpu.VMEM(base.shape, F32),
            pltpu.SemaphoreType.DMA((2,)),
        ],
    )(place, in_hbm(rests), in_hbm(base))


def all_to_all(x):
    return lax.all_to_all(x, GROUP, 0, 0, tiled=True)


def across(x, plan):
    others = [
        lax.ppermute(x, "far", [(f, (f + by) % plan.far) for f in range(plan.far)]) for by in range(1, plan.far)
    ]
    return functools.reduce(jnp.add, others)


def spread_head(head, plan):
    cols = plan.near * plan.far
    got = [head] + [lax.ppermute(head, ("far", "near"), [(d, d ^ k) for d in range(cols)]) for k in range(1, cols)]
    pair = jnp.stack([sum(got[m + plan.near :: plan.near], got[m]) for m in range(plan.near)])
    return [pair] + [lax.ppermute(pair, "prow", [(d, d ^ k) for d in range(plan.rows)]) for k in range(1, plan.rows)]


def body(child_inverse, child_coupling, child_blocks, child_map, parent_front, plan):
    place = jnp.stack([lax.axis_index(a) for a in ("prow", "far", "near")]).astype(jnp.int32)
    early, late = update_strips(
        place, child_blocks, child_map, child_coupling[0], child_inverse[0], parent_front, plan
    )
    early = all_to_all(early)
    late = all_to_all(late)
    maps = early[:, -1, 0, : plan.slots].astype(jnp.int32)
    head, token = merge_head(place, maps, early, plan)
    heads = spread_head(head, plan)
    column = merge_column(place, maps, early, plan, token)
    far_column = across(column, plan)
    keep, send, token = merge_rest(place, maps, early, late, plan, heads[0])
    sent, token = column_strips(place, column, far_column, plan, [token] + heads[1:])
    columns = all_to_all(sent)
    l, x, token = cholesky(place, heads, parent_front.shape[0], plan, token)
    sent, token = rest_strips(place, keep, across(send, plan), plan, token)
    base = panel(place, columns, parent_front, l, x, plan, token)
    rests = all_to_all(sent)
    return finish(place, rests, base, plan)


def solution(mesh):
    rows, cols = mesh.shape["prow"], mesh.shape["pcol"]
    near = 2 if cols % 2 == 0 else 1
    fine = Mesh(
        mesh.devices.reshape(mesh.shape["leaf"], rows, cols // near, near), ("leaf", "prow", "far", "near")
    )
    device = P(("leaf", "prow", "far", "near"))

    def run(child_inverse, child_coupling, child_blocks, child_map, parent_front):
        slots = child_map.shape[1]
        blk = child_coupling.shape[1] // slots
        plan = Plan(rows, near, cols // near, parent_front.shape[1] // cols // blk, slots, blk)
        tile = P(("leaf", "prow"), ("far", "near"))
        return jax.shard_map(
            functools.partial(body, plan=plan),
            mesh=fine,
            in_specs=(device, device, device, device, tile),
            out_specs=tile,
            check_vma=False,
        )(child_inverse, child_coupling, child_blocks, child_map, parent_front)

    return run
```

time: 149 us -> 145 us (0.973)
  blocking collectives: 43.6 us -> 36.5 us
  starting transfers between devices: 20.7 us -> 25.8 us
  waiting for transfers between devices: 27.4 us -> 23.5 us
    ppermute x3 -> x2, waiting for transfers between devices: 19.1 us -> 5.72 us  [across(): lax.ppermute(x, 'far', [(f, (f + by) % plan.far) for f in range(plan.far)])]
    ppermute x0 -> x6, starting transfers between devices: none -> 8.02 us  [the longest x3 4.53 us: spread_head(): lax.ppermute(head, ('far', 'near'), [(d, d ^ k) for d in range(cols)])]
    all_to_all x1, blocking collectives: 43.6 us -> 36.5 us  [all_to_all(): return lax.all_to_all(x, GROUP, 0, 0, tiled=True)]
    ppermute x0 -> x6, waiting for transfers between devices: none -> 6.79 us  [the longest x3 5.89 us: spread_head(): lax.ppermute(head, ('far', 'near'), [(d, d ^ k) for d in range(cols)])]
    ppermute x3 -> x2, starting transfers between devices: 7.05 us -> 3.95 us  [across(): lax.ppermute(x, 'far', [(f, (f + by) % plan.far) for f in range(plan.far)])]
    all_to_all x3, waiting for transfers between devices: 8.22 us -> 11 us  [all_to_all(): return lax.all_to_all(x, GROUP, 0, 0, tiled=True)]
    unnamed x24 -> x32, local copies, waits for them, and re-layouts: 8.22 us -> 9.68 us
    pallas_call x8 -> x9, Pallas kernels: 47.1 us -> 47.1 us  [the longest x1 27.8 us: cholesky(): call(functools.partial(cholesky_kernel, plan=plan), 12, in_specs=[SMEM] +...]
  transfers between devices with their start and end apart: 6 -> 11, of which waited for: 3 -> 7; matrix products, arithmetic and copies ran while one was open for 0% -> 0% of each run, Pallas kernels for 25% -> 24%
where the time goes in v4:
time: 145 us; the launch traced here: 144 us
  Pallas kernels  47.1 us (32%)
  blocking collectives  36.5 us (25%)
  starting transfers between devices  25.8 us (18%)
  waiting for transfers between devices  23.5 us (16%)
  local copies, waits for them, and re-layouts  9.68 us (7%)
    all_to_all x1, blocking collectives, all_to_all(): return lax.all_to_all(x, GROUP, 0, 0, tiled=True)  36.5 us
    pallas_call x1, Pallas kernels, cholesky(): call(functools.partial(cholesky_kernel, plan=plan), 12, in_specs=[SMEM] +...  27.8 us
    all_to_all x3, starting transfers between devices, all_to_all(): return lax.all_to_all(x, GROUP, 0, 0, tiled=True)  13.9 us
    all_to_all x3, waiting for transfers between devices, all_to_all(): return lax.all_to_all(x, GROUP, 0, 0, tiled=True)  11 us
    unnamed x32, local copies, waits for them, and re-layouts  9.68 us
    pallas_call x1, Pallas kernels, update_strips(): call(functools.partial(update_kernel, plan=plan), 24, in_specs=[SMEM] * 3...  6.26 us
    ppermute x3, waiting for transfers between devices, spread_head(): lax.ppermute(head, ('far', 'near'), [(d, d ^ k) for d in range(cols)])  5.89 us
    ppermute x2, waiting for transfers between devices, across(): lax.ppermute(x, 'far', [(f, (f + by) % plan.far) for f in range(plan.far)])  5.72 us
  transfers between devices with their start and end apart: 11, of which 7 were waited for; matrix products, arithmetic and copies ran while one was open for 0% of the time, Pallas kernels for 24%

profile of v4, /device:TPU:0, one launch (start us, length us, event | category | flops | bytes accessed | tf_op | source)
XLA Modules:
  0.0 144.4 jit_solution(14435526170591774539)
XLA Ops:
  0.7 0.1 pad_add_fusion.place
  0.7 0.7 copy-done.14
  1.4 6.3 %shard_map.100 = (f32[8,37,16,128]{3,2,1,0:T(8,128)S(1)}, f32[8,10,16,128]{3,2,1,0:T(8,128)S(1)}) custom-call(s32[3]{0:T(128)S(1)} %pad_add_fusion.place, s32[1]{0:T(128)S(6)} %copy.11.blocks, s32[1,8]{1,0:T(1,128)S(1)} %copy-done.14, f32[1024,512]{1,0:T(8,128)} %bitcast.13, f32[512,512]{1,0:T(8,128)} %bitcast.14, f32[512,512]{1,0:T(8,128)} %parent.3), custom_call_target="tpu_custom_call" | custom-call | flops 1 | bytes 1 | tf_op jit(solution)/shard_map/pallas_call | solution.py:181
  7.7 0.0 copy-start.7
  7.7 0.0 copy-start.12
  7.7 36.5 %all_to_all.20.early = f32[8,37,16,128]{3,2,1,0:T(8,128)S(1)} all-to-all(f32[8,37,16,128]{3,2,1,0:T(8,128)S(1)} %get-tuple-element.19), channel_id=1, replica_groups=mesh['leaf'=2,'prow'=4,'far'=2,'near'=2] {'prow','near'}, dimensions={0} | all-to-all | bytes 4849664 | tf_op jit(solution)/shard_map/all_to_all | solution.py:559
  44.2 3.7 %all-to-all-start.1 = ((f32[8,10,16,128]{3,2,1,0:T(8,128)}), f32[8,10,16,128]{3,2,1,0:T(8,128)S(1)}, u32[]{:S(2)}, u32[]{:S(2)}) async-start(f32[8,10,16,128]{3,2,1,0:T(8,128)} %copy-done.7), calls=%async_computation.1 | async-start | bytes 1310720 | tf_op jit(solution)/shard_map/all_to_all | solution.py:559
  47.9 1.3 shard_map.101
  49.2 0.0 copy-start.10
  49.2 2.6 %collective-permute-start = (f32[10,16,128]{2,1,0:T(8,128)S(1)}, f32[10,16,128]{2,1,0:T(8,128)S(1)}, u32[]{:S(2)}, u32[]{:S(2)}) collective-permute-start(f32[10,16,128]{2,1,0:T(8,128)S(1)} %get-tuple-element.21), channel_id=1, source_target_pairs={{0,2},{1,3},{2,0},{3,1},{4,6},{5,7},{6,4},{7,5},{8,10},{9,11},{10,... | collective-permute-start | bytes 245768 | tf_op jit(solution)/shard_map/ppermute | solution.py:571
  51.9 1.7 %collective-permute-start.2 = (f32[10,16,128]{2,1,0:T(8,128)S(1)}, f32[10,16,128]{2,1,0:T(8,128)S(1)}, u32[]{:S(2)}, u32[]{:S(2)}) collective-permute-start(f32[10,16,128]{2,1,0:T(8,128)S(1)} %get-tuple-element.21), channel_id=1, source_target_pairs={{0,3},{1,2},{2,1},{3,0},{4,7},{5,6},{6,5},{7,4},{8,11},{9,10},{10,... | collective-permute-start | bytes 245768 | tf_op jit(solution)/shard_map/ppermute | solution.py:571
  53.6 0.2 collective-permute-start.1
  53.8 2.1 %shard_map.103.mine = f32[48,16,128]{2,1,0:T(8,128)S(1)} custom-call(s32[3]{0:T(128)S(1)} %pad_add_fusion.place, s32[8,8]{1,0:T(8,128)S(1)} %bitcast.11, s32[17,17]{1,0:T(8,128)S(1)} %copy-done.11, f32[8,37,16,128]{3,2,1,0:T(8,128)S(1)} %all_to_all.20.early, f32[8,128]{1,0:T(8,128)S(1)} %get-tuple-element.24.after), custom_call_target="tpu_custom_call" | custom-call | flops 1 | bytes 1 | tf_op jit(solution)/shard_map/pallas_call | solution.py:270
  55.9 2.4 %collective-permute-start.7 = (f32[48,16,128]{2,1,0:T(8,128)S(1)}, f32[48,16,128]{2,1,0:T(8,128)}, u32[]{:S(2)}, u32[]{:S(2)}) collective-permute-start(f32[48,16,128]{2,1,0:T(8,128)S(1)} %shard_map.103.mine), channel_id=1, source_target_pairs={{0,2},{2,0},{1,3},{3,1},{4,6},{6,4},{5,7},{7,5},{8,10},{10,8},{9,1... | collective-permute-start | bytes 1179656 | tf_op jit(solution)/shard_map/ppermute | solution.py:564
  58.4 5.9 %collective-permute-done.2 = f32[10,16,128]{2,1,0:T(8,128)S(1)} collective-permute-done((f32[10,16,128]{2,1,0:T(8,128)S(1)}, f32[10,16,128]{2,1,0:T(8,128)S(1)}, u32[]{:S(2)}, u32[]{:S(2)}) %collective-permute-start.2) | collective-permute-done | bytes 81952 | tf_op jit(solution)/shard_map/ppermute | solution.py:571
  64.3 0.7 pad_maximum_fusion.after.refs_0_
  65.0 2.4 %collective-permute-start.6 = (f32[2,10,16,128]{3,2,1,0:T(8,128)}, f32[2,10,16,128]{3,2,1,0:T(8,128)}, u32[]{:S(2)}, u32[]{:S(2)}) collective-permute-start(f32[2,10,16,128]{3,2,1,0:T(8,128)} %pad_maximum_fusion.after.refs_0_), channel_id=1, source_target_pairs={{0,12},{4,8},{8,4},{12,0},{1,13},{5,9},{9,5},{13,1},{2,14},{6,10},... | collective-permute-start | bytes 491528 | tf_op jit(solution)/shard_map/ppermute | solution.py:573
  67.4 0.5 collective-permute-start.5
  67.9 0.6 collective-permute-start.4
  68.5 0.0 all-to-all-done.1.late
  68.5 2.5 %shard_map.102 = (f32[68,16,128]{2,1,0:T(8,128)S(1)}, f32[68,16,128]{2,1,0:T(8,128)S(1)}, f32[8,128]{1,0:T(8,128)S(1)}) custom-call(s32[3]{0:T(128)S(1)} %pad_add_fusion.place, s32[8,8]{1,0:T(8,128)S(1)} %bitcast.12, s32[17,17]{1,0:T(8,128)S(1)} %copy-done.10, s32[2]{0:T(128)S(1)} %iota_multiply_fusion.begins, f32[8,37,16,128]{3,2,1,0:T(8,128)S(1)} %all_to_all.20.early, ...), custom_call_target="tpu_custom_call" | custom-call | flops 1 | bytes 1 | tf_op jit(solution)/shard_map/pallas_call | solution.py:300
  71.0 0.0 copy-start.8
  71.0 0.8 copy-done.8
  71.8 0.8 copy-done.15
  72.7 0.6 collective-permute-done.5.refs_2_
  73.3 0.3 collective-permute-done.4.refs_1_
  73.5 3.8 %collective-permute-done.7.other = f32[48,16,128]{2,1,0:T(8,128)} collective-permute-done((f32[48,16,128]{2,1,0:T(8,128)S(1)}, f32[48,16,128]{2,1,0:T(8,128)}, u32[]{:S(2)}, u32[]{:S(2)}) %collective-permute-start.7) | collective-permute-done | bytes 393248 | tf_op jit(solution)/shard_map/ppermute | solution.py:564
  77.4 2.5 %shard_map.104 = (f32[8,32,16,128]{3,2,1,0:T(8,128)}, f32[8,128]{1,0:T(8,128)S(1)}) custom-call(s32[3]{0:T(128)S(1)} %pad_add_fusion.place, f32[48,16,128]{2,1,0:T(8,128)S(1)} %shard_map.103.mine, f32[48,16,128]{2,1,0:T(8,128)} %collective-permute-done.7.other, f32[8,128]{1,0:T(8,128)S(1)} %get-tuple-element.25.refs_0_, ...), custom_call_target="tpu_custom_call" | custom-call | flops 1 | bytes 1 | tf_op jit(solution)/shard_map/pallas_call | solution.py:328
  79.9 0.0 copy-start.13
  79.9 3.8 %all-to-all-start.3 = ((f32[8,32,16,128]{3,2,1,0:T(8,128)}), f32[8,32,16,128]{3,2,1,0:T(8,128)S(1)}, u32[]{:S(2)}, u32[]{:S(2)}) async-start(f32[8,32,16,128]{3,2,1,0:T(8,128)} %get-tuple-element.29), calls=%async_computation.3 | async-start | bytes 4194304 | tf_op jit(solution)/shard_map/all_to_all | solution.py:559
  83.7 0.0 copy-start
  83.7 1.5 %collective-permute-start.3 = (f32[68,16,128]{2,1,0:T(8,128)}, f32[68,16,128]{2,1,0:T(8,128)S(1)}, u32[]{:S(2)}, u32[]{:S(2)}) collective-permute-start(f32[68,16,128]{2,1,0:T(8,128)} %copy-done.15), channel_id=1, source_target_pairs={{0,2},{2,0},{1,3},{3,1},{4,6},{6,4},{5,7},{7,5},{8,10},{10,8},{9,1... | collective-permute-start | bytes 1671176 | tf_op jit(solution)/shard_map/ppermute | solution.py:564
  85.2 27.8 %shard_map.105 = (f32[512,512]{1,0:T(8,128)S(1)}, f32[512,512]{1,0:T(8,128)S(1)}, f32[8,128]{1,0:T(8,128)S(1)}) custom-call(s32[3]{0:T(128)S(1)} %pad_add_fusion.place, f32[2,10,16,128]{3,2,1,0:T(8,128)} %pad_maximum_fusion.after.refs_0_, f32[2,10,16,128]{3,2,1,0:T(8,128)} %collective-permute-done.4.refs_1_, ...), custom_call_target="tpu_custom_call" | custom-call | flops 1 | bytes 1 | tf_op jit(solution)/shard_map/pallas_call | solution.py:444
  113.1 1.0 copy-done.3
  114.0 1.0 copy-done.5
  115.0 1.9 %collective-permute-done.3.other = f32[68,16,128]{2,1,0:T(8,128)S(1)} collective-permute-done((f32[68,16,128]{2,1,0:T(8,128)}, f32[68,16,128]{2,1,0:T(8,128)S(1)}, u32[]{:S(2)}, u32[]{:S(2)}) %collective-permute-start.3) | collective-permute-done | bytes 557088 | tf_op jit(solution)/shard_map/ppermute | solution.py:564
  116.9 1.1 copy-done.9
  118.0 0.7 shard_map.106
  118.7 0.0 copy-start.2
  118.7 1.0 copy-done.2
  119.6 1.1 all-to-all-done.3.columns
  120.7 6.4 %all-to-all-start.2 = ((f32[8,16,16,128]{3,2,1,0:T(8,128)}), f32[8,16,16,128]{3,2,1,0:T(8,128)}, u32[]{:S(2)}, u32[]{:S(2)}) async-start(f32[8,16,16,128]{3,2,1,0:T(8,128)} %copy-done.2), calls=%async_computation.2 | async-start | bytes 2097152 | tf_op jit(solution)/shard_map/all_to_all | solution.py:559
  127.1 1.2 copy-done.4
  128.3 1.2 copy-done.6
  129.5 0.6 shard_map.107.base_in
  130.2 1.0 copy-done.1
  131.2 9.9 %all-to-all-done.2.rests_in = f32[8,16,16,128]{3,2,1,0:T(8,128)} async-done(((f32[8,16,16,128]{3,2,1,0:T(8,128)}), f32[8,16,16,128]{3,2,1,0:T(8,128)}, u32[]{:S(2)}, u32[]{:S(2)}) %all-to-all-start.2) | async-done | bytes 1048608 | tf_op jit(solution)/shard_map/all_to_all | solution.py:559
  141.1 3.1 %shard_map.108 = f32[512,512]{1,0:T(8,128)} custom-call(s32[3]{0:T(128)S(1)} %pad_add_fusion.place, f32[8,16,16,128]{3,2,1,0:T(8,128)} %all-to-all-done.2.rests_in, f32[512,512]{1,0:T(8,128)} %copy-done.1), custom_call_target="tpu_custom_call" | custom-call | flops 1 | bytes 1 | tf_op jit(solution)/shard_map/pallas_call | solution.py:543
  (22 shorter events, 0.1 us)
Async XLA Ops:
  0.7 0.7 copy-start.14
  7.7 36.5 %copy-start.7 = (f32[8,10,16,128]{3,2,1,0:T(8,128)}, f32[8,10,16,128]{3,2,1,0:T(8,128)S(1)}, u32[]{:S(2)}) copy-start(f32[8,10,16,128]{3,2,1,0:T(8,128)S(1)} %get-tuple-element.20) | copy-start | bytes 1966084
  7.7 40.2 %copy-start.12 = (s32[17,17]{1,0:T(8,128)S(1)}, s32[17,17]{1,0:T(8,128)}, u32[]{:S(2)}) copy-start(s32[17,17]{1,0:T(8,128)} %constant.22.clone.table) | copy-start | bytes 3472
  44.2 9.6 %copy-start.11 = (s32[17,17]{1,0:T(8,128)S(1)}, s32[17,17]{1,0:T(8,128)}, u32[]{:S(2)}) copy-start(s32[17,17]{1,0:T(8,128)} %constant.23.clone.table) | copy-start | bytes 3472
  44.2 24.3 %all-to-all-start.1 = ((f32[8,10,16,128]{3,2,1,0:T(8,128)}), f32[8,10,16,128]{3,2,1,0:T(8,128)S(1)}, u32[]{:S(2)}, u32[]{:S(2)}) async-start(f32[8,10,16,128]{3,2,1,0:T(8,128)} %copy-done.7), calls=%async_computation.1 | async-start | bytes 1310720 | tf_op jit(solution)/shard_map/all_to_all | solution.py:559
  49.2 19.2 %copy-start.10 = (s32[17,17]{1,0:T(8,128)S(1)}, s32[17,17]{1,0:T(8,128)}, u32[]{:S(2)}) copy-start(s32[17,17]{1,0:T(8,128)} %constant.24.clone.table) | copy-start | bytes 3472
  49.2 9.1 %collective-permute-start = (f32[10,16,128]{2,1,0:T(8,128)S(1)}, f32[10,16,128]{2,1,0:T(8,128)S(1)}, u32[]{:S(2)}, u32[]{:S(2)}) collective-permute-start(f32[10,16,128]{2,1,0:T(8,128)S(1)} %get-tuple-element.21), channel_id=1, source_target_pairs={{0,2},{1,3},{2,0},{3,1},{4,6},{5,7},{6,4},{7,5},{8,10},{9,11},{10,... | collective-permute-start | bytes 245768 | tf_op jit(solution)/shard_map/ppermute | solution.py:571
  51.9 12.4 %collective-permute-start.2 = (f32[10,16,128]{2,1,0:T(8,128)S(1)}, f32[10,16,128]{2,1,0:T(8,128)S(1)}, u32[]{:S(2)}, u32[]{:S(2)}) collective-permute-start(f32[10,16,128]{2,1,0:T(8,128)S(1)} %get-tuple-element.21), channel_id=1, source_target_pairs={{0,3},{1,2},{2,1},{3,0},{4,7},{5,6},{6,5},{7,4},{8,11},{9,10},{10,... | collective-permute-start | bytes 245768 | tf_op jit(solution)/shard_map/ppermute | solution.py:571
  53.6 10.7 %collective-permute-start.1 = (f32[10,16,128]{2,1,0:T(8,128)S(1)}, f32[10,16,128]{2,1,0:T(8,128)S(1)}, u32[]{:S(2)}, u32[]{:S(2)}) collective-permute-start(f32[10,16,128]{2,1,0:T(8,128)S(1)} %get-tuple-element.21), channel_id=1, source_target_pairs={{0,1},{1,0},{2,3},{3,2},{4,5},{5,4},{6,7},{7,6},{8,9},{9,8},{10,11... | collective-permute-start | bytes 245768 | tf_op jit(solution)/shard_map/ppermute | solution.py:571
  55.9 21.4 %collective-permute-start.7 = (f32[48,16,128]{2,1,0:T(8,128)S(1)}, f32[48,16,128]{2,1,0:T(8,128)}, u32[]{:S(2)}, u32[]{:S(2)}) collective-permute-start(f32[48,16,128]{2,1,0:T(8,128)S(1)} %shard_map.103.mine), channel_id=1, source_target_pairs={{0,2},{2,0},{1,3},{3,1},{4,6},{6,4},{5,7},{7,5},{8,10},{10,8},{9,1... | collective-permute-start | bytes 1179656 | tf_op jit(solution)/shard_map/ppermute | solution.py:564
  65.0 7.7 %collective-permute-start.6 = (f32[2,10,16,128]{3,2,1,0:T(8,128)}, f32[2,10,16,128]{3,2,1,0:T(8,128)}, u32[]{:S(2)}, u32[]{:S(2)}) collective-permute-start(f32[2,10,16,128]{3,2,1,0:T(8,128)} %pad_maximum_fusion.after.refs_0_), channel_id=1, source_target_pairs={{0,12},{4,8},{8,4},{12,0},{1,13},{5,9},{9,5},{13,1},{2,14},{6,10},... | collective-permute-start | bytes 491528 | tf_op jit(solution)/shard_map/ppermute | solution.py:573
  67.4 5.9 %collective-permute-start.5 = (f32[2,10,16,128]{3,2,1,0:T(8,128)}, f32[2,10,16,128]{3,2,1,0:T(8,128)}, u32[]{:S(2)}, u32[]{:S(2)}) collective-permute-start(f32[2,10,16,128]{3,2,1,0:T(8,128)} %pad_maximum_fusion.after.refs_0_), channel_id=1, source_target_pairs={{0,8},{4,12},{8,0},{12,4},{1,9},{5,13},{9,1},{13,5},{2,10},{6,14},... | collective-permute-start | bytes 491528 | tf_op jit(solution)/shard_map/ppermute | solution.py:573
  67.9 5.6 %collective-permute-start.4 = (f32[2,10,16,128]{3,2,1,0:T(8,128)}, f32[2,10,16,128]{3,2,1,0:T(8,128)}, u32[]{:S(2)}, u32[]{:S(2)}) collective-permute-start(f32[2,10,16,128]{3,2,1,0:T(8,128)} %pad_maximum_fusion.after.refs_0_), channel_id=1, source_target_pairs={{0,4},{4,0},{8,12},{12,8},{1,5},{5,1},{9,13},{13,9},{2,6},{6,2},{1... | collective-permute-start | bytes 491528 | tf_op jit(solution)/shard_map/ppermute | solution.py:573
  71.0 0.8 copy-start.8
  71.8 0.8 copy-start.15
  79.9 37.0 %copy-start.13 = (s32[4,4]{1,0:T(4,128)S(1)}, s32[4,4]{1,0:T(4,128)}, u32[]{:S(2)}) copy-start(s32[4,4]{1,0:T(4,128)} %constant.26.clone.starts) | copy-start | bytes 196
  79.9 40.8 %all-to-all-start.3 = ((f32[8,32,16,128]{3,2,1,0:T(8,128)}), f32[8,32,16,128]{3,2,1,0:T(8,128)S(1)}, u32[]{:S(2)}, u32[]{:S(2)}) async-start(f32[8,32,16,128]{3,2,1,0:T(8,128)} %get-tuple-element.29), calls=%async_computation.3 | async-start | bytes 4194304 | tf_op jit(solution)/shard_map/all_to_all | solution.py:559
  83.7 43.4 %copy-start = (f32[512,512]{1,0:T(8,128)S(1)}, f32[512,512]{1,0:T(8,128)}, u32[]{:S(2)}) copy-start(f32[512,512]{1,0:T(8,128)} %parent.3) | copy-start | bytes 3145732
  83.7 33.2 %collective-permute-start.3 = (f32[68,16,128]{2,1,0:T(8,128)}, f32[68,16,128]{2,1,0:T(8,128)S(1)}, u32[]{:S(2)}, u32[]{:S(2)}) collective-permute-start(f32[68,16,128]{2,1,0:T(8,128)} %copy-done.15), channel_id=1, source_target_pairs={{0,2},{2,0},{1,3},{3,1},{4,6},{6,4},{5,7},{7,5},{8,10},{10,8},{9,1... | collective-permute-start | bytes 1671176 | tf_op jit(solution)/shard_map/ppermute | solution.py:564
  113.0 1.0 copy-start.3
  114.0 1.0 copy-start.5
  116.9 1.1 copy-start.9
  118.7 1.0 copy-start.2
  120.7 20.4 %all-to-all-start.2 = ((f32[8,16,16,128]{3,2,1,0:T(8,128)}), f32[8,16,16,128]{3,2,1,0:T(8,128)}, u32[]{:S(2)}, u32[]{:S(2)}) async-start(f32[8,16,16,128]{3,2,1,0:T(8,128)} %copy-done.2), calls=%async_computation.2 | async-start | bytes 2097152 | tf_op jit(solution)/shard_map/all_to_all | solution.py:559
  127.1 1.2 copy-start.4
  128.3 1.2 copy-start.6
  130.2 1.0 copy-start.1

commit v5 on v4

--- a/solution.py
+++ b/solution.py
@@ -308,44 +308,50 @@
 
 
 def column_kernel(place, mine, other, *refs, plan):
-    sent, token, total, out, sems = refs[-5:]
-    token[...] = jnp.zeros_like(token)
+    sent, token, total, sems = refs[-4:]
     nb2 = len(plan.full)
     total[...] = mine[...] + other[...]
+    copies = []
     for r in range(plan.rows):
         for n in range(plan.near):
             d = r * plan.near + n
-            out[d, :nb2] = total[max(r - 1, 0) * nb2 : max(r - 1, 0) * nb2 + nb2]
             col = jnp.maximum(place[1] * plan.near + n - 1, 0)
-            out[d, nb2:] = total[pl.ds(col * nb2, nb2)]
-            pltpu.make_async_copy(out.at[d], sent.at[d], sems.at[d]).start()
-    for d in range(plan.members):
-        pltpu.make_async_copy(out.at[d], sent.at[d], sems.at[d]).wait()
+            for k, first in enumerate((max(r - 1, 0) * nb2, col * nb2)):
+                source, dest = total.at[pl.ds(first, nb2)], sent.at[d, pl.ds(k * nb2, nb2)]
+                copies.append(pltpu.make_async_copy(source, dest, sems.at[2 * d + k]))
+    for copy in copies:
+        copy.start()
+    token[...] = jnp.zeros_like(token)
+    for copy in copies:
+        copy.wait()
 
 
 def column_strips(place, mine, other, plan, after):
     shape = (plan.members, 2 * len(plan.full)) + mine.shape[1:]
     return call(
         functools.partial(column_kernel, plan=plan),
-        12,
+        8,
         in_specs=[SMEM] + [VMEM] * 2 + [AFTER] * len(after),
         out_specs=[HBM, VMEM],
         out_shape=[pltpu.HBM(shape, F32), TOKEN],
-        scratch_shapes=[
-            pltpu.VMEM(mine.shape, F32),
-            pltpu.VMEM(shape, F32),
-            pltpu.SemaphoreType.DMA((plan.members,)),
-        ],
+        scratch_shapes=[pltpu.VMEM(mine.shape, F32), pltpu.SemaphoreType.DMA((2 * plan.members,))],
     )(place, mine, other, *after)
 
 
-def rest_kernel(place, starts, mine, other, after, out, token, total, *, plan):
-    token[...] = jnp.zeros_like(token)
+def rest_kernel(place, starts, mine, other, after, sent, token, total, sems, *, plan):
     nb2 = len(plan.full)
     total[...] = mine[...] + other[...]
+    copies = []
     for r in range(plan.rows):
         for n in range(plan.near):
-            out[r * plan.near + n] = total[pl.ds(starts[place[1] * plan.near + n, r], nb2)]
+            d = r * plan.near + n
+            source = total.at[pl.ds(starts[place[1] * plan.near + n, r], nb2)]
+            copies.append(pltpu.make_async_copy(source, sent.at[d], sems.at[d]))
+    for copy in copies:
+        copy.start()
+    token[...] = jnp.zeros_like(token)
+    for copy in copies:
+        copy.wait()
 
 
 def rest_strips(place, mine, other, plan, after):
@@ -355,13 +361,14 @@
     for c in range(1, cols):
         for r in range(1, plan.rows):
             starts[c, r] = min(plan.rest_at(r, c) - plan.begins[c // plan.near], plan.window - nb2)
+    shape = (plan.members, nb2) + mine.shape[1:]
     return call(
         functools.partial(rest_kernel, plan=plan),
-        6,
+        4,
         in_specs=[SMEM] * 2 + [VMEM] * 2 + [AFTER],
-        out_specs=[VMEM] * 2,
-        out_shape=[jax.ShapeDtypeStruct((plan.members, len(plan.full)) + mine.shape[1:], F32), TOKEN],
-        scratch_shapes=[pltpu.VMEM(mine.shape, F32)],
+        out_specs=[HBM, VMEM],
+        out_shape=[pltpu.HBM(shape, F32), TOKEN],
+        scratch_shapes=[pltpu.VMEM(mine.shape, F32), pltpu.SemaphoreType.DMA((plan.members,))],
     )(place, jnp.asarray(starts), mine, other, after)
 
 
@@ -408,7 +415,9 @@
 
 
 def cholesky_kernel(place, *refs, plan):
-    heads, (l_ref, x_ref, token, s) = refs[: plan.rows], refs[-4:]
+    heads, (keep, _, l_ref, x_ref, brought, token, s, sem) = refs[: plan.rows], refs[plan.rows :]
+    copy = pltpu.make_async_copy(keep, brought, sem)
+    copy.start()
     token[...] = jnp.zeros_like(token)
     n = l_ref.shape[0]
     blk, nb = plan.blk, plan.blk // 2
@@ -437,18 +446,19 @@
             s[end:, end:] -= dot_nt(below, below)
             l_ref[end:, off:end] = below
             x_ref[end:, :end] -= dot_nn(below, x_ref[off:end, :end])
-
-
-def cholesky(place, heads, n, plan, after):
+    copy.wait()
+
+
+def cholesky(place, heads, keep, n, plan, after):
     square = jax.ShapeDtypeStruct((n, n), F32)
     return call(
         functools.partial(cholesky_kernel, plan=plan),
         12,
-        in_specs=[SMEM] + [VMEM] * plan.rows + [AFTER],
-        out_specs=[VMEM] * 3,
-        out_shape=[square, square, TOKEN],
-        scratch_shapes=[pltpu.VMEM((n, n), F32)],
-    )(place, *heads, after)
+        in_specs=[SMEM] + [VMEM] * plan.rows + [HBM, AFTER],
+        out_specs=[VMEM] * 4,
+        out_shape=[square, square, jax.ShapeDtypeStruct(keep.shape, F32), TOKEN],
+        scratch_shapes=[pltpu.VMEM((n, n), F32), pltpu.SemaphoreType.DMA(())],
+    )(place, *heads, in_hbm(keep), after)
 
 
 def put(ref, source, first, blocks, plan):
@@ -504,9 +514,9 @@
     )(place, columns, parent, l, x, after)
 
 
-def finish_kernel(place, rests_in, base_in, out, tile, rests, base, sems, *, plan):
-    blk = plan.blk
-    copies = [pltpu.make_async_copy(rests_in, rests, sems.at[0]), pltpu.make_async_copy(base_in, base, sems.at[1])]
+def finish_kernel(place, rests_in, base_in, out_ref, tile, rests, base, out, sems, *, plan):
+    blk, nb = plan.blk, plan.per_tile
+    copies = [pltpu.make_async_copy(base_in, base, sems.at[0]), pltpu.make_async_copy(rests_in, rests, sems.at[1])]
     for copy in copies:
         copy.start()
     for copy in copies:
@@ -514,9 +524,20 @@
     row = place[0]
     col = place[1] * plan.near + place[2]
 
+    def write(value):
+        parts = []
+        for a in range(nb):
+            rows = slice(a * blk, (a + 1) * blk)
+            out[rows, :] = value(rows)
+            window = pl.ds(a * blk, blk)
+            parts.append(pltpu.make_async_copy(out.at[window], out_ref.at[window], sems.at[2 + a]))
+            parts[-1].start()
+        for copy in parts:
+            copy.wait()
+
     @pl.when((row == 0) | (col == 0))
     def _():
-        out[...] = base[...]
+        write(lambda rows: base[rows, :])
 
     @pl.when((row > 0) & (col == row))
     def _():
@@ -526,17 +547,17 @@
                 tile[b * blk : (b + 1) * blk, a * blk : (a + 1) * blk] = tile[
                     a * blk : (a + 1) * blk, b * blk : (b + 1) * blk
                 ].T
-        out[...] = base[...] + tile[...]
+        write(lambda rows: base[rows, :] + tile[rows, :])
 
     @pl.when((row > col) & (col > 0))
     def _():
         put(tile, rests, 0, plan.full, plan)
-        out[...] = base[...] + tile[...]
+        write(lambda rows: base[rows, :] + tile[rows, :])
 
     @pl.when((row > 0) & (row < col))
     def _():
         put(tile, rests, 0, plan.full, plan)
-        out[...] = base[...] + tile[...].T
+        write(lambda rows: base[rows, :] + tile[:, rows].T)
 
 
 def finish(place, rests, base, plan):
@@ -544,13 +565,14 @@
         functools.partial(finish_kernel, plan=plan),
         10,
         in_specs=[SMEM] + [HBM] * 2,
-        out_specs=VMEM,
+        out_specs=HBM,
         out_shape=jax.ShapeDtypeStruct(base.shape, F32),
         scratch_shapes=[
             pltpu.VMEM(base.shape, F32),
             pltpu.VMEM(rests.shape, F32),
             pltpu.VMEM(base.shape, F32),
-            pltpu.SemaphoreType.DMA((2,)),
+            pltpu.VMEM(base.shape, F32),
+            pltpu.SemaphoreType.DMA((2 + plan.per_tile,)),
         ],
     )(place, in_hbm(rests), in_hbm(base))
 
@@ -588,7 +610,7 @@
     keep, send, token = merge_rest(place, maps, early, late, plan, heads[0])
     sent, token = column_strips(place, column, far_column, plan, [token] + heads[1:])
     columns = all_to_all(sent)
-    l, x, token = cholesky(place, heads, parent_front.shape[0], plan, token)
+    l, x, keep, token = cholesky(place, heads, keep, parent_front.shape[0], plan, token)
     sent, token = rest_strips(place, keep, across(send, plan), plan, token)
     base = panel(place, columns, parent_front, l, x, plan, token)
     rests = all_to_all(sent)

time: 145 us -> 144 us (level)
  local copies, waits for them, and re-layouts: 9.68 us -> 7.67 us
  Pallas kernels: 47.1 us -> 48.6 us
    unnamed x32 -> x28, local copies, waits for them, and re-layouts: 9.68 us -> 7.67 us
  transfers between devices with their start and end apart: 11 -> 11, of which waited for: 7 -> 7; matrix products, arithmetic and copies ran while one was open for 0% -> 0% of each run, Pallas kernels for 24% -> 26%
where the time goes in v5:
time: 144 us; the launch traced here: 143 us
  Pallas kernels  48.6 us (34%)
  blocking collectives  36.5 us (25%)
  starting transfers between devices  24.7 us (17%)
  waiting for transfers between devices  24 us (17%)
  local copies, waits for them, and re-layouts  7.67 us (5%)
    all_to_all x1, blocking collectives, all_to_all(): return lax.all_to_all(x, GROUP, 0, 0, tiled=True)  36.5 us
    pallas_call x1, Pallas kernels, cholesky(): call(functools.partial(cholesky_kernel, plan=plan), 12, in_specs=[SMEM] +...  28.6 us
    all_to_all x3, starting transfers between devices, all_to_all(): return lax.all_to_all(x, GROUP, 0, 0, tiled=True)  12.6 us
    all_to_all x3, waiting for transfers between devices, all_to_all(): return lax.all_to_all(x, GROUP, 0, 0, tiled=True)  12.1 us
    unnamed x28, local copies, waits for them, and re-layouts  7.67 us
    pallas_call x1, Pallas kernels, update_strips(): call(functools.partial(update_kernel, plan=plan), 24, in_specs=[SMEM] * 3...  6.26 us
    ppermute x3, waiting for transfers between devices, spread_head(): lax.ppermute(head, ('far', 'near'), [(d, d ^ k) for d in range(cols)])  5.87 us
    ppermute x2, waiting for transfers between devices, across(): lax.ppermute(x, 'far', [(f, (f + by) % plan.far) for f in range(plan.far)])  5.14 us
  transfers between devices with their start and end apart: 11, of which 7 were waited for; matrix products, arithmetic and copies ran while one was open for 0% of the time, Pallas kernels for 26%

profile of v5, /device:TPU:0, one launch (start us, length us, event | category | flops | bytes accessed | tf_op | source)
XLA Modules:
  0.0 143.3 jit_solution(8959823080765928749)
XLA Ops:
  0.7 0.1 pad_add_fusion.place
  0.7 0.7 copy-done.12
  1.4 6.3 %shard_map.100 = (f32[8,37,16,128]{3,2,1,0:T(8,128)S(1)}, f32[8,10,16,128]{3,2,1,0:T(8,128)S(1)}) custom-call(s32[3]{0:T(128)S(1)} %pad_add_fusion.place, s32[1]{0:T(128)S(6)} %copy.11.blocks, s32[1,8]{1,0:T(1,128)S(1)} %copy-done.12, f32[1024,512]{1,0:T(8,128)} %bitcast.13, f32[512,512]{1,0:T(8,128)} %bitcast.14, f32[512,512]{1,0:T(8,128)} %parent.3), custom_call_target="tpu_custom_call" | custom-call | flops 1 | bytes 1 | tf_op jit(solution)/shard_map/pallas_call | solution.py:181
  7.7 0.0 copy-start.6
  7.7 0.0 copy-start.10
  7.7 36.5 %all_to_all.20.early = f32[8,37,16,128]{3,2,1,0:T(8,128)S(1)} all-to-all(f32[8,37,16,128]{3,2,1,0:T(8,128)S(1)} %get-tuple-element.20), channel_id=1, replica_groups=mesh['leaf'=2,'prow'=4,'far'=2,'near'=2] {'prow','near'}, dimensions={0} | all-to-all | bytes 4849664 | tf_op jit(solution)/shard_map/all_to_all | solution.py:581
  44.2 3.7 %all-to-all-start.1 = ((f32[8,10,16,128]{3,2,1,0:T(8,128)}), f32[8,10,16,128]{3,2,1,0:T(8,128)S(1)}, u32[]{:S(2)}, u32[]{:S(2)}) async-start(f32[8,10,16,128]{3,2,1,0:T(8,128)} %copy-done.6), calls=%async_computation.1 | async-start | bytes 1310720 | tf_op jit(solution)/shard_map/all_to_all | solution.py:581
  47.9 1.3 shard_map.101
  49.2 0.0 copy-start.8
  49.2 2.7 %collective-permute-start = (f32[10,16,128]{2,1,0:T(8,128)S(1)}, f32[10,16,128]{2,1,0:T(8,128)S(1)}, u32[]{:S(2)}, u32[]{:S(2)}) collective-permute-start(f32[10,16,128]{2,1,0:T(8,128)S(1)} %get-tuple-element.21), channel_id=1, source_target_pairs={{0,2},{1,3},{2,0},{3,1},{4,6},{5,7},{6,4},{7,5},{8,10},{9,11},{10,... | collective-permute-start | bytes 245768 | tf_op jit(solution)/shard_map/ppermute | solution.py:593
  51.9 1.7 %collective-permute-start.2 = (f32[10,16,128]{2,1,0:T(8,128)S(1)}, f32[10,16,128]{2,1,0:T(8,128)S(1)}, u32[]{:S(2)}, u32[]{:S(2)}) collective-permute-start(f32[10,16,128]{2,1,0:T(8,128)S(1)} %get-tuple-element.21), channel_id=1, source_target_pairs={{0,3},{1,2},{2,1},{3,0},{4,7},{5,6},{6,5},{7,4},{8,11},{9,10},{10,... | collective-permute-start | bytes 245768 | tf_op jit(solution)/shard_map/ppermute | solution.py:593
  53.5 0.2 collective-permute-start.1
  53.8 2.1 %shard_map.103.mine = f32[48,16,128]{2,1,0:T(8,128)S(1)} custom-call(s32[3]{0:T(128)S(1)} %pad_add_fusion.place, s32[8,8]{1,0:T(8,128)S(1)} %bitcast.11, s32[17,17]{1,0:T(8,128)S(1)} %copy-done.9, f32[8,37,16,128]{3,2,1,0:T(8,128)S(1)} %all_to_all.20.early, f32[8,128]{1,0:T(8,128)S(1)} %get-tuple-element.24.after), custom_call_target="tpu_custom_call" | custom-call | flops 1 | bytes 1 | tf_op jit(solution)/shard_map/pallas_call | solution.py:270
  55.8 2.6 %collective-permute-start.6 = (f32[48,16,128]{2,1,0:T(8,128)S(1)}, f32[48,16,128]{2,1,0:T(8,128)}, u32[]{:S(2)}, u32[]{:S(2)}) collective-permute-start(f32[48,16,128]{2,1,0:T(8,128)S(1)} %shard_map.103.mine), channel_id=1, source_target_pairs={{0,2},{2,0},{1,3},{3,1},{4,6},{6,4},{5,7},{7,5},{8,10},{10,8},{9,1... | collective-permute-start | bytes 1179656 | tf_op jit(solution)/shard_map/ppermute | solution.py:586
  58.4 0.0 collective-permute-done
  58.4 5.9 %collective-permute-done.2 = f32[10,16,128]{2,1,0:T(8,128)S(1)} collective-permute-done((f32[10,16,128]{2,1,0:T(8,128)S(1)}, f32[10,16,128]{2,1,0:T(8,128)S(1)}, u32[]{:S(2)}, u32[]{:S(2)}) %collective-permute-start.2) | collective-permute-done | bytes 81952 | tf_op jit(solution)/shard_map/ppermute | solution.py:593
  64.3 0.0 collective-permute-done.1
  64.3 0.7 pad_maximum_fusion.after.refs_0_
  65.0 2.4 %collective-permute-start.5 = (f32[2,10,16,128]{3,2,1,0:T(8,128)}, f32[2,10,16,128]{3,2,1,0:T(8,128)}, u32[]{:S(2)}, u32[]{:S(2)}) collective-permute-start(f32[2,10,16,128]{3,2,1,0:T(8,128)} %pad_maximum_fusion.after.refs_0_), channel_id=1, source_target_pairs={{0,12},{4,8},{8,4},{12,0},{1,13},{5,9},{9,5},{13,1},{2,14},{6,10},... | collective-permute-start | bytes 491528 | tf_op jit(solution)/shard_map/ppermute | solution.py:595
  67.4 0.5 collective-permute-start.4
  67.9 0.6 collective-permute-start.3
  68.5 0.0 all-to-all-done.1.late
  68.5 2.5 %shard_map.102 = (f32[68,16,128]{2,1,0:T(8,128)S(1)}, f32[68,16,128]{2,1,0:T(8,128)S(1)}, f32[8,128]{1,0:T(8,128)S(1)}) custom-call(s32[3]{0:T(128)S(1)} %pad_add_fusion.place, s32[8,8]{1,0:T(8,128)S(1)} %bitcast.12, s32[17,17]{1,0:T(8,128)S(1)} %copy-done.8, s32[2]{0:T(128)S(1)} %iota_multiply_fusion.begins, f32[8,37,16,128]{3,2,1,0:T(8,128)S(1)} %all_to_all.20.early, ...), custom_call_target="tpu_custom_call" | custom-call | flops 1 | bytes 1 | tf_op jit(solution)/shard_map/pallas_call | solution.py:300
  71.0 0.0 copy-start.7
  71.0 0.8 copy-done.7
  71.8 0.8 copy-done.13
  72.6 0.0 collective-permute-done.5.refs_3_
  72.6 0.7 collective-permute-done.4.refs_2_
  73.3 0.3 collective-permute-done.3.refs_1_
  73.6 3.8 %collective-permute-done.6.other = f32[48,16,128]{2,1,0:T(8,128)} collective-permute-done((f32[48,16,128]{2,1,0:T(8,128)S(1)}, f32[48,16,128]{2,1,0:T(8,128)}, u32[]{:S(2)}, u32[]{:S(2)}) %collective-permute-start.6) | collective-permute-done | bytes 393248 | tf_op jit(solution)/shard_map/ppermute | solution.py:586
  77.4 2.6 %shard_map.104 = (f32[8,32,16,128]{3,2,1,0:T(8,128)}, f32[8,128]{1,0:T(8,128)S(1)}) custom-call(s32[3]{0:T(128)S(1)} %pad_add_fusion.place, f32[48,16,128]{2,1,0:T(8,128)S(1)} %shard_map.103.mine, f32[48,16,128]{2,1,0:T(8,128)} %collective-permute-done.6.other, f32[8,128]{1,0:T(8,128)S(1)} %get-tuple-element.25.refs_0_, ...), custom_call_target="tpu_custom_call" | custom-call | flops 1 | bytes 1 | tf_op jit(solution)/shard_map/pallas_call | solution.py:331
  79.9 0.0 copy-start.11
  80.0 3.8 %all-to-all-start.3 = ((f32[8,32,16,128]{3,2,1,0:T(8,128)}), f32[8,32,16,128]{3,2,1,0:T(8,128)S(1)}, u32[]{:S(2)}, u32[]{:S(2)}) async-start(f32[8,32,16,128]{3,2,1,0:T(8,128)} %get-tuple-element.31), calls=%async_computation.3 | async-start | bytes 4194304 | tf_op jit(solution)/shard_map/all_to_all | solution.py:581
  83.8 0.0 copy-start
  83.8 1.5 %collective-permute-start.7 = (f32[68,16,128]{2,1,0:T(8,128)}, f32[68,16,128]{2,1,0:T(8,128)S(1)}, u32[]{:S(2)}, u32[]{:S(2)}) collective-permute-start(f32[68,16,128]{2,1,0:T(8,128)} %copy-done.13), channel_id=1, source_target_pairs={{0,2},{2,0},{1,3},{3,1},{4,6},{6,4},{5,7},{7,5},{8,10},{10,8},{9,1... | collective-permute-start | bytes 1671176 | tf_op jit(solution)/shard_map/ppermute | solution.py:586
  85.2 28.6 %shard_map.105 = (f32[512,512]{1,0:T(8,128)S(1)}, f32[512,512]{1,0:T(8,128)S(1)}, f32[68,16,128]{2,1,0:T(8,128)S(1)}, f32[8,128]{1,0:T(8,128)S(1)}) custom-call(s32[3]{0:T(128)S(1)} %pad_add_fusion.place, f32[2,10,16,128]{3,2,1,0:T(8,128)} %pad_maximum_fusion.after.refs_0_, f32[2,10,16,128]{3,2,1,0:T(8,128)} %collective-permute-done.3.refs_1_, ...), custom_call_target="tpu_custom_call" | custom-call | flops 1 | bytes 1 | tf_op jit(solution)/shard_map/pallas_call | solution.py:454
  113.8 1.0 copy-done.2
  114.8 1.0 copy-done.4
  115.8 1.3 collective-permute-done.7.other
  117.1 1.6 %shard_map.106 = (f32[8,16,16,128]{3,2,1,0:T(8,128)}, f32[8,128]{1,0:T(8,128)S(1)}) custom-call(s32[3]{0:T(128)S(1)} %pad_add_fusion.place, s32[4,4]{1,0:T(4,128)S(1)} %copy-done.11, f32[68,16,128]{2,1,0:T(8,128)S(1)} %get-tuple-element.27.mine, f32[68,16,128]{2,1,0:T(8,128)S(1)} %collective-permute-done.7.other, f32[8,128]{1,0:T(8,128)S(1)} %get-tuple-element.29.after), custom_call_target="tpu_custom_call" | custom-call | flops 1 | bytes 1 | tf_op jit(solution)/shard_map/pallas_call | solution.py:365
  118.7 2.1 %all-to-all-done.3.columns = f32[8,32,16,128]{3,2,1,0:T(8,128)S(1)} async-done(((f32[8,32,16,128]{3,2,1,0:T(8,128)}), f32[8,32,16,128]{3,2,1,0:T(8,128)S(1)}, u32[]{:S(2)}, u32[]{:S(2)}) %all-to-all-start.3) | async-done | bytes 2097184 | tf_op jit(solution)/shard_map/all_to_all | solution.py:581
  120.9 5.2 %all-to-all-start.2 = ((f32[8,16,16,128]{3,2,1,0:T(8,128)}), f32[8,16,16,128]{3,2,1,0:T(8,128)}, u32[]{:S(2)}, u32[]{:S(2)}) async-start(f32[8,16,16,128]{3,2,1,0:T(8,128)} %get-tuple-element.30), calls=%async_computation.2 | async-start | bytes 2097152 | tf_op jit(solution)/shard_map/all_to_all | solution.py:581
  126.0 1.2 copy-done.3
  127.3 1.2 copy-done.5
  128.5 0.6 shard_map.107.base_in
  129.1 1.0 copy-done.1
  130.1 9.9 %all-to-all-done.2.rests_in = f32[8,16,16,128]{3,2,1,0:T(8,128)} async-done(((f32[8,16,16,128]{3,2,1,0:T(8,128)}), f32[8,16,16,128]{3,2,1,0:T(8,128)}, u32[]{:S(2)}, u32[]{:S(2)}) %all-to-all-start.2) | async-done | bytes 1048608 | tf_op jit(solution)/shard_map/all_to_all | solution.py:581
  140.0 3.1 %shard_map.108 = f32[512,512]{1,0:T(8,128)} custom-call(s32[3]{0:T(128)S(1)} %pad_add_fusion.place, f32[8,16,16,128]{3,2,1,0:T(8,128)} %all-to-all-done.2.rests_in, f32[512,512]{1,0:T(8,128)} %copy-done.1), custom_call_target="tpu_custom_call" | custom-call | flops 1 | bytes 1 | tf_op jit(solution)/shard_map/pallas_call | solution.py:564
  (18 shorter events, 0.1 us)
Async XLA Ops:
  0.7 0.7 copy-start.12
  7.7 36.5 %copy-start.6 = (f32[8,10,16,128]{3,2,1,0:T(8,128)}, f32[8,10,16,128]{3,2,1,0:T(8,128)S(1)}, u32[]{:S(2)}) copy-start(f32[8,10,16,128]{3,2,1,0:T(8,128)S(1)} %get-tuple-element.22) | copy-start | bytes 1966084
  7.7 40.2 %copy-start.10 = (s32[17,17]{1,0:T(8,128)S(1)}, s32[17,17]{1,0:T(8,128)}, u32[]{:S(2)}) copy-start(s32[17,17]{1,0:T(8,128)} %constant.22.clone.table) | copy-start | bytes 3472
  44.2 9.6 %copy-start.9 = (s32[17,17]{1,0:T(8,128)S(1)}, s32[17,17]{1,0:T(8,128)}, u32[]{:S(2)}) copy-start(s32[17,17]{1,0:T(8,128)} %constant.23.clone.table) | copy-start | bytes 3472
  44.2 24.3 %all-to-all-start.1 = ((f32[8,10,16,128]{3,2,1,0:T(8,128)}), f32[8,10,16,128]{3,2,1,0:T(8,128)S(1)}, u32[]{:S(2)}, u32[]{:S(2)}) async-start(f32[8,10,16,128]{3,2,1,0:T(8,128)} %copy-done.6), calls=%async_computation.1 | async-start | bytes 1310720 | tf_op jit(solution)/shard_map/all_to_all | solution.py:581
  49.2 19.3 %copy-start.8 = (s32[17,17]{1,0:T(8,128)S(1)}, s32[17,17]{1,0:T(8,128)}, u32[]{:S(2)}) copy-start(s32[17,17]{1,0:T(8,128)} %constant.24.clone.table) | copy-start | bytes 3472
  49.2 9.2 %collective-permute-start = (f32[10,16,128]{2,1,0:T(8,128)S(1)}, f32[10,16,128]{2,1,0:T(8,128)S(1)}, u32[]{:S(2)}, u32[]{:S(2)}) collective-permute-start(f32[10,16,128]{2,1,0:T(8,128)S(1)} %get-tuple-element.21), channel_id=1, source_target_pairs={{0,2},{1,3},{2,0},{3,1},{4,6},{5,7},{6,4},{7,5},{8,10},{9,11},{10,... | collective-permute-start | bytes 245768 | tf_op jit(solution)/shard_map/ppermute | solution.py:593
  51.9 12.4 %collective-permute-start.2 = (f32[10,16,128]{2,1,0:T(8,128)S(1)}, f32[10,16,128]{2,1,0:T(8,128)S(1)}, u32[]{:S(2)}, u32[]{:S(2)}) collective-permute-start(f32[10,16,128]{2,1,0:T(8,128)S(1)} %get-tuple-element.21), channel_id=1, source_target_pairs={{0,3},{1,2},{2,1},{3,0},{4,7},{5,6},{6,5},{7,4},{8,11},{9,10},{10,... | collective-permute-start | bytes 245768 | tf_op jit(solution)/shard_map/ppermute | solution.py:593
  53.5 10.7 %collective-permute-start.1 = (f32[10,16,128]{2,1,0:T(8,128)S(1)}, f32[10,16,128]{2,1,0:T(8,128)S(1)}, u32[]{:S(2)}, u32[]{:S(2)}) collective-permute-start(f32[10,16,128]{2,1,0:T(8,128)S(1)} %get-tuple-element.21), channel_id=1, source_target_pairs={{0,1},{1,0},{2,3},{3,2},{4,5},{5,4},{6,7},{7,6},{8,9},{9,8},{10,11... | collective-permute-start | bytes 245768 | tf_op jit(solution)/shard_map/ppermute | solution.py:593
  55.8 21.5 %collective-permute-start.6 = (f32[48,16,128]{2,1,0:T(8,128)S(1)}, f32[48,16,128]{2,1,0:T(8,128)}, u32[]{:S(2)}, u32[]{:S(2)}) collective-permute-start(f32[48,16,128]{2,1,0:T(8,128)S(1)} %shard_map.103.mine), channel_id=1, source_target_pairs={{0,2},{2,0},{1,3},{3,1},{4,6},{6,4},{5,7},{7,5},{8,10},{10,8},{9,1... | collective-permute-start | bytes 1179656 | tf_op jit(solution)/shard_map/ppermute | solution.py:586
  65.0 7.6 %collective-permute-start.5 = (f32[2,10,16,128]{3,2,1,0:T(8,128)}, f32[2,10,16,128]{3,2,1,0:T(8,128)}, u32[]{:S(2)}, u32[]{:S(2)}) collective-permute-start(f32[2,10,16,128]{3,2,1,0:T(8,128)} %pad_maximum_fusion.after.refs_0_), channel_id=1, source_target_pairs={{0,12},{4,8},{8,4},{12,0},{1,13},{5,9},{9,5},{13,1},{2,14},{6,10},... | collective-permute-start | bytes 491528 | tf_op jit(solution)/shard_map/ppermute | solution.py:595
  67.4 5.9 %collective-permute-start.4 = (f32[2,10,16,128]{3,2,1,0:T(8,128)}, f32[2,10,16,128]{3,2,1,0:T(8,128)}, u32[]{:S(2)}, u32[]{:S(2)}) collective-permute-start(f32[2,10,16,128]{3,2,1,0:T(8,128)} %pad_maximum_fusion.after.refs_0_), channel_id=1, source_target_pairs={{0,8},{4,12},{8,0},{12,4},{1,9},{5,13},{9,1},{13,5},{2,10},{6,14},... | collective-permute-start | bytes 491528 | tf_op jit(solution)/shard_map/ppermute | solution.py:595
  67.9 5.6 %collective-permute-start.3 = (f32[2,10,16,128]{3,2,1,0:T(8,128)}, f32[2,10,16,128]{3,2,1,0:T(8,128)}, u32[]{:S(2)}, u32[]{:S(2)}) collective-permute-start(f32[2,10,16,128]{3,2,1,0:T(8,128)} %pad_maximum_fusion.after.refs_0_), channel_id=1, source_target_pairs={{0,4},{4,0},{8,12},{12,8},{1,5},{5,1},{9,13},{13,9},{2,6},{6,2},{1... | collective-permute-start | bytes 491528 | tf_op jit(solution)/shard_map/ppermute | solution.py:595
  71.0 0.8 copy-start.7
  71.8 0.8 copy-start.13
  79.9 37.1 %copy-start.11 = (s32[4,4]{1,0:T(4,128)S(1)}, s32[4,4]{1,0:T(4,128)}, u32[]{:S(2)}) copy-start(s32[4,4]{1,0:T(4,128)} %constant.26.clone.starts) | copy-start | bytes 196
  80.0 40.9 %all-to-all-start.3 = ((f32[8,32,16,128]{3,2,1,0:T(8,128)}), f32[8,32,16,128]{3,2,1,0:T(8,128)S(1)}, u32[]{:S(2)}, u32[]{:S(2)}) async-start(f32[8,32,16,128]{3,2,1,0:T(8,128)} %get-tuple-element.31), calls=%async_computation.3 | async-start | bytes 4194304 | tf_op jit(solution)/shard_map/all_to_all | solution.py:581
  83.8 42.3 %copy-start = (f32[512,512]{1,0:T(8,128)S(1)}, f32[512,512]{1,0:T(8,128)}, u32[]{:S(2)}) copy-start(f32[512,512]{1,0:T(8,128)} %parent.3) | copy-start | bytes 3145732
  83.8 33.3 %collective-permute-start.7 = (f32[68,16,128]{2,1,0:T(8,128)}, f32[68,16,128]{2,1,0:T(8,128)S(1)}, u32[]{:S(2)}, u32[]{:S(2)}) collective-permute-start(f32[68,16,128]{2,1,0:T(8,128)} %copy-done.13), channel_id=1, source_target_pairs={{0,2},{2,0},{1,3},{3,1},{4,6},{6,4},{5,7},{7,5},{8,10},{10,8},{9,1... | collective-permute-start | bytes 1671176 | tf_op jit(solution)/shard_map/ppermute | solution.py:586
  113.8 1.0 copy-start.2
  114.8 1.0 copy-start.4
  120.9 19.1 %all-to-all-start.2 = ((f32[8,16,16,128]{3,2,1,0:T(8,128)}), f32[8,16,16,128]{3,2,1,0:T(8,128)}, u32[]{:S(2)}, u32[]{:S(2)}) async-start(f32[8,16,16,128]{3,2,1,0:T(8,128)} %get-tuple-element.30), calls=%async_computation.2 | async-start | bytes 2097152 | tf_op jit(solution)/shard_map/all_to_all | solution.py:581
  126.0 1.2 copy-start.3
  127.2 1.2 copy-start.5
  129.1 1.0 copy-start.1

commit v6 on v5

--- a/solution.py
+++ b/solution.py
@@ -110,7 +110,7 @@
 
 
 def update_kernel(
-    place, blocks, mapping, coupling, inverse, parent, early, late, left, right, own, high, low, update, sems, *, plan
+    place, blocks, mapping_in, coupling, inverse, parent, early, late, left, right, own, high, low, update, mapping, sems, *, plan
 ):
     blk, size = plan.blk, plan.strip
     order = coupling.shape[0]
@@ -121,15 +121,11 @@
         window = pl.ds(start, width)
         copies.append(pltpu.make_async_copy(coupling.at[window], left.at[window], sems.at[k + 1]))
     copies.append(pltpu.make_async_copy(parent, own, sems.at[len(starts) + 1]))
+    ids = pltpu.make_async_copy(mapping_in, mapping, sems.at[len(starts) + 2])
+    ids.start()
     for copy in copies:
         copy.start()
     base = plan.early
-    lanes = lax.broadcasted_iota(jnp.int32, (size, blk), 1)
-    coded = jnp.zeros((size, blk), F32)
-    for s in range(plan.slots):
-        coded = jnp.where(lanes == s, mapping[0, s].astype(F32), coded)
-    for d in range(plan.members):
-        early[d, base + plan.n_parent] = coded
     copies[0].wait()
     factor_of = split(right[...])
     for k, start in enumerate(starts):
@@ -151,6 +147,13 @@
             else:
                 late[d, e - plan.early] = strip
 
+    ids.wait()
+    lanes = lax.broadcasted_iota(jnp.int32, (size, blk), 1)
+    coded = jnp.zeros((size, blk), F32)
+    for s in range(plan.slots):
+        coded = jnp.where(lanes == s, mapping[0, s].astype(F32), coded)
+    for d in range(plan.members):
+        early[d, base + plan.n_parent] = coded
     copies[-1].wait()
     row, col = place[0], place[1] * plan.near + place[2]
 
@@ -181,7 +184,7 @@
     return call(
         functools.partial(update_kernel, plan=plan),
         24,
-        in_specs=[SMEM] * 3 + [HBM] * 3,
+        in_specs=[SMEM] * 2 + [HBM] * 4,
         out_specs=[VMEM] * 2,
         out_shape=[jax.ShapeDtypeStruct((plan.members, n, plan.strip, plan.blk), F32) for n in counts],
         scratch_shapes=[
@@ -191,9 +194,10 @@
             pltpu.VMEM((order, pivots), BF16),
             pltpu.VMEM((order, pivots), BF16),
             pltpu.VMEM((order, order), F32),
-            pltpu.SemaphoreType.DMA((4,)),
+            pltpu.SMEM(mapping.shape, jnp.int32),
+            pltpu.SemaphoreType.DMA((5,)),
         ],
-    )(place, blocks, mapping, *(in_hbm(v) for v in (coupling, inverse, parent)))
+    )(place, blocks, *(in_hbm(v) for v in (mapping, coupling, inverse, parent)))
 
 
 def merge_head_kernel(place, maps, table, early, head, token, total, *, plan):
@@ -437,14 +441,17 @@
         end = off + nb
         both = factor_block(jnp.concatenate([s[off:end, off:end], (r == c).astype(F32)], 1))
         w = both[:, nb:]
+        if end < n:
+            below = dot_nt(s[end:, off:end], w)
+            s[end : end + nb, end : end + nb] -= dot_nt(below[:nb], below[:nb])
+            if end + nb < n:
+                s[end + nb :, end:] -= dot_nt(below[nb:], below)
+            l_ref[end:, off:end] = below
         l_ref[off:end, off:end] = jnp.where(r >= c, both[:, :nb].T, 0.0)
         x_ref[off:end, off:end] = w
         if off:
             x_ref[off:end, :off] = dot_nn(w, x_ref[off:end, :off])
         if end < n:
-            below = dot_nt(s[end:, off:end], w)
-            s[end:, end:] -= dot_nt(below, below)
-            l_ref[end:, off:end] = below
             x_ref[end:, :end] -= dot_nn(below, x_ref[off:end, :end])
     copy.wait()
 

time: 144 us -> 143 us (level)
  Pallas kernels: 48.6 us -> 46 us
  waiting for transfers between devices: 24 us -> 26.6 us
    pallas_call x1, Pallas kernels: 28.6 us -> 25.9 us  [cholesky(): call(functools.partial(cholesky_kernel, plan=plan), 12, in_specs=[SMEM] +...]
    ppermute x2, waiting for transfers between devices: 5.14 us -> 7.67 us  [across(): lax.ppermute(x, 'far', [(f, (f + by) % plan.far) for f in range(plan.far)])]
    unnamed x28 -> x26, local copies, waits for them, and re-layouts: 7.67 us -> 7.03 us
  transfers between devices with their start and end apart: 11 -> 11, of which waited for: 7 -> 7; matrix products, arithmetic and copies ran while one was open for 0% -> 1% of each run, Pallas kernels for 26% -> 24%
where the time goes in v6:
time: 143 us
  Pallas kernels  46 us (32%)
  blocking collectives  36.5 us (26%)
  waiting for transfers between devices  26.6 us (19%)
  starting transfers between devices  24.9 us (17%)
  local copies, waits for them, and re-layouts  7.03 us (5%)
    all_to_all x1, blocking collectives, all_to_all(): return lax.all_to_all(x, GROUP, 0, 0, tiled=True)  36.5 us
    pallas_call x1, Pallas kernels, cholesky(): call(functools.partial(cholesky_kernel, plan=plan), 12, in_specs=[SMEM] +...  25.9 us
    all_to_all x3, starting transfers between devices, all_to_all(): return lax.all_to_all(x, GROUP, 0, 0, tiled=True)  12.7 us
    all_to_all x3, waiting for transfers between devices, all_to_all(): return lax.all_to_all(x, GROUP, 0, 0, tiled=True)  12 us
    ppermute x2, waiting for transfers between devices, across(): lax.ppermute(x, 'far', [(f, (f + by) % plan.far) for f in range(plan.far)])  7.67 us
    unnamed x26, local copies, waits for them, and re-layouts  7.03 us
    pallas_call x1, Pallas kernels, update_strips(): call(functools.partial(update_kernel, plan=plan), 24, in_specs=[SMEM] * 2...  6.29 us
    ppermute x3, waiting for transfers between devices, spread_head(): lax.ppermute(head, ('far', 'near'), [(d, d ^ k) for d in range(cols)])  5.85 us
  transfers between devices with their start and end apart: 11, of which 7 were waited for; matrix products, arithmetic and copies ran while one was open for 1% of the time, Pallas kernels for 24%

profile of v6, /device:TPU:0, one launch (start us, length us, event | category | flops | bytes accessed | tf_op | source)
XLA Modules:
  0.0 142.8 jit_solution(9926056042017627000)
XLA Ops:
  0.7 0.1 pad_add_fusion.place
  0.7 6.3 %shard_map.100 = (f32[8,37,16,128]{3,2,1,0:T(8,128)S(1)}, f32[8,10,16,128]{3,2,1,0:T(8,128)S(1)}) custom-call(s32[3]{0:T(128)S(1)} %pad_add_fusion.place, s32[1]{0:T(128)S(6)} %copy.11.blocks, s32[1,8]{1,0:T(1,128)} %mapping_in.1, f32[1024,512]{1,0:T(8,128)} %bitcast.13, f32[512,512]{1,0:T(8,128)} %bitcast.14, f32[512,512]{1,0:T(8,128)} %parent.3), custom_call_target="tpu_custom_call" | custom-call | flops 1 | bytes 1 | tf_op jit(solution)/shard_map/pallas_call | solution.py:184
  7.0 0.0 copy-start.6
  7.0 0.0 copy-start.10
  7.1 36.5 %all_to_all.20.early = f32[8,37,16,128]{3,2,1,0:T(8,128)S(1)} all-to-all(f32[8,37,16,128]{3,2,1,0:T(8,128)S(1)} %get-tuple-element.20), channel_id=1, replica_groups=mesh['leaf'=2,'prow'=4,'far'=2,'near'=2] {'prow','near'}, dimensions={0} | all-to-all | bytes 4849664 | tf_op jit(solution)/shard_map/all_to_all | solution.py:588
  43.6 3.7 %all-to-all-start.1 = ((f32[8,10,16,128]{3,2,1,0:T(8,128)}), f32[8,10,16,128]{3,2,1,0:T(8,128)S(1)}, u32[]{:S(2)}, u32[]{:S(2)}) async-start(f32[8,10,16,128]{3,2,1,0:T(8,128)} %copy-done.6), calls=%async_computation.1 | async-start | bytes 1310720 | tf_op jit(solution)/shard_map/all_to_all | solution.py:588
  47.3 0.0 copy-done.10
  47.3 1.3 shard_map.101
  48.6 0.0 copy-start.8
  48.6 2.6 %collective-permute-start = (f32[10,16,128]{2,1,0:T(8,128)S(1)}, f32[10,16,128]{2,1,0:T(8,128)S(1)}, u32[]{:S(2)}, u32[]{:S(2)}) collective-permute-start(f32[10,16,128]{2,1,0:T(8,128)S(1)} %get-tuple-element.21), channel_id=1, source_target_pairs={{0,2},{1,3},{2,0},{3,1},{4,6},{5,7},{6,4},{7,5},{8,10},{9,11},{10,... | collective-permute-start | bytes 245768 | tf_op jit(solution)/shard_map/ppermute | solution.py:600
  51.2 1.7 %collective-permute-start.2 = (f32[10,16,128]{2,1,0:T(8,128)S(1)}, f32[10,16,128]{2,1,0:T(8,128)S(1)}, u32[]{:S(2)}, u32[]{:S(2)}) collective-permute-start(f32[10,16,128]{2,1,0:T(8,128)S(1)} %get-tuple-element.21), channel_id=1, source_target_pairs={{0,3},{1,2},{2,1},{3,0},{4,7},{5,6},{6,5},{7,4},{8,11},{9,10},{10,... | collective-permute-start | bytes 245768 | tf_op jit(solution)/shard_map/ppermute | solution.py:600
  52.9 0.2 collective-permute-start.1
  53.2 2.1 %shard_map.103.mine = f32[48,16,128]{2,1,0:T(8,128)S(1)} custom-call(s32[3]{0:T(128)S(1)} %pad_add_fusion.place, s32[8,8]{1,0:T(8,128)S(1)} %bitcast.11, s32[17,17]{1,0:T(8,128)S(1)} %copy-done.9, f32[8,37,16,128]{3,2,1,0:T(8,128)S(1)} %all_to_all.20.early, f32[8,128]{1,0:T(8,128)S(1)} %get-tuple-element.24.after), custom_call_target="tpu_custom_call" | custom-call | flops 1 | bytes 1 | tf_op jit(solution)/shard_map/pallas_call | solution.py:274
  55.2 2.6 %collective-permute-start.6 = (f32[48,16,128]{2,1,0:T(8,128)S(1)}, f32[48,16,128]{2,1,0:T(8,128)}, u32[]{:S(2)}, u32[]{:S(2)}) collective-permute-start(f32[48,16,128]{2,1,0:T(8,128)S(1)} %shard_map.103.mine), channel_id=1, source_target_pairs={{0,2},{2,0},{1,3},{3,1},{4,6},{6,4},{5,7},{7,5},{8,10},{10,8},{9,1... | collective-permute-start | bytes 1179656 | tf_op jit(solution)/shard_map/ppermute | solution.py:593
  57.8 0.0 collective-permute-done
  57.8 5.8 %collective-permute-done.2 = f32[10,16,128]{2,1,0:T(8,128)S(1)} collective-permute-done((f32[10,16,128]{2,1,0:T(8,128)S(1)}, f32[10,16,128]{2,1,0:T(8,128)S(1)}, u32[]{:S(2)}, u32[]{:S(2)}) %collective-permute-start.2) | collective-permute-done | bytes 81952 | tf_op jit(solution)/shard_map/ppermute | solution.py:600
  63.7 0.0 collective-permute-done.1
  63.7 0.7 pad_maximum_fusion.after.refs_0_
  64.4 2.4 %collective-permute-start.5 = (f32[2,10,16,128]{3,2,1,0:T(8,128)}, f32[2,10,16,128]{3,2,1,0:T(8,128)}, u32[]{:S(2)}, u32[]{:S(2)}) collective-permute-start(f32[2,10,16,128]{3,2,1,0:T(8,128)} %pad_maximum_fusion.after.refs_0_), channel_id=1, source_target_pairs={{0,12},{4,8},{8,4},{12,0},{1,13},{5,9},{9,5},{13,1},{2,14},{6,10},... | collective-permute-start | bytes 491528 | tf_op jit(solution)/shard_map/ppermute | solution.py:602
  66.8 0.5 collective-permute-start.4
  67.3 0.6 collective-permute-start.3
  67.9 0.0 all-to-all-done.1.late
  67.9 2.4 %shard_map.102 = (f32[68,16,128]{2,1,0:T(8,128)S(1)}, f32[68,16,128]{2,1,0:T(8,128)S(1)}, f32[8,128]{1,0:T(8,128)S(1)}) custom-call(s32[3]{0:T(128)S(1)} %pad_add_fusion.place, s32[8,8]{1,0:T(8,128)S(1)} %bitcast.12, s32[17,17]{1,0:T(8,128)S(1)} %copy-done.8, s32[2]{0:T(128)S(1)} %iota_multiply_fusion.begins, f32[8,37,16,128]{3,2,1,0:T(8,128)S(1)} %all_to_all.20.early, ...), custom_call_target="tpu_custom_call" | custom-call | flops 1 | bytes 1 | tf_op jit(solution)/shard_map/pallas_call | solution.py:304
  70.3 0.0 copy-start.7
  70.3 0.8 copy-done.7
  71.1 0.8 copy-done.12
  71.9 0.0 collective-permute-done.5.refs_3_
  71.9 0.7 collective-permute-done.4.refs_2_
  72.7 0.3 collective-permute-done.3.refs_1_
  72.9 3.8 %collective-permute-done.6.other = f32[48,16,128]{2,1,0:T(8,128)} collective-permute-done((f32[48,16,128]{2,1,0:T(8,128)S(1)}, f32[48,16,128]{2,1,0:T(8,128)}, u32[]{:S(2)}, u32[]{:S(2)}) %collective-permute-start.6) | collective-permute-done | bytes 393248 | tf_op jit(solution)/shard_map/ppermute | solution.py:593
  76.8 2.6 %shard_map.104 = (f32[8,32,16,128]{3,2,1,0:T(8,128)}, f32[8,128]{1,0:T(8,128)S(1)}) custom-call(s32[3]{0:T(128)S(1)} %pad_add_fusion.place, f32[48,16,128]{2,1,0:T(8,128)S(1)} %shard_map.103.mine, f32[48,16,128]{2,1,0:T(8,128)} %collective-permute-done.6.other, f32[8,128]{1,0:T(8,128)S(1)} %get-tuple-element.25.refs_0_, ...), custom_call_target="tpu_custom_call" | custom-call | flops 1 | bytes 1 | tf_op jit(solution)/shard_map/pallas_call | solution.py:335
  79.3 0.0 copy-start.11
  79.3 3.8 %all-to-all-start.3 = ((f32[8,32,16,128]{3,2,1,0:T(8,128)}), f32[8,32,16,128]{3,2,1,0:T(8,128)S(1)}, u32[]{:S(2)}, u32[]{:S(2)}) async-start(f32[8,32,16,128]{3,2,1,0:T(8,128)} %get-tuple-element.31), calls=%async_computation.3 | async-start | bytes 4194304 | tf_op jit(solution)/shard_map/all_to_all | solution.py:588
  83.1 0.0 copy-start
  83.2 1.5 %collective-permute-start.7 = (f32[68,16,128]{2,1,0:T(8,128)}, f32[68,16,128]{2,1,0:T(8,128)S(1)}, u32[]{:S(2)}, u32[]{:S(2)}) collective-permute-start(f32[68,16,128]{2,1,0:T(8,128)} %copy-done.12), channel_id=1, source_target_pairs={{0,2},{2,0},{1,3},{3,1},{4,6},{6,4},{5,7},{7,5},{8,10},{10,8},{9,1... | collective-permute-start | bytes 1671176 | tf_op jit(solution)/shard_map/ppermute | solution.py:593
  84.7 25.9 %shard_map.105 = (f32[512,512]{1,0:T(8,128)S(1)}, f32[512,512]{1,0:T(8,128)S(1)}, f32[68,16,128]{2,1,0:T(8,128)S(1)}, f32[8,128]{1,0:T(8,128)S(1)}) custom-call(s32[3]{0:T(128)S(1)} %pad_add_fusion.place, f32[2,10,16,128]{3,2,1,0:T(8,128)} %pad_maximum_fusion.after.refs_0_, f32[2,10,16,128]{3,2,1,0:T(8,128)} %collective-permute-done.3.refs_1_, ...), custom_call_target="tpu_custom_call" | custom-call | flops 1 | bytes 1 | tf_op jit(solution)/shard_map/pallas_call | solution.py:461
  110.6 1.0 copy-done.2
  111.6 1.0 copy-done.4
  112.6 3.9 %collective-permute-done.7.other = f32[68,16,128]{2,1,0:T(8,128)S(1)} collective-permute-done((f32[68,16,128]{2,1,0:T(8,128)}, f32[68,16,128]{2,1,0:T(8,128)S(1)}, u32[]{:S(2)}, u32[]{:S(2)}) %collective-permute-start.7) | collective-permute-done | bytes 557088 | tf_op jit(solution)/shard_map/ppermute | solution.py:593
  116.4 1.6 %shard_map.106 = (f32[8,16,16,128]{3,2,1,0:T(8,128)}, f32[8,128]{1,0:T(8,128)S(1)}) custom-call(s32[3]{0:T(128)S(1)} %pad_add_fusion.place, s32[4,4]{1,0:T(4,128)S(1)} %copy-done.11, f32[68,16,128]{2,1,0:T(8,128)S(1)} %get-tuple-element.27.mine, f32[68,16,128]{2,1,0:T(8,128)S(1)} %collective-permute-done.7.other, f32[8,128]{1,0:T(8,128)S(1)} %get-tuple-element.29.after), custom_call_target="tpu_custom_call" | custom-call | flops 1 | bytes 1 | tf_op jit(solution)/shard_map/pallas_call | solution.py:369
  118.1 2.1 %all-to-all-done.3.columns = f32[8,32,16,128]{3,2,1,0:T(8,128)S(1)} async-done(((f32[8,32,16,128]{3,2,1,0:T(8,128)}), f32[8,32,16,128]{3,2,1,0:T(8,128)S(1)}, u32[]{:S(2)}, u32[]{:S(2)}) %all-to-all-start.3) | async-done | bytes 2097184 | tf_op jit(solution)/shard_map/all_to_all | solution.py:588
  120.2 5.3 %all-to-all-start.2 = ((f32[8,16,16,128]{3,2,1,0:T(8,128)}), f32[8,16,16,128]{3,2,1,0:T(8,128)}, u32[]{:S(2)}, u32[]{:S(2)}) async-start(f32[8,16,16,128]{3,2,1,0:T(8,128)} %get-tuple-element.30), calls=%async_computation.2 | async-start | bytes 2097152 | tf_op jit(solution)/shard_map/all_to_all | solution.py:588
  125.5 1.2 copy-done.3
  126.7 1.2 copy-done.5
  128.0 0.6 shard_map.107.base_in
  128.6 1.0 copy-done.1
  129.6 9.9 %all-to-all-done.2.rests_in = f32[8,16,16,128]{3,2,1,0:T(8,128)} async-done(((f32[8,16,16,128]{3,2,1,0:T(8,128)}), f32[8,16,16,128]{3,2,1,0:T(8,128)}, u32[]{:S(2)}, u32[]{:S(2)}) %all-to-all-start.2) | async-done | bytes 1048608 | tf_op jit(solution)/shard_map/all_to_all | solution.py:588
  139.5 3.1 %shard_map.108 = f32[512,512]{1,0:T(8,128)} custom-call(s32[3]{0:T(128)S(1)} %pad_add_fusion.place, f32[8,16,16,128]{3,2,1,0:T(8,128)} %all-to-all-done.2.rests_in, f32[512,512]{1,0:T(8,128)} %copy-done.1), custom_call_target="tpu_custom_call" | custom-call | flops 1 | bytes 1 | tf_op jit(solution)/shard_map/pallas_call | solution.py:571
  (16 shorter events, 0.1 us)
Async XLA Ops:
  7.0 36.5 %copy-start.6 = (f32[8,10,16,128]{3,2,1,0:T(8,128)}, f32[8,10,16,128]{3,2,1,0:T(8,128)S(1)}, u32[]{:S(2)}) copy-start(f32[8,10,16,128]{3,2,1,0:T(8,128)S(1)} %get-tuple-element.22) | copy-start | bytes 1966084
  7.0 40.2 %copy-start.10 = (s32[17,17]{1,0:T(8,128)S(1)}, s32[17,17]{1,0:T(8,128)}, u32[]{:S(2)}) copy-start(s32[17,17]{1,0:T(8,128)} %constant.22.clone.table) | copy-start | bytes 3472
  43.6 9.6 %copy-start.9 = (s32[17,17]{1,0:T(8,128)S(1)}, s32[17,17]{1,0:T(8,128)}, u32[]{:S(2)}) copy-start(s32[17,17]{1,0:T(8,128)} %constant.23.clone.table) | copy-start | bytes 3472
  43.6 24.3 %all-to-all-start.1 = ((f32[8,10,16,128]{3,2,1,0:T(8,128)}), f32[8,10,16,128]{3,2,1,0:T(8,128)S(1)}, u32[]{:S(2)}, u32[]{:S(2)}) async-start(f32[8,10,16,128]{3,2,1,0:T(8,128)} %copy-done.6), calls=%async_computation.1 | async-start | bytes 1310720 | tf_op jit(solution)/shard_map/all_to_all | solution.py:588
  48.6 19.3 %copy-start.8 = (s32[17,17]{1,0:T(8,128)S(1)}, s32[17,17]{1,0:T(8,128)}, u32[]{:S(2)}) copy-start(s32[17,17]{1,0:T(8,128)} %constant.24.clone.table) | copy-start | bytes 3472
  48.6 9.2 %collective-permute-start = (f32[10,16,128]{2,1,0:T(8,128)S(1)}, f32[10,16,128]{2,1,0:T(8,128)S(1)}, u32[]{:S(2)}, u32[]{:S(2)}) collective-permute-start(f32[10,16,128]{2,1,0:T(8,128)S(1)} %get-tuple-element.21), channel_id=1, source_target_pairs={{0,2},{1,3},{2,0},{3,1},{4,6},{5,7},{6,4},{7,5},{8,10},{9,11},{10,... | collective-permute-start | bytes 245768 | tf_op jit(solution)/shard_map/ppermute | solution.py:600
  51.2 12.4 %collective-permute-start.2 = (f32[10,16,128]{2,1,0:T(8,128)S(1)}, f32[10,16,128]{2,1,0:T(8,128)S(1)}, u32[]{:S(2)}, u32[]{:S(2)}) collective-permute-start(f32[10,16,128]{2,1,0:T(8,128)S(1)} %get-tuple-element.21), channel_id=1, source_target_pairs={{0,3},{1,2},{2,1},{3,0},{4,7},{5,6},{6,5},{7,4},{8,11},{9,10},{10,... | collective-permute-start | bytes 245768 | tf_op jit(solution)/shard_map/ppermute | solution.py:600
  52.9 10.7 %collective-permute-start.1 = (f32[10,16,128]{2,1,0:T(8,128)S(1)}, f32[10,16,128]{2,1,0:T(8,128)S(1)}, u32[]{:S(2)}, u32[]{:S(2)}) collective-permute-start(f32[10,16,128]{2,1,0:T(8,128)S(1)} %get-tuple-element.21), channel_id=1, source_target_pairs={{0,1},{1,0},{2,3},{3,2},{4,5},{5,4},{6,7},{7,6},{8,9},{9,8},{10,11... | collective-permute-start | bytes 245768 | tf_op jit(solution)/shard_map/ppermute | solution.py:600
  55.2 21.5 %collective-permute-start.6 = (f32[48,16,128]{2,1,0:T(8,128)S(1)}, f32[48,16,128]{2,1,0:T(8,128)}, u32[]{:S(2)}, u32[]{:S(2)}) collective-permute-start(f32[48,16,128]{2,1,0:T(8,128)S(1)} %shard_map.103.mine), channel_id=1, source_target_pairs={{0,2},{2,0},{1,3},{3,1},{4,6},{6,4},{5,7},{7,5},{8,10},{10,8},{9,1... | collective-permute-start | bytes 1179656 | tf_op jit(solution)/shard_map/ppermute | solution.py:593
  64.4 7.6 %collective-permute-start.5 = (f32[2,10,16,128]{3,2,1,0:T(8,128)}, f32[2,10,16,128]{3,2,1,0:T(8,128)}, u32[]{:S(2)}, u32[]{:S(2)}) collective-permute-start(f32[2,10,16,128]{3,2,1,0:T(8,128)} %pad_maximum_fusion.after.refs_0_), channel_id=1, source_target_pairs={{0,12},{4,8},{8,4},{12,0},{1,13},{5,9},{9,5},{13,1},{2,14},{6,10},... | collective-permute-start | bytes 491528 | tf_op jit(solution)/shard_map/ppermute | solution.py:602
  66.8 5.9 %collective-permute-start.4 = (f32[2,10,16,128]{3,2,1,0:T(8,128)}, f32[2,10,16,128]{3,2,1,0:T(8,128)}, u32[]{:S(2)}, u32[]{:S(2)}) collective-permute-start(f32[2,10,16,128]{3,2,1,0:T(8,128)} %pad_maximum_fusion.after.refs_0_), channel_id=1, source_target_pairs={{0,8},{4,12},{8,0},{12,4},{1,9},{5,13},{9,1},{13,5},{2,10},{6,14},... | collective-permute-start | bytes 491528 | tf_op jit(solution)/shard_map/ppermute | solution.py:602
  67.3 5.6 %collective-permute-start.3 = (f32[2,10,16,128]{3,2,1,0:T(8,128)}, f32[2,10,16,128]{3,2,1,0:T(8,128)}, u32[]{:S(2)}, u32[]{:S(2)}) collective-permute-start(f32[2,10,16,128]{3,2,1,0:T(8,128)} %pad_maximum_fusion.after.refs_0_), channel_id=1, source_target_pairs={{0,4},{4,0},{8,12},{12,8},{1,5},{5,1},{9,13},{13,9},{2,6},{6,2},{1... | collective-permute-start | bytes 491528 | tf_op jit(solution)/shard_map/ppermute | solution.py:602
  70.3 0.8 copy-start.7
  71.1 0.8 copy-start.12
  79.3 37.1 %copy-start.11 = (s32[4,4]{1,0:T(4,128)S(1)}, s32[4,4]{1,0:T(4,128)}, u32[]{:S(2)}) copy-start(s32[4,4]{1,0:T(4,128)} %constant.26.clone.starts) | copy-start | bytes 196
  79.3 40.9 %all-to-all-start.3 = ((f32[8,32,16,128]{3,2,1,0:T(8,128)}), f32[8,32,16,128]{3,2,1,0:T(8,128)S(1)}, u32[]{:S(2)}, u32[]{:S(2)}) async-start(f32[8,32,16,128]{3,2,1,0:T(8,128)} %get-tuple-element.31), calls=%async_computation.3 | async-start | bytes 4194304 | tf_op jit(solution)/shard_map/all_to_all | solution.py:588
  83.1 42.4 %copy-start = (f32[512,512]{1,0:T(8,128)S(1)}, f32[512,512]{1,0:T(8,128)}, u32[]{:S(2)}) copy-start(f32[512,512]{1,0:T(8,128)} %parent.3) | copy-start | bytes 3145732
  83.2 33.3 %collective-permute-start.7 = (f32[68,16,128]{2,1,0:T(8,128)}, f32[68,16,128]{2,1,0:T(8,128)S(1)}, u32[]{:S(2)}, u32[]{:S(2)}) collective-permute-start(f32[68,16,128]{2,1,0:T(8,128)} %copy-done.12), channel_id=1, source_target_pairs={{0,2},{2,0},{1,3},{3,1},{4,6},{6,4},{5,7},{7,5},{8,10},{10,8},{9,1... | collective-permute-start | bytes 1671176 | tf_op jit(solution)/shard_map/ppermute | solution.py:593
  110.6 1.0 copy-start.2
  111.6 1.0 copy-start.4
  120.2 19.2 %all-to-all-start.2 = ((f32[8,16,16,128]{3,2,1,0:T(8,128)}), f32[8,16,16,128]{3,2,1,0:T(8,128)}, u32[]{:S(2)}, u32[]{:S(2)}) async-start(f32[8,16,16,128]{3,2,1,0:T(8,128)} %get-tuple-element.30), calls=%async_computation.2 | async-start | bytes 2097152 | tf_op jit(solution)/shard_map/all_to_all | solution.py:588
  125.5 1.2 copy-start.3
  126.7 1.2 copy-start.5
  128.6 1.0 copy-start.1
